TPU v7x, 32 devices: a whole 2x2x4 slice. The times are simulated.
32 devices in a mesh: tm: 8 (over z, y), clip: 4 (over x, core).
Axes of the slice: x: 2, y: 2, z: 4, core: 2. Of those that a mesh axis runs over, the one named last changes fastest.
Arguments:
- student_query: bfloat16 [4096, 1024], P('tm', 'clip'), may hold values from -12 to 12
- teacher_key: bfloat16 [16384, 1024], P('tm', 'clip'), may hold values from -1000 to 1000
- teacher_value: bfloat16 [16384, 1024], P('tm', 'clip'), may hold values from -12 to 12
- clip_order: int32 [16384], replicated, may hold values from 0 to 16383, as said below
- band_start: int32 [128], P('tm'), may hold values from -16 to -1
- band_end: int32 [128], P('tm'), may hold values from 1 to 16
- output_weight: bfloat16 [1024, 1024], P('clip'), may hold values from -0.1875 to 0.1875
- cotangent: bfloat16 [4096, 1024], P('tm', 'clip'), may hold values from -6 to 6
Outputs:
- joined: bfloat16 [4096, 1024], P('tm', 'clip')
- grad_query: bfloat16 [4096, 1024], P('tm', 'clip')
- grad_output_weight: float32 [1024, 1024], P('clip')
Inputs may be any that keep to these rules, and one draw needn't show every extreme that they name: clip_order is a permutation. For a time row t of time shard j = t // 2048, clip_order[t] % 2048 lies in [j * 256, (j + 1) * 256): every input shard holds exactly 256 rows of every time shard, as one run.
All inputs are finite; a program needn't handle non-finite values.
Results may differ from a plain program's by a relative error of at most 0.0094.
Values may be sent and summed in bfloat16 or wider, within the bound.
No kernel may reach another device: no remote copies, remote signals or barrier semaphores. Data moves between devices by JAX's collectives and lax.ppermute only.
A program may use at most 128 MiB of HBM per device.

v0:
```python
import functools
import itertools
import math

import jax
import jax.numpy as jnp
from jax import lax
from jax.experimental import pallas as pl
from jax.experimental.pallas import tpu as pltpu
from jax.sharding import PartitionSpec as P

HDIM = 64
SBLK = 32
TBLK = 128
TILE = 128
CHUNK = 1024
NEG = -1e30
STATS = 16
OUT = 3 * HDIM + STATS
BF = jnp.bfloat16
F32 = jnp.float32
NT = (((1,), (1,)), ((), ()))
CLIPS = (0, 2, 1, 3)
VMEM_LIMIT = 48 * 1024 * 1024


def params(*semantics):
    return pltpu.CompilerParams(
        dimension_semantics=semantics or None, vmem_limit_bytes=VMEM_LIMIT
    )


def cost(flops, nbytes, trans=0):
    return pl.CostEstimate(flops=flops, bytes_accessed=nbytes, transcendentals=trans)


def pack_kernel(slots, slot, k_ref, v_ref, *refs):
    out = refs[-1]
    for half in range(2):
        c = (half * slots + slot) * HDIM
        out[0, half] = jnp.concatenate([k_ref[:, c : c + HDIM], v_ref[:, c : c + HDIM]], axis=1)


def pack(keys, values, groups, slots, slot, *after):
    rows, feats = keys.shape
    part = rows // groups
    block = pl.BlockSpec((part, feats), lambda i: (i, 0))
    return pl.pallas_call(
        functools.partial(pack_kernel, slots, slot),
        grid=(groups,),
        in_specs=[block, block] + [pl.BlockSpec(memory_space=pl.ANY)] * len(after),
        out_specs=pl.BlockSpec((1, 2, part, 2 * HDIM), lambda i: (i, 0, 0, 0)),
        out_shape=jax.ShapeDtypeStruct((groups, 2, part, 2 * HDIM), BF),
        compiler_params=params("arbitrary"),
        cost_estimate=cost(0, 3 * rows * feats * 2),
    )(keys, values, *after)


def order_kernel(idx_ref, arr_ref, *refs):
    kv_ref, kvt_ref, arrt, hot = refs[-4:]
    rows = arrt.shape[1]
    arr = arr_ref[...].reshape(rows, arrt.shape[0])
    for j in range(0, rows, 256):
        arrt[:, j : j + 256] = arr[j : j + 256].T
    idx = idx_ref[0]
    iota = lax.broadcasted_iota(jnp.int32, (256, rows), 0).astype(F32).astype(BF)
    for j in range(0, rows, 256):
        near = idx - j
        near = jnp.where((near >= 0) & (near < 256), near, -1).astype(F32).astype(BF)
        hot[j : j + 256] = jnp.where(iota == near, BF(1), BF(0))
    acc = jnp.dot(arrt[...], hot[...], preferred_element_type=F32)
    kvt_ref[...] = acc.astype(BF)
    kv_ref[...] = acc.T.astype(BF)


def put_in_order(arrived, index, rows, *after):
    sources, twice, width = arrived.shape
    return pl.pallas_call(
        order_kernel,
        grid=(2,),
        in_specs=[
            pl.BlockSpec((1, 1, rows), lambda u: (u, 0, 0)),
            pl.BlockSpec((sources, twice // 2, width), lambda u: (0, u, 0)),
        ]
        + [pl.BlockSpec(memory_space=pl.ANY)] * len(after),
        out_specs=[
            pl.BlockSpec((rows, width), lambda u: (u, 0)),
            pl.BlockSpec((width, rows), lambda u: (0, u)),
        ],
        out_shape=[
            jax.ShapeDtypeStruct((2 * rows, width), BF),
            jax.ShapeDtypeStruct((width, 2 * rows), BF),
        ],
        scratch_shapes=[pltpu.VMEM((width, rows), BF), pltpu.VMEM((rows, rows), BF)],
        compiler_params=params("arbitrary"),
        cost_estimate=cost(4 * rows * rows * width, 6 * rows * width * 2),
    )(index.reshape(2, 1, rows), arrived, *after)


def student_kernel(slots, place_ref, here_ref, there_ref, w_ref, q_ref, band_ref, mine_ref, give_ref):
    rows, feats = q_ref.shape
    half, clip = place_ref[0], place_ref[1]
    total = None
    for i, ref in enumerate((here_ref, here_ref, there_ref, there_ref)):
        c = pl.multiple_of((clip ^ CLIPS[i]) * feats, feats)
        part = lax.dot_general(
            ref[i % 2], w_ref[:, pl.ds(c, feats)], NT, preferred_element_type=F32
        )
        total = part if total is None else total + part
    g = total.astype(BF)
    q = q_ref[...] * BF(1.0 / math.sqrt(HDIM))
    heads = []
    for y in range(2):
        cols = []
        for s in range(slots):
            c = (y * slots + s) * HDIM
            cols += [q[:, c : c + HDIM], g[:, c : c + HDIM]]
        heads.append(jnp.concatenate(cols, axis=1))
    mine_ref[:rows] = jnp.where(half == 0, heads[0], heads[1])
    give_ref[:rows] = jnp.where(half == 0, heads[1], heads[0])
    mine_ref[rows:] = band_ref[...]
    give_ref[rows:] = band_ref[...]


def student_side(place, here, there, weight, query, band, slots):
    rows, feats = query.shape
    vm = pl.BlockSpec(memory_space=pltpu.VMEM)
    return pl.pallas_call(
        functools.partial(student_kernel, slots),
        in_specs=[pl.BlockSpec(memory_space=pltpu.SMEM)] + [vm] * 5,
        out_specs=[vm] * 2,
        out_shape=[jax.ShapeDtypeStruct((rows + band.shape[0], 2 * slots * HDIM), BF)] * 2,
        compiler_params=params(),
        cost_estimate=cost(8 * rows * feats * feats, 16 * rows * feats),
    )(place, here, there, weight, query, band)


def cotangent_kernel(place_ref, here_ref, there_ref, after_ref, out_ref):
    cols = here_ref.shape[2]
    for i, ref in enumerate((here_ref, here_ref, there_ref, there_ref)):
        c = pl.multiple_of((place_ref[1] ^ CLIPS[i]) * cols, cols)
        out_ref[:, pl.ds(c, cols)] = ref[i % 2]


def whole_cotangent(place, here, there, after):
    _, rows, cols = here.shape
    vm = pl.BlockSpec(memory_space=pltpu.VMEM)
    return pl.pallas_call(
        cotangent_kernel,
        in_specs=[
            pl.BlockSpec(memory_space=pltpu.SMEM),
            vm,
            vm,
            pl.BlockSpec(memory_space=pl.ANY),
        ],
        out_specs=vm,
        out_shape=jax.ShapeDtypeStruct((rows, 4 * cols), BF),
        compiler_params=params(),
        cost_estimate=cost(0, 16 * rows * cols),
    )(place, here, there, after)


def edge_kernel(place_ref, mine_ref, peer_ref, after_ref, a_ref, b_ref):
    first = place_ref[0] == 0
    mine, peer = mine_ref[...], peer_ref[...]
    a_ref[...] = jnp.where(first, mine, peer)
    b_ref[...] = jnp.where(first, peer, mine)


def edges(place, mine, peer, after):
    vm = pl.BlockSpec(memory_space=pltpu.VMEM)
    return pl.pallas_call(
        edge_kernel,
        in_specs=[
            pl.BlockSpec(memory_space=pltpu.SMEM),
            vm,
            vm,
            pl.BlockSpec(memory_space=pl.ANY),
        ],
        out_specs=[vm] * 2,
        out_shape=[jax.ShapeDtypeStruct(mine.shape, BF)] * 2,
        compiler_params=params(),
        cost_estimate=cost(0, 8 * mine.size),
    )(place, mine, peer, after)


def split3(x):
    a = x.astype(BF).astype(F32)
    b = (x - a).astype(BF).astype(F32)
    c = (x - a - b).astype(BF).astype(F32)
    return [a, b, c]


def attend_kernel(slots, tiles, lohi_ref, qga_ref, qgb_ref, *refs):
    outa_ref, outb_ref = refs[-2 * tiles - 2 : -2 * tiles]
    s_refs, d_refs = refs[-2 * tiles : -tiles], refs[-tiles:]
    rows = outa_ref.shape[1]
    blocks = refs[0].shape[0] // TBLK
    nblk = TILE // SBLK
    cblk = CHUNK // TBLK
    lane = lax.broadcasted_iota(jnp.int32, (1, TILE), 1)
    rhs_lane = lax.broadcasted_iota(jnp.int32, (TILE, 2 * HDIM), 1)
    row_id = lax.broadcasted_iota(jnp.int32, (STATS, TILE), 0)
    z8 = jnp.zeros((8, TILE), F32)
    for (i, slot), (u, q_ref, o_ref) in itertools.product(
        enumerate(slots), ((0, qga_ref, outa_ref), (1, qgb_ref, outb_ref))
    ):
        kv_ref, kvt_ref = refs[2 * i : 2 * i + 2]
        own = slice(slot * 2 * HDIM, (slot + 1) * 2 * HDIM)
        out_rows = slice(i * OUT, (i + 1) * OUT)

        def group(g, carry):
            held = []
            n = jnp.int32(0)
            for k in range(tiles):
                t = g * tiles + k
                base = u * (rows // SBLK) + t * nblk
                los = [lohi_ref[0, base + i] for i in range(nblk)]
                his = [lohi_ref[1, base + i] for i in range(nblk)]
                lo, hi = los[0], his[0]
                lo_lane = jnp.full((1, TILE), los[0])
                hi_lane = jnp.full((1, TILE), his[0])
                for i in range(1, nblk):
                    lo = jnp.minimum(lo, los[i])
                    hi = jnp.maximum(hi, his[i])
                    lo_lane = jnp.where(lane < i * SBLK, lo_lane, los[i])
                    hi_lane = jnp.where(lane < i * SBLK, hi_lane, his[i])
                lo = jnp.maximum(lo, 0)
                hi = jnp.minimum(hi, blocks - 1)
                n = jnp.maximum(n, jnp.maximum(hi - lo + cblk, 0) // cblk)
                r = pl.multiple_of(t * TILE, TILE)
                qg = q_ref[pl.ds(r, TILE), own]
                zero = jnp.zeros_like(qg)
                rhs = jnp.concatenate(
                    [
                        jnp.where(rhs_lane < HDIM, qg, zero),
                        jnp.where(rhs_lane < HDIM, zero, qg),
                    ],
                    axis=0,
                )
                held.append((lo, lo_lane, hi_lane, rhs, r))

            def start(i, lo):
                kb = jnp.minimum(lo + i * cblk, blocks - cblk)
                return kb, pl.multiple_of(kb * TBLK, TBLK)

            def scores(i, tops):
                s0 = pl.multiple_of(i * CHUNK, CHUNK)
                new = []
                for k, (lo, lo_lane, hi_lane, rhs, _) in enumerate(held):
                    kb0, k0 = start(i, lo)
                    low = jnp.maximum(lo_lane, lo + i * cblk)
                    sd = lax.dot_general(
                        kv_ref[pl.ds(k0, CHUNK), :], rhs, NT, preferred_element_type=F32
                    )
                    d_refs[k][pl.ds(s0, CHUNK), :] = sd[:, TILE:]
                    m = tops[k]
                    for b in range(cblk):
                        ok = (low <= kb0 + b) & (hi_lane >= kb0 + b)
                        s = jnp.where(ok, sd[b * TBLK : (b + 1) * TBLK, :TILE], NEG)
                        s_refs[k][pl.ds(s0 + b * TBLK, TBLK), :] = s
                        m = jnp.maximum(m, jnp.max(s.reshape(TBLK // 8, 8, TILE), axis=0))
                    new.append(m)
                return tuple(new)

            tops = lax.fori_loop(
                0, n, scores, tuple(jnp.full((8, TILE), NEG, F32) for _ in range(tiles))
            )
            tops = [jnp.max(m, axis=0, keepdims=True) for m in tops]

            def expo(i, sums):
                s0 = pl.multiple_of(i * CHUNK, CHUNK)
                new = []
                for k in range(tiles):
                    l, dl = sums[k]
                    p = jnp.exp(s_refs[k][pl.ds(s0, CHUNK), :] - tops[k])
                    s_refs[k][pl.ds(s0, CHUNK), :] = p
                    l = l + jnp.sum(p.reshape(CHUNK // 8, 8, TILE), axis=0)
                    pd = p * d_refs[k][pl.ds(s0, CHUNK), :]
                    dl = dl + jnp.sum(pd.reshape(CHUNK // 8, 8, TILE), axis=0)
                    new.append((l, dl))
                return tuple(new)

            ends = []
            for l, dl in lax.fori_loop(0, n, expo, ((z8, z8),) * tiles):
                l = jnp.sum(l, axis=0, keepdims=True)
                inv = 1.0 / jnp.maximum(l, 1e-30)
                ends.append((l, inv, jnp.sum(dl, axis=0, keepdims=True) * inv))

            def products(i, accs):
                s0 = pl.multiple_of(i * CHUNK, CHUNK)
                new = []
                for k in range(tiles):
                    _, k0 = start(i, held[k][0])
                    p = s_refs[k][pl.ds(s0, CHUNK), :]
                    ds = p * (d_refs[k][pl.ds(s0, CHUNK), :] - ends[k][2])
                    both = jnp.concatenate([p.astype(BF), ds.astype(BF)], axis=1)
                    new.append(
                        accs[k]
                        + jnp.dot(
                            kvt_ref[:, pl.ds(k0, CHUNK)], both, preferred_element_type=F32
                        )
                    )
                return tuple(new)

            accs = lax.fori_loop(
                0, n, products, tuple(jnp.zeros((2 * HDIM, 2 * TILE), F32) for _ in range(tiles))
            )
            for k in range(tiles):
                l, inv, delta = ends[k]
                acc = accs[k] * jnp.concatenate([inv, inv], axis=1)
                stats = jnp.where(row_id == 9, 1.0, 0.0)
                for i, piece in enumerate(split3(tops[k]) + split3(l) + split3(delta)):
                    stats = jnp.where(row_id == i, piece, stats)
                out = jnp.concatenate([acc[:, :TILE], acc[:HDIM, TILE:], stats], axis=0)
                o_ref[out_rows, pl.ds(held[k][4], TILE)] = out.astype(o_ref.dtype)
            return carry

        lax.fori_loop(0, rows // (TILE * tiles), group, 0)


def attend(slots, tiles, rows, lohi, qga, qgb, kvs, out_dtype, *after):
    keys = kvs[0].shape[0]
    n = len(slots)
    vm = pl.BlockSpec(memory_space=pltpu.VMEM)
    return pl.pallas_call(
        functools.partial(attend_kernel, slots, tiles),
        in_specs=[pl.BlockSpec(memory_space=pltpu.SMEM)]
        + [vm] * (2 + 2 * n)
        + [pl.BlockSpec(memory_space=pl.ANY)] * len(after),
        out_specs=[vm] * 2,
        out_shape=[jax.ShapeDtypeStruct((n * OUT, rows), out_dtype)] * 2,
        scratch_shapes=[pltpu.VMEM((keys, TILE), F32)] * (2 * tiles),
        compiler_params=params(),
        cost_estimate=cost(
            n * rows * keys * 1024, n * (4 * keys * 128 + 16 * rows * 256), n * rows * keys
        ),
    )(lohi, qga, qgb, *kvs, *after)


def combine_kernel(groups, slots, place_ref, cot_ref, pcot_ref, *refs):
    parts, refs = refs[: 2 * slots + 2], refs[2 * slots + 2 :]
    oqa_ref, oqb_ref, shares, buf = refs[0], refs[1], refs[2:-1], refs[-1]
    scale = 1.0 / math.sqrt(HDIM)
    for u, oq_ref in enumerate((oqa_ref, oqb_ref)):
        for s in range(slots):
            own = parts[2 * s + u][...]
            rem = parts[2 * slots + u][s * OUT : (s + 1) * OUT].astype(F32)

            def stat(x, i):
                r = 3 * HDIM + 3 * i
                return x[r : r + 1] + x[r + 1 : r + 2] + x[r + 2 : r + 3]

            flag = rem[3 * HDIM + 9 : 3 * HDIM + 10]
            m_o, m_r = stat(own, 0), jnp.where(flag > 0.5, stat(rem, 0), NEG)
            l_o, l_r = stat(own, 1), stat(rem, 1)
            d_o, d_r = stat(own, 2), stat(rem, 2)
            top = jnp.maximum(m_o, m_r)
            w_o = l_o * jnp.exp(m_o - top)
            w_r = jnp.where(m_r > 0.5 * NEG, l_r * jnp.exp(m_r - top), 0.0)
            norm = 1.0 / (w_o + w_r)
            w_o, w_r = w_o * norm, w_r * norm
            delta = w_o * d_o + w_r * d_r
            attn = w_o * own[HDIM : 2 * HDIM] + w_r * rem[HDIM : 2 * HDIM]
            s_o, s_r = scale * w_o, scale * w_r
            dq = s_o * own[2 * HDIM : 3 * HDIM] - (s_o * (delta - d_o)) * own[:HDIM]
            dq += s_r * rem[2 * HDIM : 3 * HDIM] - (s_r * (delta - d_r)) * rem[:HDIM]
            oq_ref[s * HDIM : (s + 1) * HDIM] = attn.astype(BF)
            oq_ref[(slots + s) * HDIM : (slots + s + 1) * HDIM] = dq.astype(BF)
    first = place_ref[0] == 0
    attn_a, attn_b = oqa_ref[: slots * HDIM], oqb_ref[: slots * HDIM]
    total = jnp.dot(
        jnp.where(first, attn_a, attn_b), cot_ref[...], preferred_element_type=F32
    )
    total += jnp.dot(
        jnp.where(first, attn_b, attn_a), pcot_ref[...], preferred_element_type=F32
    )
    total = total.astype(BF)
    step = total.shape[1] // groups
    for g in range(groups):
        buf[g] = total[:, g * step : (g + 1) * step]
    for d in range(groups):
        shares[d][...] = buf[place_ref[2] ^ d]


def combine(place, cot, peer_cot, parts, groups, slots):
    rows = parts[0].shape[1]
    width = cot.shape[1]
    vm = pl.BlockSpec(memory_space=pltpu.VMEM)
    share = (slots * HDIM, width // groups)
    return pl.pallas_call(
        functools.partial(combine_kernel, groups, slots),
        in_specs=[pl.BlockSpec(memory_space=pltpu.SMEM)] + [vm] * (4 + 2 * slots),
        out_specs=[vm] * (2 + groups),
        out_shape=[jax.ShapeDtypeStruct((2 * slots * HDIM, rows), BF)] * 2
        + [jax.ShapeDtypeStruct(share, BF)] * groups,
        scratch_shapes=[pltpu.VMEM((groups, *share), BF)],
        compiler_params=params(),
        cost_estimate=cost(
            4 * rows * slots * HDIM * width, 4 * rows * width + 24 * rows * slots * 256
        ),
    )(place, cot, peer_cot, *parts)


def turn_kernel(place_ref, oqa_ref, oqb_ref, mine_ref, give_ref, xmine_ref, xgive_ref):
    width = xmine_ref.shape[1]
    first = place_ref[0] == 0
    a, b = oqa_ref[...], oqb_ref[...]
    mine = jnp.where(first, a, b).T
    give = jnp.where(first, b, a).T
    mine_ref[...] = mine
    give_ref[...] = give
    xmine_ref[...] = mine[:, :width]
    xgive_ref[...] = give[:, :width]


def turn(place, oqa, oqb):
    width, rows = oqa.shape
    vm = pl.BlockSpec(memory_space=pltpu.VMEM)
    return pl.pallas_call(
        turn_kernel,
        in_specs=[pl.BlockSpec(memory_space=pltpu.SMEM)] + [vm] * 2,
        out_specs=[vm] * 4,
        out_shape=[jax.ShapeDtypeStruct((rows, width), BF)] * 2
        + [jax.ShapeDtypeStruct((rows, width // 2), BF)] * 2,
        compiler_params=params(),
        cost_estimate=cost(0, 10 * rows * width),
    )(place, oqa, oqb)


def heads_kernel(place_ref, mine_ref, peer_ref, xmine_ref, xpeer_ref, x_ref, gq_ref):
    first = place_ref[0] == 0
    width = gq_ref.shape[1]

    def put(near, far):
        return jnp.concatenate(
            [jnp.where(first, near, far), jnp.where(first, far, near)], axis=1
        )

    mine, peer = mine_ref[...], peer_ref[...]
    x_ref[:, :width] = put(mine[:, : width // 2], peer[:, : width // 2])
    x_ref[:, width:] = put(xmine_ref[...], xpeer_ref[...])
    gq_ref[...] = put(mine[:, width // 2 :], peer[:, width // 2 :])


def heads(place, mine, peer, xmine, xpeer):
    rows, width = mine.shape
    vm = pl.BlockSpec(memory_space=pltpu.VMEM)
    return pl.pallas_call(
        heads_kernel,
        in_specs=[pl.BlockSpec(memory_space=pltpu.SMEM)] + [vm] * 4,
        out_specs=[vm] * 2,
        out_shape=[
            jax.ShapeDtypeStruct((rows, 2 * width), BF),
            jax.ShapeDtypeStruct((rows, width), BF),
        ],
        compiler_params=params(),
        cost_estimate=cost(0, 12 * rows * width),
    )(place, mine, peer, xmine, xpeer)


def project_kernel(here_ref, there_ref, *refs):
    columns, out_ref = refs[:-1], refs[-1]
    cols = columns[0].shape[0]
    total = None
    for i, w in enumerate(columns):
        ref = (here_ref, there_ref)[i % 2]
        c = i // 2 * cols
        part = jnp.dot(ref[:, c : c + cols], w[...], preferred_element_type=F32)
        total = part if total is None else total + part
    out_ref[...] = total.astype(BF)


def project(here, there, columns):
    rows, cols = here.shape[0], columns[0].shape[1]
    vm = pl.BlockSpec(memory_space=pltpu.VMEM)
    return pl.pallas_call(
        project_kernel,
        in_specs=[vm] * (2 + len(columns)),
        out_specs=vm,
        out_shape=jax.ShapeDtypeStruct((rows, cols), BF),
        compiler_params=params(),
        cost_estimate=cost(2 * rows * cols * 4 * cols, 12 * rows * cols),
    )(here, there, *columns)


def spread_kernel(groups, place_ref, *refs):
    held, out_ref, buf = refs[:groups], refs[-2], refs[-1]
    _, rows, step = held[0].shape
    for d, ref in enumerate(held):
        buf[d] = ref[...].astype(F32)
    for y in range(2):
        for g in range(groups):
            out_ref[y * rows : (y + 1) * rows, g * step : (g + 1) * step] = buf[
                g ^ place_ref[2], y ^ place_ref[0]
            ]


def spread(place, held, *after):
    groups = len(held)
    _, rows, step = held[0].shape
    vm = pl.BlockSpec(memory_space=pltpu.VMEM)
    return pl.pallas_call(
        functools.partial(spread_kernel, groups),
        in_specs=[pl.BlockSpec(memory_space=pltpu.SMEM)]
        + [vm] * groups
        + [pl.BlockSpec(memory_space=pl.ANY)] * len(after),
        out_specs=vm,
        out_shape=jax.ShapeDtypeStruct((2 * rows, groups * step), F32),
        scratch_shapes=[pltpu.VMEM((groups, 2, rows, step), F32)],
        compiler_params=params(),
        cost_estimate=cost(0, 2 * groups * rows * step * 6),
    )(place, *held, *after)


def on_device(
    groups,
    student_query,
    teacher_key,
    teacher_value,
    clip_order,
    band_start,
    band_end,
    output_weight,
    cotangent,
):
    shards = 2 * groups
    me = lax.axis_index("tm")
    clip = lax.axis_index("clip")
    half = me % 2
    z = me // 2
    place = jnp.stack([half, clip, z]).astype(jnp.int32)
    clips = lax.axis_size("clip")
    teacher_rows = teacher_key.shape[0]
    rows, feats = student_query.shape
    piece = teacher_rows // shards
    slots = feats // HDIM // 2
    hw = slots * HDIM

    def swap(x, d):
        return lax.ppermute(x, "tm", [(i, i ^ d) for i in range(shards)])

    def swap_clip(x, d):
        return lax.ppermute(x, "clip", [(i, i ^ d) for i in range(clips)])

    def swap_both(x, d):
        n = shards * clips
        return lax.ppermute(x, ("tm", "clip"), [(i, i ^ (clips + d)) for i in range(n)])

    def up(x):
        return lax.ppermute(x, "tm", [(i, i + 2) for i in range(shards - 2)])

    def down(x):
        return lax.ppermute(x, "tm", [(i + 2, i) for i in range(shards - 2)])

    here = jnp.stack([cotangent, swap_clip(cotangent, 2)])
    there = swap_clip(here, 1)
    blocks = band_start.shape[0]
    band = jnp.stack([band_start, band_end]).astype(BF)
    band = jnp.pad(band, ((0, 14), (0, 2 * hw - blocks)))
    qg_mine, qg_give = student_side(
        place, here, there, output_weight, student_query, band, slots
    )
    qg_peer = swap(qg_give, 1)
    sent = [pack(teacher_key, teacher_value, groups, slots, 0)]
    sent += [
        pack(teacher_key, teacher_value, groups, slots, s, qg_peer) for s in range(1, slots)
    ]
    qga = jnp.where(half == 0, qg_mine, qg_peer)
    qgb = jnp.where(half == 0, qg_peer, qg_mine)

    origin = z * 2 * blocks

    def limits(first_rows, *firsts):
        bands = [x[rows : rows + 2, :blocks] for x in first_rows]
        bands = jnp.concatenate(bands, axis=1).astype(F32).astype(jnp.int32)
        frame = [origin + f + jnp.arange(blocks, dtype=jnp.int32) for f in firsts]
        frame = jnp.concatenate(frame)
        lo = jnp.maximum(frame + bands[0], 0) - origin
        hi = jnp.minimum(frame + bands[1], shards * blocks - 1) - origin
        return jnp.stack([lo, hi])

    own_limits = limits((qga, qgb), 0, blocks)

    def columns_for(d):
        c = (clip ^ d) * feats
        return lax.dynamic_slice_in_dim(output_weight, c, feats, axis=1)

    columns = [columns_for(0)] + [swap_clip(columns_for(d), d) for d in range(1, clips)]

    lookup = lax.dynamic_slice_in_dim(clip_order, z * 2 * teacher_rows, 2 * teacher_rows)
    index = lookup // teacher_rows * piece + lookup % piece

    kvs, parts = [], []
    for s in range(slots):
        arrived = lax.all_to_all(
            sent[s].reshape(shards, 2 * piece, 2 * HDIM), "tm", 0, 0
        )
        kvs += put_in_order(arrived, index, teacher_rows, *parts[-2:])
        if s == slots - 1:
            far = attend(
                range(slots), 2, rows, halo_limits, qg_left, qg_right, kvs, BF
            )
            parts += attend([s], 4, rows, own_limits, qga, qgb, kvs[-2:], F32, *far)
        else:
            parts += attend([s], 4, rows, own_limits, qga, qgb, kvs[-2:], F32)
        if s == 0:
            edge_a, edge_b = edges(place, qg_mine, qg_peer, parts[0])
            qg_left, qg_right = up(edge_b), down(edge_a)
            halo_limits = limits((qg_left, qg_right), -blocks, 2 * blocks)
            cot = whole_cotangent(place, here, there, parts[0])
    parts += [up(far[1]), down(far[0])]
    oqa, oqb, *got = combine(place, cot, swap(cot, 1), parts, groups, slots)
    mine, give, xmine, xgive = turn(place, oqa, oqb)
    total = got[0].astype(F32)
    for d in range(1, groups):
        total += swap(got[d], 2 * d).astype(F32)
    total = total.astype(BF)
    both = jnp.stack([total, swap(total, 1)])
    held = [both] + [swap(both, 2 * d) for d in range(1, groups)]
    near, grad_query = heads(
        place, mine, swap(give, 1), swap_clip(xmine, 2), swap_both(xgive, 2)
    )
    joined = project(near, swap_clip(near, 1), columns)
    return joined, grad_query, spread(place, held, joined)


def solution(mesh):
    return jax.shard_map(
        functools.partial(on_device, mesh.shape["tm"] // 2),
        mesh=mesh,
        in_specs=(
            P("tm", "clip"),
            P("tm", "clip"),
            P("tm", "clip"),
            P(),
            P("tm"),
            P("tm"),
            P("clip", None),
            P("tm", "clip"),
        ),
        out_specs=(P("tm", "clip"), P("tm", "clip"), P("clip", None)),
        check_vma=False,
    )
```

profile of v0, /device:TPU:0, one launch (start us, length us, event | category | flops | bytes accessed | tf_op | source)
XLA Modules:
  0.0 142.0 jit_solution(3576433028195435302)
XLA Ops:
  0.6 1.2 copy-done
  1.9 1.2 copy-done.2
  3.1 1.8 %shard_map.104 = bf16[4,2,512,128]{3,2,1,0:T(8,128)(2,1)} custom-call(bf16[2048,256]{1,0:T(8,128)(2,1)S(1)} %copy-done, bf16[2048,256]{1,0:T(8,128)(2,1)S(1)} %copy-done.2), custom_call_target="tpu_custom_call" | custom-call | bytes 3145728 | tf_op jit(solution)/shard_map/pallas_call | solution.py:48
  4.9 7.4 %all-to-all-start = ((bf16[8,512,128]{2,1,0:T(8,128)(2,1)}), bf16[8,512,128]{2,1,0:T(8,128)(2,1)}, u32[]{:S(2)}, u32[]{:S(2)}) async-start(bf16[8,512,128]{2,1,0:T(8,128)(2,1)} %bitcast.8), calls=%async_computation | async-start | bytes 2097152 | tf_op jit(solution)/shard_map/all_to_all | solution.py:596
  12.4 1.6 %collective-permute-start = (bf16[512,256]{1,0:T(8,128)(2,1)S(1)}, bf16[512,256]{1,0:T(8,128)(2,1)S(1)}, u32[]{:S(2)}, u32[]{:S(2)}) collective-permute-start(bf16[512,256]{1,0:T(8,128)(2,1)S(1)} %copy-done.20), channel_id=1, source_target_pairs={{0,2},{1,3},{2,0},{3,1},{4,6},{5,7},{6,4},{7,5},{8,10},{9,11},{10,... | collective-permute-start | bytes 786440 | tf_op jit(solution)/shard_map/ppermute | solution.py:544
  13.9 6.3 %collective-permute-done = bf16[512,256]{1,0:T(8,128)(2,1)S(1)} collective-permute-done((bf16[512,256]{1,0:T(8,128)(2,1)S(1)}, bf16[512,256]{1,0:T(8,128)(2,1)S(1)}, u32[]{:S(2)}, u32[]{:S(2)}) %collective-permute-start) | collective-permute-done | bytes 262176 | tf_op jit(solution)/shard_map/ppermute | solution.py:544
  20.5 1.9 %collective-permute-done.1.there_ref = bf16[2,512,256]{2,1,0:T(8,128)(2,1)} collective-permute-done((bf16[2,512,256]{2,1,0:T(8,128)(2,1)S(1)}, bf16[2,512,256]{2,1,0:T(8,128)(2,1)}, u32[]{:S(2)}, u32[]{:S(2)}) %collective-permute-start.1) | collective-permute-done | bytes 524320 | tf_op jit(solution)/shard_map/ppermute | solution.py:544
  22.4 0.9 copy-done.15
  23.3 2.3 %shard_map.103 = (bf16[528,256]{1,0:T(8,128)(2,1)S(1)}, bf16[528,256]{1,0:T(8,128)(2,1)}) custom-call(s32[3]{0:T(128)S(1)} %pad_add_fusion.2.place_ref, bf16[2,512,256]{2,1,0:T(8,128)(2,1)S(1)} %pad_maximum_fusion.here_ref, bf16[2,512,256]{2,1,0:T(8,128)(2,1)} %collective-permute-done.1.there_ref, bf16[256,1024]{1,0:T(8,128)(2,1)S(1)} %copy-done.5, ...), custom_call_target="tpu_custom_call" | custom-call | flops 268435456 | bytes 2097152 | tf_op jit(solution)/shard_map/pallas_call | solution.py:128
  26.3 1.7 %collective-permute-start.2 = (bf16[528,256]{1,0:T(8,128)(2,1)}, bf16[528,256]{1,0:T(8,128)(2,1)S(1)}, u32[]{:S(2)}, u32[]{:S(2)}) collective-permute-start(bf16[528,256]{1,0:T(8,128)(2,1)} %get-tuple-element.30), channel_id=1, source_target_pairs={{0,4},{4,0},{8,12},{12,8},{16,20},{20,16},{24,28},{28,24},{1,5},{5... | collective-permute-start | bytes 811016 | tf_op jit(solution)/shard_map/ppermute | solution.py:541
  28.0 0.7 fusion.2
  28.7 8.1 %collective-permute-done.2.refs_0_.peer_ref = bf16[528,256]{1,0:T(8,128)(2,1)S(1)} collective-permute-done((bf16[528,256]{1,0:T(8,128)(2,1)}, bf16[528,256]{1,0:T(8,128)(2,1)S(1)}, u32[]{:S(2)}, u32[]{:S(2)}) %collective-permute-start.2) | collective-permute-done | bytes 270368 | tf_op jit(solution)/shard_map/ppermute | solution.py:541
  37.5 1.0 copy-done.4
  38.5 6.7 %all-to-all-start.1 = ((bf16[8,512,128]{2,1,0:T(8,128)(2,1)}), bf16[8,512,128]{2,1,0:T(8,128)(2,1)}, u32[]{:S(2)}, u32[]{:S(2)}) async-start(bf16[8,512,128]{2,1,0:T(8,128)(2,1)} %bitcast.14), calls=%async_computation.1 | async-start | bytes 2097152 | tf_op jit(solution)/shard_map/all_to_all | solution.py:596
  45.4 3.9 %shard_map.105 = (bf16[4096,128]{1,0:T(8,128)(2,1)S(1)}, bf16[128,4096]{1,0:T(8,128)(2,1)S(1)}) custom-call(s32[2,1,2048]{2,1,0:T(1,128)S(1)} %bitcast.15, bf16[8,512,128]{2,1,0:T(8,128)(2,1)} %all-to-all-done.arr_ref), custom_call_target="tpu_custom_call" | custom-call | flops 2147483648 | bytes 3145728 | tf_op jit(solution)/shard_map/pallas_call | solution.py:78
  49.3 7.6 %shard_map.106 = (f32[208,512]{1,0:T(8,128)S(1)}, f32[208,512]{1,0:T(8,128)S(1)}) custom-call(s32[2,32]{1,0:T(2,128)S(1)} %pad_add_fusion.lohi_ref, bf16[528,256]{1,0:T(8,128)(2,1)S(1)} %get-tuple-element.55.qga_ref, bf16[528,256]{1,0:T(8,128)(2,1)S(1)} %get-tuple-element.56.qgb_ref, bf16[4096,128]{1,0:T(8,128)(2,1)S(1)} %get-tuple-element.31.refs_0_, ...), custom_call_target="tpu_custom_call" | custom-call | flops 2147483648 | bytes 4194304 | tf_op jit(solution)/shard_map/pallas_call | solution.py:326
  57.0 1.4 shard_map.110
  58.4 5.5 %collective-permute-start.4 = (bf16[528,256]{1,0:T(8,128)(2,1)}, bf16[528,256]{1,0:T(8,128)(2,1)S(1)}, u32[]{:S(2)}, u32[]{:S(2)}) collective-permute-start(bf16[528,256]{1,0:T(8,128)(2,1)} %get-tuple-element.37), channel_id=1, source_target_pairs={{0,8},{4,12},{8,16},{12,20},{16,24},{20,28},{1,9},{5,13},{9,17},{1... | collective-permute-start | bytes 811016 | tf_op jit(solution)/shard_map/ppermute | solution.py:551
  63.9 1.5 %collective-permute-start.5 = (bf16[528,256]{1,0:T(8,128)(2,1)}, bf16[528,256]{1,0:T(8,128)(2,1)}, u32[]{:S(2)}, u32[]{:S(2)}) collective-permute-start(bf16[528,256]{1,0:T(8,128)(2,1)} %get-tuple-element.38), channel_id=1, source_target_pairs={{8,0},{12,4},{16,8},{20,12},{24,16},{28,20},{9,1},{13,5},{17,9},{2... | collective-permute-start | bytes 811016 | tf_op jit(solution)/shard_map/ppermute | solution.py:554
  65.4 1.2 shard_map.107.cot_ref
  66.6 1.5 %collective-permute-start.3 = (bf16[512,1024]{1,0:T(8,128)(2,1)S(1)}, bf16[512,1024]{1,0:T(8,128)(2,1)}, u32[]{:S(2)}, u32[]{:S(2)}) collective-permute-start(bf16[512,1024]{1,0:T(8,128)(2,1)S(1)} %shard_map.107.cot_ref), channel_id=1, source_target_pairs={{0,4},{4,0},{8,12},{12,8},{16,20},{20,16},{24,28},{28,24},{1,5},{5... | collective-permute-start | bytes 3145736 | tf_op jit(solution)/shard_map/ppermute | solution.py:541
  68.8 7.7 %collective-permute-done.5.qgb_ref = bf16[528,256]{1,0:T(8,128)(2,1)} collective-permute-done((bf16[528,256]{1,0:T(8,128)(2,1)}, bf16[528,256]{1,0:T(8,128)(2,1)}, u32[]{:S(2)}, u32[]{:S(2)}) %collective-permute-start.5) | collective-permute-done | bytes 270368 | tf_op jit(solution)/shard_map/ppermute | solution.py:554
  77.4 4.0 %shard_map.109 = (bf16[4096,128]{1,0:T(8,128)(2,1)S(1)}, bf16[128,4096]{1,0:T(8,128)(2,1)S(1)}) custom-call(s32[2,1,2048]{2,1,0:T(1,128)S(1)} %bitcast.16, bf16[8,512,128]{2,1,0:T(8,128)(2,1)} %all-to-all-done.1.arr_ref, f32[208,512]{1,0:T(8,128)S(1)} %get-tuple-element.33.after_ref.refs_0_, f32[208,512]{1,0:T(8,128)S(1)} %copy-done.10), custom_call_target="tpu_custom_call" | custom-call | flops 2147483648 | bytes 3145728 | tf_op jit(solution)/shard_map/pallas_call | solution.py:78
  81.4 7.9 %shard_map.111 = (bf16[416,512]{1,0:T(8,128)(2,1)S(1)}, bf16[416,512]{1,0:T(8,128)(2,1)S(1)}) custom-call(s32[2,32]{1,0:T(2,128)S(1)} %pad_add_fusion.1.lohi_ref, bf16[528,256]{1,0:T(8,128)(2,1)S(1)} %collective-permute-done.4.qga_ref, bf16[528,256]{1,0:T(8,128)(2,1)} %collective-permute-done.5.qgb_ref, bf16[4096,128]{1,0:T(8,128)(2,1)S(1)} %copy-done.17, ...), custom_call_target="tpu_custom_call" | custom-call | flops 4294967296 | bytes 8388608 | tf_op jit(solution)/shard_map/pallas_call | solution.py:326
  89.3 4.5 %collective-permute-start.6 = (bf16[416,512]{1,0:T(8,128)(2,1)S(1)}, bf16[416,512]{1,0:T(8,128)(2,1)S(1)}, u32[]{:S(2)}, u32[]{:S(2)}) collective-permute-start(bf16[416,512]{1,0:T(8,128)(2,1)S(1)} %get-tuple-element.40.refs_3_), channel_id=1, source_target_pairs={{0,8},{4,12},{8,16},{12,20},{16,24},{20,28},{1,9},{5,13},{9,17},{1... | collective-permute-start | bytes 1277960 | tf_op jit(solution)/shard_map/ppermute | solution.py:551
  93.9 1.3 collective-permute-start.7
  95.2 7.7 %shard_map.112 = (f32[208,512]{1,0:T(8,128)S(1)}, f32[208,512]{1,0:T(8,128)S(1)}) custom-call(s32[2,32]{1,0:T(2,128)S(1)} %pad_add_fusion.lohi_ref, bf16[528,256]{1,0:T(8,128)(2,1)S(1)} %copy-done.12, bf16[528,256]{1,0:T(8,128)(2,1)S(1)} %copy-done.14, bf16[4096,128]{1,0:T(8,128)(2,1)S(1)} %get-tuple-element.35.refs_2_.refs_0_, ...), custom_call_target="tpu_custom_call" | custom-call | flops 2147483648 | bytes 4194304 | tf_op jit(solution)/shard_map/pallas_call | solution.py:326
  102.9 2.8 %collective-permute-done.7.refs_5_ = bf16[416,512]{1,0:T(8,128)(2,1)S(1)} collective-permute-done((bf16[416,512]{1,0:T(8,128)(2,1)S(1)}, bf16[416,512]{1,0:T(8,128)(2,1)S(1)}, u32[]{:S(2)}, u32[]{:S(2)}) %collective-permute-start.7) | collective-permute-done | bytes 426016 | tf_op jit(solution)/shard_map/ppermute | solution.py:554
  105.7 2.8 %shard_map.113 = (bf16[256,512]{1,0:T(8,128)(2,1)S(1)}, bf16[256,512]{1,0:T(8,128)(2,1)S(1)}, bf16[128,256]{1,0:T(8,128)(2,1)S(1)}, bf16[128,256]{1,0:T(8,128)(2...) custom-call(s32[3]{0:T(128)S(1)} %pad_add_fusion.2.place_ref, bf16[512,1024]{1,0:T(8,128)(2,1)S(1)} %shard_map.107.cot_ref, ...), custom_call_target="tpu_custom_call" | custom-call | flops 268435456 | bytes 8388608 | tf_op jit(solution)/shard_map/pallas_call | solution.py:391
  109.3 1.1 collective-permute-start.8
  110.3 1.9 %collective-permute-start.10 = (bf16[512,128]{1,0:T(8,128)(2,1)S(1)}, bf16[512,128]{1,0:T(8,128)(2,1)S(1)}, u32[]{:S(2)}, u32[]{:S(2)}) collective-permute-start(bf16[512,128]{1,0:T(8,128)(2,1)S(1)} %get-tuple-element.48), channel_id=1, source_target_pairs={{0,6},{1,7},{2,4},{3,5},{4,2},{5,3},{6,0},{7,1},{8,14},{9,15},{10,... | collective-permute-start | bytes 393224 | tf_op jit(solution)/shard_map/ppermute | solution.py:548
  112.8 1.5 %collective-permute-start.15 = (bf16[128,256]{1,0:T(8,128)(2,1)}, bf16[128,256]{1,0:T(8,128)(2,1)S(1)}, u32[]{:S(2)}, u32[]{:S(2)}) collective-permute-start(bf16[128,256]{1,0:T(8,128)(2,1)} %get-tuple-element.52), channel_id=1, source_target_pairs={{0,8},{4,12},{8,0},{12,4},{16,24},{20,28},{24,16},{28,20},{1,9},{5... | collective-permute-start | bytes 196616 | tf_op jit(solution)/shard_map/ppermute | solution.py:541
  114.3 1.1 collective-permute-start.16
  115.5 0.9 collective-permute-done.10.xpeer_ref
  116.3 0.9 collective-permute-start.17
  117.7 1.3 shard_map.115
  119.0 1.4 %collective-permute-done.16 = bf16[128,256]{1,0:T(8,128)(2,1)S(1)} collective-permute-done((bf16[128,256]{1,0:T(8,128)(2,1)}, bf16[128,256]{1,0:T(8,128)(2,1)S(1)}, u32[]{:S(2)}, u32[]{:S(2)}) %collective-permute-start.16) | collective-permute-done | bytes 65568 | tf_op jit(solution)/shard_map/ppermute | solution.py:541
  120.4 2.1 %collective-permute-done.17 = bf16[128,256]{1,0:T(8,128)(2,1)S(1)} collective-permute-done((bf16[128,256]{1,0:T(8,128)(2,1)S(1)}, bf16[128,256]{1,0:T(8,128)(2,1)S(1)}, u32[]{:S(2)}, u32[]{:S(2)}) %collective-permute-start.17) | collective-permute-done | bytes 65568 | tf_op jit(solution)/shard_map/ppermute | solution.py:541
  122.5 1.0 collective-permute-start.18
  123.6 1.6 %collective-permute-start.13 = (bf16[256,256]{1,0:T(8,128)(2,1)S(1)}, bf16[256,256]{1,0:T(8,128)(2,1)S(1)}, u32[]{:S(2)}, u32[]{:S(2)}) collective-permute-start(bf16[256,256]{1,0:T(8,128)(2,1)S(1)} %get-tuple-element.60), channel_id=1, source_target_pairs={{0,2},{1,3},{2,0},{3,1},{4,6},{5,7},{6,4},{7,5},{8,10},{9,11},{10,... | collective-permute-start | bytes 393224 | tf_op jit(solution)/shard_map/ppermute | solution.py:544
  125.5 1.3 collective-permute-done.18
  126.9 1.3 collective-permute-start.20
  128.3 1.7 %collective-permute-done.13.refs_2_ = bf16[256,256]{1,0:T(8,128)(2,1)S(1)} collective-permute-done((bf16[256,256]{1,0:T(8,128)(2,1)S(1)}, bf16[256,256]{1,0:T(8,128)(2,1)S(1)}, u32[]{:S(2)}, u32[]{:S(2)}) %collective-permute-start.13) | collective-permute-done | bytes 131104 | tf_op jit(solution)/shard_map/ppermute | solution.py:544
  130.0 1.3 collective-permute-start.21
  131.9 1.1 shard_map.116.refs_4_
  133.1 6.3 %collective-permute-done.20.refs_2_ = bf16[2,128,256]{2,1,0:T(8,128)(2,1)S(1)} collective-permute-done((bf16[2,128,256]{2,1,0:T(8,128)(2,1)S(1)}, bf16[2,128,256]{2,1,0:T(8,128)(2,1)S(1)}, u32[]{:S(2)}, u32[]{:S(2)}) %collective-permute-start.20) | collective-permute-done | bytes 131104 | tf_op jit(solution)/shard_map/ppermute | solution.py:541
  139.4 0.9 copy-done.8
  140.3 1.6 %shard_map.117 = f32[256,1024]{1,0:T(8,128)} custom-call(s32[3]{0:T(128)S(1)} %pad_add_fusion.2.place_ref, bf16[2,128,256]{2,1,0:T(8,128)(2,1)S(1)} %pad_maximum_fusion.1.refs_0_, bf16[2,128,256]{2,1,0:T(8,128)(2,1)S(1)} %collective-permute-done.19.refs_1_, bf16[2,128,256]{2,1,0:T(8,128)(2,1)S(1)} %collective-permute-done.20.refs_2_, ...), custom_call_target="tpu_custom_call" | custom-call | bytes 1572864 | tf_op jit(solution)/shard_map/pallas_call | solution.py:503
  (82 shorter events, 6.3 us)
Async XLA Ops:
  0.6 1.2 copy-start
  1.9 1.2 copy-start.2
  4.9 7.4 %copy-start.20 = (bf16[512,256]{1,0:T(8,128)(2,1)S(1)}, bf16[512,256]{1,0:T(8,128)(2,1)}, u32[]{:S(2)}) copy-start(bf16[512,256]{1,0:T(8,128)(2,1)} %param.15) | copy-start | bytes 786436
  4.9 15.5 %copy-start.21 = (s32[16]{0:T(128)S(1)}, s32[16]{0:T(128)}, u32[]{:S(2)}) copy-start(s32[16]{0:T(128)} %param.13) | copy-start | bytes 196
  4.9 15.5 %copy-start.22 = (s32[16]{0:T(128)S(1)}, s32[16]{0:T(128)}, u32[]{:S(2)}) copy-start(s32[16]{0:T(128)} %param.12) | copy-start | bytes 196
  4.9 17.4 %copy-start.5 = (bf16[256,1024]{1,0:T(8,128)(2,1)S(1)}, bf16[256,1024]{1,0:T(8,128)(2,1)}, u32[]{:S(2)}) copy-start(bf16[256,1024]{1,0:T(8,128)(2,1)} %w_ref.1) | copy-start | bytes 1572868
  4.9 33.5 %all-to-all-start = ((bf16[8,512,128]{2,1,0:T(8,128)(2,1)}), bf16[8,512,128]{2,1,0:T(8,128)(2,1)}, u32[]{:S(2)}, u32[]{:S(2)}) async-start(bf16[8,512,128]{2,1,0:T(8,128)(2,1)} %bitcast.8), calls=%async_computation | async-start | bytes 2097152 | tf_op jit(solution)/shard_map/all_to_all | solution.py:596
  12.4 7.8 %collective-permute-start = (bf16[512,256]{1,0:T(8,128)(2,1)S(1)}, bf16[512,256]{1,0:T(8,128)(2,1)S(1)}, u32[]{:S(2)}, u32[]{:S(2)}) collective-permute-start(bf16[512,256]{1,0:T(8,128)(2,1)S(1)} %copy-done.20), channel_id=1, source_target_pairs={{0,2},{1,3},{2,0},{3,1},{4,6},{5,7},{6,4},{7,5},{8,10},{9,11},{10,... | collective-permute-start | bytes 786440 | tf_op jit(solution)/shard_map/ppermute | solution.py:544
  20.2 16.7 %copy-start.3 = (bf16[2048,256]{1,0:T(8,128)(2,1)S(1)}, bf16[2048,256]{1,0:T(8,128)(2,1)}, u32[]{:S(2)}) copy-start(bf16[2048,256]{1,0:T(8,128)(2,1)} %v_ref.3) | copy-start | bytes 3145732
  20.2 16.6 %copy-start.1 = (bf16[2048,256]{1,0:T(8,128)(2,1)S(1)}, bf16[2048,256]{1,0:T(8,128)(2,1)}, u32[]{:S(2)}) copy-start(bf16[2048,256]{1,0:T(8,128)(2,1)} %k_ref.3) | copy-start | bytes 3145732
  20.2 2.1 %collective-permute-start.1 = (bf16[2,512,256]{2,1,0:T(8,128)(2,1)S(1)}, bf16[2,512,256]{2,1,0:T(8,128)(2,1)}, u32[]{:S(2)}, u32[]{:S(2)}) collective-permute-start(bf16[2,512,256]{2,1,0:T(8,128)(2,1)S(1)} %pad_maximum_fusion.here_ref), channel_id=1, source_target_pairs={{0,1},{1,0},{2,3},{3,2},{4,5},{5,4},{6,7},{7,6},{8,9},{9,8},{10,11... | collective-permute-start | bytes 1572872 | tf_op jit(solution)/shard_map/ppermute | solution.py:544
  22.4 1.0 copy-start.15
  25.6 0.7 copy-start.6
  26.3 10.5 %collective-permute-start.2 = (bf16[528,256]{1,0:T(8,128)(2,1)}, bf16[528,256]{1,0:T(8,128)(2,1)S(1)}, u32[]{:S(2)}, u32[]{:S(2)}) collective-permute-start(bf16[528,256]{1,0:T(8,128)(2,1)} %get-tuple-element.30), channel_id=1, source_target_pairs={{0,4},{4,0},{8,12},{12,8},{16,20},{20,16},{24,28},{28,24},{1,5},{5... | collective-permute-start | bytes 811016 | tf_op jit(solution)/shard_map/ppermute | solution.py:541
  37.5 1.0 copy-start.4
  38.5 6.7 %copy-start.7 = (bf16[528,256]{1,0:T(8,128)(2,1)S(1)}, bf16[528,256]{1,0:T(8,128)(2,1)}, u32[]{:S(2)}) copy-start(bf16[528,256]{1,0:T(8,128)(2,1)} %copy-done.6) | copy-start | bytes 811012
  38.5 38.9 %all-to-all-start.1 = ((bf16[8,512,128]{2,1,0:T(8,128)(2,1)}), bf16[8,512,128]{2,1,0:T(8,128)(2,1)}, u32[]{:S(2)}, u32[]{:S(2)}) async-start(bf16[8,512,128]{2,1,0:T(8,128)(2,1)} %bitcast.14), calls=%async_computation.1 | async-start | bytes 2097152 | tf_op jit(solution)/shard_map/all_to_all | solution.py:596
  45.2 4.1 %copy-start.11 = (bf16[528,256]{1,0:T(8,128)(2,1)}, bf16[528,256]{1,0:T(8,128)(2,1)S(1)}, u32[]{:S(2)}) copy-start(bf16[528,256]{1,0:T(8,128)(2,1)S(1)} %get-tuple-element.55.qga_ref) | copy-start | bytes 811012
  45.2 4.1 %copy-start.13 = (bf16[528,256]{1,0:T(8,128)(2,1)}, bf16[528,256]{1,0:T(8,128)(2,1)S(1)}, u32[]{:S(2)}) copy-start(bf16[528,256]{1,0:T(8,128)(2,1)S(1)} %get-tuple-element.56.qgb_ref) | copy-start | bytes 811012
  49.3 7.7 %copy-start.16 = (bf16[4096,128]{1,0:T(8,128)(2,1)}, bf16[4096,128]{1,0:T(8,128)(2,1)S(1)}, u32[]{:S(2)}) copy-start(bf16[4096,128]{1,0:T(8,128)(2,1)S(1)} %get-tuple-element.31.refs_0_) | copy-start | bytes 3145732
  49.3 7.7 %copy-start.18 = (bf16[128,4096]{1,0:T(8,128)(2,1)}, bf16[128,4096]{1,0:T(8,128)(2,1)S(1)}, u32[]{:S(2)}) copy-start(bf16[128,4096]{1,0:T(8,128)(2,1)S(1)} %get-tuple-element.32.refs_1_) | copy-start | bytes 3145732
  57.0 1.4 copy-start.9
  58.4 10.4 %collective-permute-start.4 = (bf16[528,256]{1,0:T(8,128)(2,1)}, bf16[528,256]{1,0:T(8,128)(2,1)S(1)}, u32[]{:S(2)}, u32[]{:S(2)}) collective-permute-start(bf16[528,256]{1,0:T(8,128)(2,1)} %get-tuple-element.37), channel_id=1, source_target_pairs={{0,8},{4,12},{8,16},{12,20},{16,24},{20,28},{1,9},{5,13},{9,17},{1... | collective-permute-start | bytes 811016 | tf_op jit(solution)/shard_map/ppermute | solution.py:551
  63.9 12.6 %collective-permute-start.5 = (bf16[528,256]{1,0:T(8,128)(2,1)}, bf16[528,256]{1,0:T(8,128)(2,1)}, u32[]{:S(2)}, u32[]{:S(2)}) collective-permute-start(bf16[528,256]{1,0:T(8,128)(2,1)} %get-tuple-element.38), channel_id=1, source_target_pairs={{8,0},{12,4},{16,8},{20,12},{24,16},{28,20},{9,1},{13,5},{17,9},{2... | collective-permute-start | bytes 811016 | tf_op jit(solution)/shard_map/ppermute | solution.py:554
  65.4 12.0 %copy-start.10 = (f32[208,512]{1,0:T(8,128)S(1)}, f32[208,512]{1,0:T(8,128)}, u32[]{:S(2)}) copy-start(f32[208,512]{1,0:T(8,128)} %copy-done.9) | copy-start | bytes 1277956
  66.6 36.3 %collective-permute-start.3 = (bf16[512,1024]{1,0:T(8,128)(2,1)S(1)}, bf16[512,1024]{1,0:T(8,128)(2,1)}, u32[]{:S(2)}, u32[]{:S(2)}) collective-permute-start(bf16[512,1024]{1,0:T(8,128)(2,1)S(1)} %shard_map.107.cot_ref), channel_id=1, source_target_pairs={{0,4},{4,0},{8,12},{12,8},{16,20},{20,16},{24,28},{28,24},{1,5},{5... | collective-permute-start | bytes 3145736 | tf_op jit(solution)/shard_map/ppermute | solution.py:541
  77.3 4.0 %copy-start.17 = (bf16[4096,128]{1,0:T(8,128)(2,1)S(1)}, bf16[4096,128]{1,0:T(8,128)(2,1)}, u32[]{:S(2)}) copy-start(bf16[4096,128]{1,0:T(8,128)(2,1)} %copy-done.16) | copy-start | bytes 3145732
  77.4 4.0 %copy-start.19 = (bf16[128,4096]{1,0:T(8,128)(2,1)S(1)}, bf16[128,4096]{1,0:T(8,128)(2,1)}, u32[]{:S(2)}) copy-start(bf16[128,4096]{1,0:T(8,128)(2,1)} %copy-done.18) | copy-start | bytes 3145732
  81.4 13.8 %copy-start.12 = (bf16[528,256]{1,0:T(8,128)(2,1)S(1)}, bf16[528,256]{1,0:T(8,128)(2,1)}, u32[]{:S(2)}) copy-start(bf16[528,256]{1,0:T(8,128)(2,1)} %copy-done.11) | copy-start | bytes 811012
  81.4 13.8 %copy-start.14 = (bf16[528,256]{1,0:T(8,128)(2,1)S(1)}, bf16[528,256]{1,0:T(8,128)(2,1)}, u32[]{:S(2)}) copy-start(bf16[528,256]{1,0:T(8,128)(2,1)} %copy-done.13) | copy-start | bytes 811012
  89.3 13.6 %collective-permute-start.6 = (bf16[416,512]{1,0:T(8,128)(2,1)S(1)}, bf16[416,512]{1,0:T(8,128)(2,1)S(1)}, u32[]{:S(2)}, u32[]{:S(2)}) collective-permute-start(bf16[416,512]{1,0:T(8,128)(2,1)S(1)} %get-tuple-element.40.refs_3_), channel_id=1, source_target_pairs={{0,8},{4,12},{8,16},{12,20},{16,24},{20,28},{1,9},{5,13},{9,17},{1... | collective-permute-start | bytes 1277960 | tf_op jit(solution)/shard_map/ppermute | solution.py:551
  93.9 11.9 %collective-permute-start.7 = (bf16[416,512]{1,0:T(8,128)(2,1)S(1)}, bf16[416,512]{1,0:T(8,128)(2,1)S(1)}, u32[]{:S(2)}, u32[]{:S(2)}) collective-permute-start(bf16[416,512]{1,0:T(8,128)(2,1)S(1)} %get-tuple-element.39.refs_2_), channel_id=1, source_target_pairs={{8,0},{12,4},{16,8},{20,12},{24,16},{28,20},{9,1},{13,5},{17,9},{2... | collective-permute-start | bytes 1277960 | tf_op jit(solution)/shard_map/ppermute | solution.py:554
  109.3 8.4 %collective-permute-start.8 = (bf16[512,256]{1,0:T(8,128)(2,1)S(1)}, bf16[512,256]{1,0:T(8,128)(2,1)S(1)}, u32[]{:S(2)}, u32[]{:S(2)}) collective-permute-start(bf16[512,256]{1,0:T(8,128)(2,1)S(1)} %get-tuple-element.46), channel_id=1, source_target_pairs={{0,4},{4,0},{8,12},{12,8},{16,20},{20,16},{24,28},{28,24},{1,5},{5... | collective-permute-start | bytes 786440 | tf_op jit(solution)/shard_map/ppermute | solution.py:541
  110.3 6.0 %collective-permute-start.10 = (bf16[512,128]{1,0:T(8,128)(2,1)S(1)}, bf16[512,128]{1,0:T(8,128)(2,1)S(1)}, u32[]{:S(2)}, u32[]{:S(2)}) collective-permute-start(bf16[512,128]{1,0:T(8,128)(2,1)S(1)} %get-tuple-element.48), channel_id=1, source_target_pairs={{0,6},{1,7},{2,4},{3,5},{4,2},{5,3},{6,0},{7,1},{8,14},{9,15},{10,... | collective-permute-start | bytes 393224 | tf_op jit(solution)/shard_map/ppermute | solution.py:548
  112.3 5.0 %collective-permute-start.9 = (bf16[512,128]{1,0:T(8,128)(2,1)S(1)}, bf16[512,128]{1,0:T(8,128)(2,1)S(1)}, u32[]{:S(2)}, u32[]{:S(2)}) collective-permute-start(bf16[512,128]{1,0:T(8,128)(2,1)S(1)} %get-tuple-element.47), channel_id=1, source_target_pairs={{0,2},{1,3},{2,0},{3,1},{4,6},{5,7},{6,4},{7,5},{8,10},{9,11},{10,... | collective-permute-start | bytes 393224 | tf_op jit(solution)/shard_map/ppermute | solution.py:544
  112.8 6.2 %collective-permute-start.15 = (bf16[128,256]{1,0:T(8,128)(2,1)}, bf16[128,256]{1,0:T(8,128)(2,1)S(1)}, u32[]{:S(2)}, u32[]{:S(2)}) collective-permute-start(bf16[128,256]{1,0:T(8,128)(2,1)} %get-tuple-element.52), channel_id=1, source_target_pairs={{0,8},{4,12},{8,0},{12,4},{16,24},{20,28},{24,16},{28,20},{1,9},{5... | collective-permute-start | bytes 196616 | tf_op jit(solution)/shard_map/ppermute | solution.py:541
  114.3 6.1 %collective-permute-start.16 = (bf16[128,256]{1,0:T(8,128)(2,1)}, bf16[128,256]{1,0:T(8,128)(2,1)S(1)}, u32[]{:S(2)}, u32[]{:S(2)}) collective-permute-start(bf16[128,256]{1,0:T(8,128)(2,1)} %get-tuple-element.53), channel_id=1, source_target_pairs={{0,16},{4,20},{8,24},{12,28},{16,0},{20,4},{24,8},{28,12},{1,17},{... | collective-permute-start | bytes 196616 | tf_op jit(solution)/shard_map/ppermute | solution.py:541
  116.3 6.1 %collective-permute-start.17 = (bf16[128,256]{1,0:T(8,128)(2,1)S(1)}, bf16[128,256]{1,0:T(8,128)(2,1)S(1)}, u32[]{:S(2)}, u32[]{:S(2)}) collective-permute-start(bf16[128,256]{1,0:T(8,128)(2,1)S(1)} %get-tuple-element.54), channel_id=1, source_target_pairs={{0,24},{4,28},{8,16},{12,20},{16,8},{20,12},{24,0},{28,4},{1,25},{... | collective-permute-start | bytes 196616 | tf_op jit(solution)/shard_map/ppermute | solution.py:541
  119.0 12.9 %collective-permute-start.11 = (bf16[512,512]{1,0:T(8,128)(2,1)S(1)}, bf16[512,512]{1,0:T(8,128)(2,1)S(1)}, u32[]{:S(2)}, u32[]{:S(2)}) collective-permute-start(bf16[512,512]{1,0:T(8,128)(2,1)S(1)} %get-tuple-element.49.here_ref), channel_id=1, source_target_pairs={{0,1},{1,0},{2,3},{3,2},{4,5},{5,4},{6,7},{7,6},{8,9},{9,8},{10,11... | collective-permute-start | bytes 1572872 | tf_op jit(solution)/shard_map/ppermute | solution.py:544
  122.5 4.3 %collective-permute-start.18 = (bf16[128,256]{1,0:T(8,128)(2,1)S(1)}, bf16[128,256]{1,0:T(8,128)(2,1)S(1)}, u32[]{:S(2)}, u32[]{:S(2)}) collective-permute-start(bf16[128,256]{1,0:T(8,128)(2,1)S(1)} %add_convert_fusion), channel_id=1, source_target_pairs={{0,4},{4,0},{8,12},{12,8},{16,20},{20,16},{24,28},{28,24},{1,5},{5... | collective-permute-start | bytes 196616 | tf_op jit(solution)/shard_map/ppermute | solution.py:541
  123.6 3.4 %collective-permute-start.12 = (bf16[256,256]{1,0:T(8,128)(2,1)S(1)}, bf16[256,256]{1,0:T(8,128)(2,1)S(1)}, u32[]{:S(2)}, u32[]{:S(2)}) collective-permute-start(bf16[256,256]{1,0:T(8,128)(2,1)S(1)} %get-tuple-element.58), channel_id=1, source_target_pairs={{0,1},{1,0},{2,3},{3,2},{4,5},{5,4},{6,7},{7,6},{8,9},{9,8},{10,11... | collective-permute-start | bytes 393224 | tf_op jit(solution)/shard_map/ppermute | solution.py:544
  123.6 6.4 %collective-permute-start.13 = (bf16[256,256]{1,0:T(8,128)(2,1)S(1)}, bf16[256,256]{1,0:T(8,128)(2,1)S(1)}, u32[]{:S(2)}, u32[]{:S(2)}) collective-permute-start(bf16[256,256]{1,0:T(8,128)(2,1)S(1)} %get-tuple-element.60), channel_id=1, source_target_pairs={{0,2},{1,3},{2,0},{3,1},{4,6},{5,7},{6,4},{7,5},{8,10},{9,11},{10,... | collective-permute-start | bytes 393224 | tf_op jit(solution)/shard_map/ppermute | solution.py:544
  125.2 6.7 %collective-permute-start.14 = (bf16[256,256]{1,0:T(8,128)(2,1)S(1)}, bf16[256,256]{1,0:T(8,128)(2,1)S(1)}, u32[]{:S(2)}, u32[]{:S(2)}) collective-permute-start(bf16[256,256]{1,0:T(8,128)(2,1)S(1)} %get-tuple-element.57), channel_id=1, source_target_pairs={{0,3},{1,2},{2,1},{3,0},{4,7},{5,6},{6,5},{7,4},{8,11},{9,10},{10,... | collective-permute-start | bytes 393224 | tf_op jit(solution)/shard_map/ppermute | solution.py:544
  126.8 6.3 %collective-permute-start.19 = (bf16[2,128,256]{2,1,0:T(8,128)(2,1)S(1)}, bf16[2,128,256]{2,1,0:T(8,128)(2,1)S(1)}, u32[]{:S(2)}, u32[]{:S(2)}) collective-permute-start(bf16[2,128,256]{2,1,0:T(8,128)(2,1)S(1)} %pad_maximum_fusion.1.refs_0_), channel_id=1, source_target_pairs={{0,8},{4,12},{8,0},{12,4},{16,24},{20,28},{24,16},{28,20},{1,9},{5... | collective-permute-start | bytes 393224 | tf_op jit(solution)/shard_map/ppermute | solution.py:541
  126.9 12.4 %collective-permute-start.20 = (bf16[2,128,256]{2,1,0:T(8,128)(2,1)S(1)}, bf16[2,128,256]{2,1,0:T(8,128)(2,1)S(1)}, u32[]{:S(2)}, u32[]{:S(2)}) collective-permute-start(bf16[2,128,256]{2,1,0:T(8,128)(2,1)S(1)} %pad_maximum_fusion.1.refs_0_), channel_id=1, source_target_pairs={{0,16},{4,20},{8,24},{12,28},{16,0},{20,4},{24,8},{28,12},{1,17},{... | collective-permute-start | bytes 393224 | tf_op jit(solution)/shard_map/ppermute | solution.py:541
  130.0 9.4 %collective-permute-start.21 = (bf16[2,128,256]{2,1,0:T(8,128)(2,1)S(1)}, bf16[2,128,256]{2,1,0:T(8,128)(2,1)S(1)}, u32[]{:S(2)}, u32[]{:S(2)}) collective-permute-start(bf16[2,128,256]{2,1,0:T(8,128)(2,1)S(1)} %pad_maximum_fusion.1.refs_0_), channel_id=1, source_target_pairs={{0,24},{4,28},{8,16},{12,20},{16,8},{20,12},{24,0},{28,4},{1,25},{... | collective-permute-start | bytes 393224 | tf_op jit(solution)/shard_map/ppermute | solution.py:541
  139.4 1.0 copy-start.8
where the time goes:
time: 143 us; the launch traced here: 142 us
  Pallas kernels  46.1 us (32%)
  starting transfers between devices  44.4 us (31%)
  waiting for transfers between devices  42.2 us (30%)
  local copies, waits for them, and re-layouts  6.85 us (5%)
    pallas_call x3, Pallas kernels, attend(): pl.pallas_call(functools.partial(attend_kernel, slots, tiles), in_specs=[...  23.3 us
    ppermute x10, waiting for transfers between devices, swap(): return lax.ppermute(x, 'tm', [(i, i ^ d) for i in range(shards)])  19.7 us
    all_to_all x2, starting transfers between devices, on_device(): lax.all_to_all(sent[s].reshape(shards, 2 * piece, 2 * HDIM), 'tm', 0, 0)  14.1 us
    ppermute x10, starting transfers between devices, swap(): return lax.ppermute(x, 'tm', [(i, i ^ d) for i in range(shards)])  11.5 us
    ppermute x7, waiting for transfers between devices, swap_clip(): return lax.ppermute(x, 'clip', [(i, i ^ d) for i in range(clips)])  10.5 us
    ppermute x2, waiting for transfers between devices, down(): return lax.ppermute(x, 'tm', [(i + 2, i) for i in range(shards - 2)])  10.5 us
    ppermute x2, starting transfers between devices, up(): return lax.ppermute(x, 'tm', [(i, i + 2) for i in range(shards - 2)])  9.99 us
    pallas_call x2, Pallas kernels, put_in_order(): pl.pallas_call(order_kernel, grid=(2,), in_specs=[pl.BlockSpec((1, 1, row...  7.88 us
  transfers between devices with their start and end apart: 24, of which 15 were waited for; matrix products, arithmetic and copies ran while one was open for 1% of the time, Pallas kernels for 28%

commit v1 on v0

--- a/solution.py
+++ b/solution.py
@@ -184,6 +184,24 @@
     )(place, mine, peer, after)
 
 
+def tails_kernel(left_ref, right_ref, after_ref, out_ref):
+    n = out_ref.shape[0] // 2
+    out_ref[:n] = left_ref[left_ref.shape[0] - n :]
+    out_ref[n:] = right_ref[right_ref.shape[0] - n :]
+
+
+def tails(left, right, count, after):
+    vm = pl.BlockSpec(memory_space=pltpu.VMEM)
+    return pl.pallas_call(
+        tails_kernel,
+        in_specs=[vm, vm, pl.BlockSpec(memory_space=pl.ANY)],
+        out_specs=vm,
+        out_shape=jax.ShapeDtypeStruct((2 * count, left.shape[1]), BF),
+        compiler_params=params(),
+        cost_estimate=cost(0, 8 * count * left.shape[1]),
+    )(left, right, after)
+
+
 def split3(x):
     a = x.astype(BF).astype(F32)
     b = (x - a).astype(BF).astype(F32)
@@ -191,7 +209,7 @@
     return [a, b, c]
 
 
-def attend_kernel(slots, tiles, lohi_ref, qga_ref, qgb_ref, *refs):
+def attend_kernel(slots, tiles, by_exchange, place_ref, lohi_ref, qga_ref, qgb_ref, *refs):
     outa_ref, outb_ref = refs[-2 * tiles - 2 : -2 * tiles]
     s_refs, d_refs = refs[-2 * tiles : -tiles], refs[-tiles:]
     rows = outa_ref.shape[1]
@@ -202,8 +220,19 @@
     rhs_lane = lax.broadcasted_iota(jnp.int32, (TILE, 2 * HDIM), 1)
     row_id = lax.broadcasted_iota(jnp.int32, (STATS, TILE), 0)
     z8 = jnp.zeros((8, TILE), F32)
-    for (i, slot), (u, q_ref, o_ref) in itertools.product(
-        enumerate(slots), ((0, qga_ref, outa_ref), (1, qgb_ref, outb_ref))
+    odd = place_ref[2] % 2 == 1
+
+    def stores(place, out):
+        def first():
+            outa_ref[place] = out
+
+        def second():
+            outb_ref[place] = out
+
+        return first, second
+
+    for (i, slot), (u, q_ref) in itertools.product(
+        enumerate(slots), ((0, qga_ref), (1, qgb_ref))
     ):
         kv_ref, kvt_ref = refs[2 * i : 2 * i + 2]
         own = slice(slot * 2 * HDIM, (slot + 1) * 2 * HDIM)
@@ -313,39 +342,46 @@
                 for i, piece in enumerate(split3(tops[k]) + split3(l) + split3(delta)):
                     stats = jnp.where(row_id == i, piece, stats)
                 out = jnp.concatenate([acc[:, :TILE], acc[:HDIM, TILE:], stats], axis=0)
-                o_ref[out_rows, pl.ds(held[k][4], TILE)] = out.astype(o_ref.dtype)
+                place = (out_rows, pl.ds(held[k][4], TILE))
+                out = out.astype(outa_ref.dtype)
+                if by_exchange:
+                    jax.lax.cond(odd == (u == 0), *stores(place, out))
+                else:
+                    (outa_ref, outb_ref)[u][place] = out
             return carry
 
         lax.fori_loop(0, rows // (TILE * tiles), group, 0)
 
 
-def attend(slots, tiles, rows, lohi, qga, qgb, kvs, out_dtype, *after):
+def attend(place, slots, tiles, rows, lohi, qga, qgb, kvs, by_exchange, *after):
     keys = kvs[0].shape[0]
     n = len(slots)
     vm = pl.BlockSpec(memory_space=pltpu.VMEM)
     return pl.pallas_call(
-        functools.partial(attend_kernel, slots, tiles),
-        in_specs=[pl.BlockSpec(memory_space=pltpu.SMEM)]
+        functools.partial(attend_kernel, slots, tiles, by_exchange),
+        in_specs=[pl.BlockSpec(memory_space=pltpu.SMEM)] * 2
         + [vm] * (2 + 2 * n)
         + [pl.BlockSpec(memory_space=pl.ANY)] * len(after),
         out_specs=[vm] * 2,
-        out_shape=[jax.ShapeDtypeStruct((n * OUT, rows), out_dtype)] * 2,
+        out_shape=[jax.ShapeDtypeStruct((n * OUT, rows), BF)] * 2,
         scratch_shapes=[pltpu.VMEM((keys, TILE), F32)] * (2 * tiles),
         compiler_params=params(),
         cost_estimate=cost(
             n * rows * keys * 1024, n * (4 * keys * 128 + 16 * rows * 256), n * rows * keys
         ),
-    )(lohi, qga, qgb, *kvs, *after)
+    )(place, lohi, qga, qgb, *kvs, *after)
 
 
 def combine_kernel(groups, slots, place_ref, cot_ref, pcot_ref, *refs):
     parts, refs = refs[: 2 * slots + 2], refs[2 * slots + 2 :]
     oqa_ref, oqb_ref, shares, buf = refs[0], refs[1], refs[2:-1], refs[-1]
     scale = 1.0 / math.sqrt(HDIM)
+    odd = place_ref[2] % 2 == 1
     for u, oq_ref in enumerate((oqa_ref, oqb_ref)):
         for s in range(slots):
-            own = parts[2 * s + u][...]
-            rem = parts[2 * slots + u][s * OUT : (s + 1) * OUT].astype(F32)
+            own = parts[2 * s + u][...].astype(F32)
+            rem = [r[s * OUT : (s + 1) * OUT] for r in parts[2 * slots :]]
+            rem = jnp.where(odd == (u == 0), *rem).astype(F32)
 
             def stat(x, i):
                 r = 3 * HDIM + 3 * i
@@ -572,7 +608,7 @@
     origin = z * 2 * blocks
 
     def limits(first_rows, *firsts):
-        bands = [x[rows : rows + 2, :blocks] for x in first_rows]
+        bands = [x[:2, :blocks] for x in first_rows]
         bands = jnp.concatenate(bands, axis=1).astype(F32).astype(jnp.int32)
         frame = [origin + f + jnp.arange(blocks, dtype=jnp.int32) for f in firsts]
         frame = jnp.concatenate(frame)
@@ -580,7 +616,7 @@
         hi = jnp.minimum(frame + bands[1], shards * blocks - 1) - origin
         return jnp.stack([lo, hi])
 
-    own_limits = limits((qga, qgb), 0, blocks)
+    own_limits = limits((qga[rows:], qgb[rows:]), 0, blocks)
 
     def columns_for(d):
         c = (clip ^ d) * feats
@@ -598,18 +634,21 @@
         )
         kvs += put_in_order(arrived, index, teacher_rows, *parts[-2:])
         if s == slots - 1:
+            count = band.shape[0]
+            ends = tails(qg_left, qg_right, count, kvs[-1])
+            halo_limits = limits((ends[:count], ends[count:]), -blocks, 2 * blocks)
             far = attend(
-                range(slots), 2, rows, halo_limits, qg_left, qg_right, kvs, BF
+                place, range(slots), 2, rows, halo_limits, qg_left, qg_right, kvs, True
             )
-            parts += attend([s], 4, rows, own_limits, qga, qgb, kvs[-2:], F32, *far)
-        else:
-            parts += attend([s], 4, rows, own_limits, qga, qgb, kvs[-2:], F32)
+        own = place, [s], 4, rows, own_limits, qga, qgb, kvs[-2:], False
+        parts += attend(*own, *(far if s == slots - 1 else ()))
         if s == 0:
             edge_a, edge_b = edges(place, qg_mine, qg_peer, parts[0])
             qg_left, qg_right = up(edge_b), down(edge_a)
-            halo_limits = limits((qg_left, qg_right), -blocks, 2 * blocks)
             cot = whole_cotangent(place, here, there, parts[0])
-    parts += [up(far[1]), down(far[0])]
+    parts += [swap(far[0], 2)]
+    links = [(i, i + 2) for i in range(shards - 2) if i // 2 % 2]
+    parts += [lax.ppermute(far[1], "tm", links + [(j, i) for i, j in links])]
     oqa, oqb, *got = combine(place, cot, swap(cot, 1), parts, groups, slots)
     mine, give, xmine, xgive = turn(place, oqa, oqb)
     total = got[0].astype(F32)

time: 143 us -> 141 us (0.986); the launches traced: 142 us -> 143 us
  waiting for transfers between devices: 42.2 us -> 28.3 us
  Pallas kernels: 46.1 us -> 54.3 us
  starting transfers between devices: 44.4 us -> 49.7 us
    pallas_call x3 -> x4, Pallas kernels: 23.3 us -> 34.5 us  [the longest x3 33.5 us: attend(): pl.pallas_call(functools.partial(attend_kernel, slots, tiles, by_exchange...]
    ppermute x2 -> x1, waiting for transfers between devices: 10.5 us -> 0.45 us  [down(): return lax.ppermute(x, 'tm', [(i + 2, i) for i in range(shards - 2)])]
    ppermute x10 -> x11, starting transfers between devices: 11.5 us -> 20.9 us  [swap(): return lax.ppermute(x, 'tm', [(i, i ^ d) for i in range(shards)])]
    ppermute x2 -> x1, starting transfers between devices: 9.99 us -> 6.25 us  [up(): return lax.ppermute(x, 'tm', [(i, i + 2) for i in range(shards - 2)])]
    ppermute x7, waiting for transfers between devices: 10.5 us -> 8.05 us  [swap_clip(): return lax.ppermute(x, 'clip', [(i, i ^ d) for i in range(clips)])]
    unnamed x46 -> x50, local copies, waits for them, and re-layouts: 6.1 us -> 8.07 us
    ppermute x10 -> x11, waiting for transfers between devices: 19.7 us -> 19.8 us  [swap(): return lax.ppermute(x, 'tm', [(i, i ^ d) for i in range(shards)])]
  transfers between devices with their start and end apart: 24 -> 24, of which waited for: 15 -> 8; matrix products, arithmetic and copies ran while one was open for 1% -> 1% of each run, Pallas kernels for 28% -> 34%
where the time goes in v1:
time: 141 us; the launch traced here: 143 us
  Pallas kernels  54.3 us (39%)
  starting transfers between devices  49.7 us (35%)
  waiting for transfers between devices  28.3 us (20%)
  local copies, waits for them, and re-layouts  8.15 us (6%)
    pallas_call x3, Pallas kernels, attend(): pl.pallas_call(functools.partial(attend_kernel, slots, tiles, by_exchange...  33.5 us
    ppermute x11, starting transfers between devices, swap(): return lax.ppermute(x, 'tm', [(i, i ^ d) for i in range(shards)])  20.9 us
    ppermute x11, waiting for transfers between devices, swap(): return lax.ppermute(x, 'tm', [(i, i ^ d) for i in range(shards)])  19.8 us
    all_to_all x2, starting transfers between devices, on_device(): lax.all_to_all(sent[s].reshape(shards, 2 * piece, 2 * HDIM), 'tm', 0, 0)  13.8 us
    unnamed x50, local copies, waits for them, and re-layouts  8.07 us
    ppermute x7, waiting for transfers between devices, swap_clip(): return lax.ppermute(x, 'clip', [(i, i ^ d) for i in range(clips)])  8.05 us
    pallas_call x2, Pallas kernels, put_in_order(): pl.pallas_call(order_kernel, grid=(2,), in_specs=[pl.BlockSpec((1, 1, row...  7.8 us
    ppermute x1, starting transfers between devices, up(): return lax.ppermute(x, 'tm', [(i, i + 2) for i in range(shards - 2)])  6.25 us
  transfers between devices with their start and end apart: 24, of which 8 were waited for; matrix products, arithmetic and copies ran while one was open for 1% of the time, Pallas kernels for 34%

profile of v1, /device:TPU:0, one launch (start us, length us, event | category | flops | bytes accessed | tf_op | source)
XLA Modules:
  0.0 142.9 jit_solution(5136181589832995637)
XLA Ops:
  0.6 1.2 copy-done
  1.9 1.2 copy-done.2
  3.1 1.8 %shard_map.104 = bf16[4,2,512,128]{3,2,1,0:T(8,128)(2,1)} custom-call(bf16[2048,256]{1,0:T(8,128)(2,1)S(1)} %copy-done, bf16[2048,256]{1,0:T(8,128)(2,1)S(1)} %copy-done.2), custom_call_target="tpu_custom_call" | custom-call | bytes 3145728 | tf_op jit(solution)/shard_map/pallas_call | solution.py:48
  4.9 7.4 %all-to-all-start = ((bf16[8,512,128]{2,1,0:T(8,128)(2,1)}), bf16[8,512,128]{2,1,0:T(8,128)(2,1)}, u32[]{:S(2)}, u32[]{:S(2)}) async-start(bf16[8,512,128]{2,1,0:T(8,128)(2,1)} %bitcast.8), calls=%async_computation | async-start | bytes 2097152 | tf_op jit(solution)/shard_map/all_to_all | solution.py:632
  12.3 1.6 %collective-permute-start = (bf16[512,256]{1,0:T(8,128)(2,1)S(1)}, bf16[512,256]{1,0:T(8,128)(2,1)S(1)}, u32[]{:S(2)}, u32[]{:S(2)}) collective-permute-start(bf16[512,256]{1,0:T(8,128)(2,1)S(1)} %copy-done.22), channel_id=1, source_target_pairs={{0,2},{1,3},{2,0},{3,1},{4,6},{5,7},{6,4},{7,5},{8,10},{9,11},{10,... | collective-permute-start | bytes 786440 | tf_op jit(solution)/shard_map/ppermute | solution.py:580
  13.9 6.3 %collective-permute-done = bf16[512,256]{1,0:T(8,128)(2,1)S(1)} collective-permute-done((bf16[512,256]{1,0:T(8,128)(2,1)S(1)}, bf16[512,256]{1,0:T(8,128)(2,1)S(1)}, u32[]{:S(2)}, u32[]{:S(2)}) %collective-permute-start) | collective-permute-done | bytes 262176 | tf_op jit(solution)/shard_map/ppermute | solution.py:580
  20.4 1.8 %collective-permute-done.1.there_ref = bf16[2,512,256]{2,1,0:T(8,128)(2,1)S(1)} collective-permute-done((bf16[2,512,256]{2,1,0:T(8,128)(2,1)S(1)}, bf16[2,512,256]{2,1,0:T(8,128)(2,1)S(1)}, u32[]{:S(2)}, u32[]{:S(2)}) %collective-permute-start.1) | collective-permute-done | bytes 524320 | tf_op jit(solution)/shard_map/ppermute | solution.py:580
  22.2 1.0 copy-done.5
  23.3 0.9 copy-done.14
  24.2 1.1 shard_map.103
  25.3 0.7 copy-done.7
  26.0 1.7 %collective-permute-start.2 = (bf16[528,256]{1,0:T(8,128)(2,1)S(1)}, bf16[528,256]{1,0:T(8,128)(2,1)S(1)}, u32[]{:S(2)}, u32[]{:S(2)}) collective-permute-start(bf16[528,256]{1,0:T(8,128)(2,1)S(1)} %get-tuple-element.30), channel_id=1, source_target_pairs={{0,4},{4,0},{8,12},{12,8},{16,20},{20,16},{24,28},{28,24},{1,5},{5... | collective-permute-start | bytes 811016 | tf_op jit(solution)/shard_map/ppermute | solution.py:577
  27.7 8.9 %collective-permute-done.2.refs_0_.peer_ref = bf16[528,256]{1,0:T(8,128)(2,1)S(1)} collective-permute-done((bf16[528,256]{1,0:T(8,128)(2,1)S(1)}, bf16[528,256]{1,0:T(8,128)(2,1)S(1)}, u32[]{:S(2)}, u32[]{:S(2)}) %collective-permute-start.2) | collective-permute-done | bytes 270368 | tf_op jit(solution)/shard_map/ppermute | solution.py:577
  37.2 1.0 copy-done.4
  38.2 6.4 %all-to-all-start.1 = ((bf16[8,512,128]{2,1,0:T(8,128)(2,1)}), bf16[8,512,128]{2,1,0:T(8,128)(2,1)}, u32[]{:S(2)}, u32[]{:S(2)}) async-start(bf16[8,512,128]{2,1,0:T(8,128)(2,1)} %bitcast.14), calls=%async_computation.1 | async-start | bytes 2097152 | tf_op jit(solution)/shard_map/all_to_all | solution.py:632
  44.6 0.7 fusion.2
  45.6 3.9 %shard_map.105 = (bf16[4096,128]{1,0:T(8,128)(2,1)S(1)}, bf16[128,4096]{1,0:T(8,128)(2,1)S(1)}) custom-call(s32[2,1,2048]{2,1,0:T(1,128)S(1)} %bitcast.15, bf16[8,512,128]{2,1,0:T(8,128)(2,1)} %all-to-all-done.arr_ref), custom_call_target="tpu_custom_call" | custom-call | flops 2147483648 | bytes 3145728 | tf_op jit(solution)/shard_map/pallas_call | solution.py:78
  49.5 12.6 %shard_map.106 = (bf16[208,512]{1,0:T(8,128)(2,1)S(1)}, bf16[208,512]{1,0:T(8,128)(2,1)S(1)}) custom-call(s32[3]{0:T(128)S(1)} %pad_add_fusion.2.place_ref, s32[2,32]{1,0:T(2,128)S(1)} %pad_add_fusion.lohi_ref, bf16[528,256]{1,0:T(8,128)(2,1)S(1)} %get-tuple-element.55.qga_ref, bf16[528,256]{1,0:T(8,128)(2,1)S(1)} %get-tuple-element.56.qgb_ref, ...), custom_call_target="tpu_custom_call" | custom-call | flops 2147483648 | bytes 4194304 | tf_op jit(solution)/shard_map/pallas_call | solution.py:360
  62.1 1.4 shard_map.110
  63.6 6.2 %collective-permute-start.4 = (bf16[528,256]{1,0:T(8,128)(2,1)}, bf16[528,256]{1,0:T(8,128)(2,1)}, u32[]{:S(2)}, u32[]{:S(2)}) collective-permute-start(bf16[528,256]{1,0:T(8,128)(2,1)} %get-tuple-element.37), channel_id=1, source_target_pairs={{0,8},{4,12},{8,16},{12,20},{16,24},{20,28},{1,9},{5,13},{9,17},{1... | collective-permute-start | bytes 811016 | tf_op jit(solution)/shard_map/ppermute | solution.py:587
  69.8 1.5 %collective-permute-start.5 = (bf16[528,256]{1,0:T(8,128)(2,1)}, bf16[528,256]{1,0:T(8,128)(2,1)}, u32[]{:S(2)}, u32[]{:S(2)}) collective-permute-start(bf16[528,256]{1,0:T(8,128)(2,1)} %get-tuple-element.38), channel_id=1, source_target_pairs={{8,0},{12,4},{16,8},{20,12},{24,16},{28,20},{9,1},{13,5},{17,9},{2... | collective-permute-start | bytes 811016 | tf_op jit(solution)/shard_map/ppermute | solution.py:590
  71.3 0.7 shard_map.107.cot_ref
  72.0 1.5 %collective-permute-start.3 = (bf16[512,1024]{1,0:T(8,128)(2,1)S(1)}, bf16[512,1024]{1,0:T(8,128)(2,1)S(1)}, u32[]{:S(2)}, u32[]{:S(2)}) collective-permute-start(bf16[512,1024]{1,0:T(8,128)(2,1)S(1)} %shard_map.107.cot_ref), channel_id=1, source_target_pairs={{0,4},{4,0},{8,12},{12,8},{16,20},{20,16},{24,28},{28,24},{1,5},{5... | collective-permute-start | bytes 3145736 | tf_op jit(solution)/shard_map/ppermute | solution.py:577
  73.5 0.9 copy-done.16
  74.4 3.9 %shard_map.109 = (bf16[4096,128]{1,0:T(8,128)(2,1)S(1)}, bf16[128,4096]{1,0:T(8,128)(2,1)S(1)}) custom-call(s32[2,1,2048]{2,1,0:T(1,128)S(1)} %bitcast.16, bf16[8,512,128]{2,1,0:T(8,128)(2,1)} %all-to-all-done.1.arr_ref, bf16[208,512]{1,0:T(8,128)(2,1)S(1)} %get-tuple-element.33.after_ref.refs_0_, bf16[208,512]{1,0:T(8,128)(2,1)S(1)} %copy-done.16), custom_call_target="tpu_custom_call" | custom-call | flops 2147483648 | bytes 3145728 | tf_op jit(solution)/shard_map/pallas_call | solution.py:78
  78.9 1.0 shard_map.111
  80.1 8.2 %shard_map.112 = (bf16[416,512]{1,0:T(8,128)(2,1)S(1)}, bf16[416,512]{1,0:T(8,128)(2,1)S(1)}) custom-call(s32[3]{0:T(128)S(1)} %pad_add_fusion.2.place_ref, s32[2,32]{1,0:T(2,128)S(1)} %pad_add_fusion.1.lohi_ref, bf16[528,256]{1,0:T(8,128)(2,1)} %collective-permute-done.4.left_ref.qga_ref, bf16[528,256]{1,0:T(8,128)(2,1)} %collective-permute-done.5.right_ref.qgb_ref, ...), custom_call_target="tpu_custom_call" | custom-call | flops 4294967296 | bytes 8388608 | tf_op jit(solution)/shard_map/pallas_call | solution.py:360
  88.3 2.4 %collective-permute-start.6 = (bf16[416,512]{1,0:T(8,128)(2,1)S(1)}, bf16[416,512]{1,0:T(8,128)(2,1)S(1)}, u32[]{:S(2)}, u32[]{:S(2)}) collective-permute-start(bf16[416,512]{1,0:T(8,128)(2,1)S(1)} %get-tuple-element.39.refs_2_), channel_id=1, source_target_pairs={{0,8},{4,12},{8,0},{12,4},{16,24},{20,28},{24,16},{28,20},{1,9},{5... | collective-permute-start | bytes 1277960 | tf_op jit(solution)/shard_map/ppermute | solution.py:577
  90.7 0.8 collective-permute-start.7
  91.5 12.7 %shard_map.113 = (bf16[208,512]{1,0:T(8,128)(2,1)S(1)}, bf16[208,512]{1,0:T(8,128)(2,1)S(1)}) custom-call(s32[3]{0:T(128)S(1)} %pad_add_fusion.2.place_ref, s32[2,32]{1,0:T(2,128)S(1)} %pad_add_fusion.lohi_ref, bf16[528,256]{1,0:T(8,128)(2,1)S(1)} %copy-done.11, bf16[528,256]{1,0:T(8,128)(2,1)S(1)} %copy-done.13, ...), custom_call_target="tpu_custom_call" | custom-call | flops 2147483648 | bytes 4194304 | tf_op jit(solution)/shard_map/pallas_call | solution.py:360
  104.3 1.5 %shard_map.114 = (bf16[256,512]{1,0:T(8,128)(2,1)S(1)}, bf16[256,512]{1,0:T(8,128)(2,1)S(1)}, bf16[128,256]{1,0:T(8,128)(2,1)S(1)}, bf16[128,256]{1,0:T(8,128)(2...) custom-call(s32[3]{0:T(128)S(1)} %pad_add_fusion.2.place_ref, ...), custom_call_target="tpu_custom_call" | custom-call | flops 268435456 | bytes 8388608 | tf_op jit(solution)/shard_map/pallas_call | solution.py:427
  105.8 0.7 shard_map.115
  107.2 2.4 %collective-permute-start.10 = (bf16[512,128]{1,0:T(8,128)(2,1)S(1)}, bf16[512,128]{1,0:T(8,128)(2,1)S(1)}, u32[]{:S(2)}, u32[]{:S(2)}) collective-permute-start(bf16[512,128]{1,0:T(8,128)(2,1)S(1)} %get-tuple-element.48), channel_id=1, source_target_pairs={{0,6},{1,7},{2,4},{3,5},{4,2},{5,3},{6,0},{7,1},{8,14},{9,15},{10,... | collective-permute-start | bytes 393224 | tf_op jit(solution)/shard_map/ppermute | solution.py:584
  110.1 6.5 %collective-permute-start.15 = (bf16[128,256]{1,0:T(8,128)(2,1)S(1)}, bf16[128,256]{1,0:T(8,128)(2,1)S(1)}, u32[]{:S(2)}, u32[]{:S(2)}) collective-permute-start(bf16[128,256]{1,0:T(8,128)(2,1)S(1)} %get-tuple-element.52), channel_id=1, source_target_pairs={{0,8},{4,12},{8,0},{12,4},{16,24},{20,28},{24,16},{28,20},{1,9},{5... | collective-permute-start | bytes 196616 | tf_op jit(solution)/shard_map/ppermute | solution.py:577
  116.6 2.4 %collective-permute-start.17 = (bf16[128,256]{1,0:T(8,128)(2,1)S(1)}, bf16[128,256]{1,0:T(8,128)(2,1)S(1)}, u32[]{:S(2)}, u32[]{:S(2)}) collective-permute-start(bf16[128,256]{1,0:T(8,128)(2,1)S(1)} %get-tuple-element.54), channel_id=1, source_target_pairs={{0,24},{4,28},{8,16},{12,20},{16,8},{20,12},{24,0},{28,4},{1,25},{... | collective-permute-start | bytes 196616 | tf_op jit(solution)/shard_map/ppermute | solution.py:577
  119.0 1.3 shard_map.116
  120.3 1.6 %collective-permute-done.16 = bf16[128,256]{1,0:T(8,128)(2,1)S(1)} collective-permute-done((bf16[128,256]{1,0:T(8,128)(2,1)S(1)}, bf16[128,256]{1,0:T(8,128)(2,1)S(1)}, u32[]{:S(2)}, u32[]{:S(2)}) %collective-permute-start.16) | collective-permute-done | bytes 65568 | tf_op jit(solution)/shard_map/ppermute | solution.py:577
  121.9 0.8 collective-permute-done.17
  122.7 0.7 collective-permute-start.18
  123.5 1.6 %collective-permute-start.13 = (bf16[256,256]{1,0:T(8,128)(2,1)S(1)}, bf16[256,256]{1,0:T(8,128)(2,1)S(1)}, u32[]{:S(2)}, u32[]{:S(2)}) collective-permute-start(bf16[256,256]{1,0:T(8,128)(2,1)S(1)} %get-tuple-element.60), channel_id=1, source_target_pairs={{0,2},{1,3},{2,0},{3,1},{4,6},{5,7},{6,4},{7,5},{8,10},{9,11},{10,... | collective-permute-start | bytes 393224 | tf_op jit(solution)/shard_map/ppermute | solution.py:580
  125.4 1.7 %collective-permute-done.18 = bf16[128,256]{1,0:T(8,128)(2,1)S(1)} collective-permute-done((bf16[128,256]{1,0:T(8,128)(2,1)S(1)}, bf16[128,256]{1,0:T(8,128)(2,1)S(1)}, u32[]{:S(2)}, u32[]{:S(2)}) %collective-permute-start.18) | collective-permute-done | bytes 65568 | tf_op jit(solution)/shard_map/ppermute | solution.py:577
  127.0 1.3 collective-permute-start.19
  128.4 1.8 %collective-permute-start.20 = (bf16[2,128,256]{2,1,0:T(8,128)(2,1)S(1)}, bf16[2,128,256]{2,1,0:T(8,128)(2,1)S(1)}, u32[]{:S(2)}, u32[]{:S(2)}) collective-permute-start(bf16[2,128,256]{2,1,0:T(8,128)(2,1)S(1)} %pad_maximum_fusion.1.refs_0_), channel_id=1, source_target_pairs={{0,16},{4,20},{8,24},{12,28},{16,0},{20,4},{24,8},{28,12},{1,17},{... | collective-permute-start | bytes 393224 | tf_op jit(solution)/shard_map/ppermute | solution.py:577
  130.1 2.1 %collective-permute-start.21 = (bf16[2,128,256]{2,1,0:T(8,128)(2,1)S(1)}, bf16[2,128,256]{2,1,0:T(8,128)(2,1)S(1)}, u32[]{:S(2)}, u32[]{:S(2)}) collective-permute-start(bf16[2,128,256]{2,1,0:T(8,128)(2,1)S(1)} %pad_maximum_fusion.1.refs_0_), channel_id=1, source_target_pairs={{0,24},{4,28},{8,16},{12,20},{16,8},{20,12},{24,0},{28,4},{1,25},{... | collective-permute-start | bytes 393224 | tf_op jit(solution)/shard_map/ppermute | solution.py:577
  132.3 1.2 shard_map.117.refs_4_
  133.5 6.8 %collective-permute-done.20.refs_2_ = bf16[2,128,256]{2,1,0:T(8,128)(2,1)S(1)} collective-permute-done((bf16[2,128,256]{2,1,0:T(8,128)(2,1)S(1)}, bf16[2,128,256]{2,1,0:T(8,128)(2,1)S(1)}, u32[]{:S(2)}, u32[]{:S(2)}) %collective-permute-start.20) | collective-permute-done | bytes 131104 | tf_op jit(solution)/shard_map/ppermute | solution.py:577
  140.3 0.9 copy-done.9
  141.3 1.6 %shard_map.118 = f32[256,1024]{1,0:T(8,128)} custom-call(s32[3]{0:T(128)S(1)} %pad_add_fusion.2.place_ref, bf16[2,128,256]{2,1,0:T(8,128)(2,1)S(1)} %pad_maximum_fusion.1.refs_0_, bf16[2,128,256]{2,1,0:T(8,128)(2,1)S(1)} %collective-permute-done.19.refs_1_, bf16[2,128,256]{2,1,0:T(8,128)(2,1)S(1)} %collective-permute-done.20.refs_2_, ...), custom_call_target="tpu_custom_call" | custom-call | bytes 1572864 | tf_op jit(solution)/shard_map/pallas_call | solution.py:539
  (86 shorter events, 3.5 us)
Async XLA Ops:
  0.6 1.2 copy-start
  1.9 1.2 copy-start.2
  4.9 7.4 %copy-start.22 = (bf16[512,256]{1,0:T(8,128)(2,1)S(1)}, bf16[512,256]{1,0:T(8,128)(2,1)}, u32[]{:S(2)}) copy-start(bf16[512,256]{1,0:T(8,128)(2,1)} %param.15) | copy-start | bytes 786436
  4.9 15.5 %copy-start.23 = (s32[16]{0:T(128)S(1)}, s32[16]{0:T(128)}, u32[]{:S(2)}) copy-start(s32[16]{0:T(128)} %param.13) | copy-start | bytes 196
  4.9 15.5 %copy-start.24 = (s32[16]{0:T(128)S(1)}, s32[16]{0:T(128)}, u32[]{:S(2)}) copy-start(s32[16]{0:T(128)} %param.12) | copy-start | bytes 196
  4.9 33.3 %all-to-all-start = ((bf16[8,512,128]{2,1,0:T(8,128)(2,1)}), bf16[8,512,128]{2,1,0:T(8,128)(2,1)}, u32[]{:S(2)}, u32[]{:S(2)}) async-start(bf16[8,512,128]{2,1,0:T(8,128)(2,1)} %bitcast.8), calls=%async_computation | async-start | bytes 2097152 | tf_op jit(solution)/shard_map/all_to_all | solution.py:632
  12.3 7.8 %collective-permute-start = (bf16[512,256]{1,0:T(8,128)(2,1)S(1)}, bf16[512,256]{1,0:T(8,128)(2,1)S(1)}, u32[]{:S(2)}, u32[]{:S(2)}) collective-permute-start(bf16[512,256]{1,0:T(8,128)(2,1)S(1)} %copy-done.22), channel_id=1, source_target_pairs={{0,2},{1,3},{2,0},{3,1},{4,6},{5,7},{6,4},{7,5},{8,10},{9,11},{10,... | collective-permute-start | bytes 786440 | tf_op jit(solution)/shard_map/ppermute | solution.py:580
  20.2 16.4 %copy-start.3 = (bf16[2048,256]{1,0:T(8,128)(2,1)S(1)}, bf16[2048,256]{1,0:T(8,128)(2,1)}, u32[]{:S(2)}) copy-start(bf16[2048,256]{1,0:T(8,128)(2,1)} %v_ref.3) | copy-start | bytes 3145732
  20.2 16.4 %copy-start.1 = (bf16[2048,256]{1,0:T(8,128)(2,1)S(1)}, bf16[2048,256]{1,0:T(8,128)(2,1)}, u32[]{:S(2)}) copy-start(bf16[2048,256]{1,0:T(8,128)(2,1)} %k_ref.3) | copy-start | bytes 3145732
  20.2 2.0 %collective-permute-start.1 = (bf16[2,512,256]{2,1,0:T(8,128)(2,1)S(1)}, bf16[2,512,256]{2,1,0:T(8,128)(2,1)S(1)}, u32[]{:S(2)}, u32[]{:S(2)}) collective-permute-start(bf16[2,512,256]{2,1,0:T(8,128)(2,1)S(1)} %pad_maximum_fusion.here_ref), channel_id=1, source_target_pairs={{0,1},{1,0},{2,3},{3,2},{4,5},{5,4},{6,7},{7,6},{8,9},{9,8},{10,11... | collective-permute-start | bytes 1572872 | tf_op jit(solution)/shard_map/ppermute | solution.py:580
  22.2 1.0 copy-start.5
  23.3 0.9 copy-start.14
  26.0 10.6 %collective-permute-start.2 = (bf16[528,256]{1,0:T(8,128)(2,1)S(1)}, bf16[528,256]{1,0:T(8,128)(2,1)S(1)}, u32[]{:S(2)}, u32[]{:S(2)}) collective-permute-start(bf16[528,256]{1,0:T(8,128)(2,1)S(1)} %get-tuple-element.30), channel_id=1, source_target_pairs={{0,4},{4,0},{8,12},{12,8},{16,20},{20,16},{24,28},{28,24},{1,5},{5... | collective-permute-start | bytes 811016 | tf_op jit(solution)/shard_map/ppermute | solution.py:577
  37.2 1.0 copy-start.4
  38.2 7.1 %copy-start.8 = (bf16[528,256]{1,0:T(8,128)(2,1)S(1)}, bf16[528,256]{1,0:T(8,128)(2,1)}, u32[]{:S(2)}) copy-start(bf16[528,256]{1,0:T(8,128)(2,1)} %copy-done.7) | copy-start | bytes 811012
  38.2 35.3 %all-to-all-start.1 = ((bf16[8,512,128]{2,1,0:T(8,128)(2,1)}), bf16[8,512,128]{2,1,0:T(8,128)(2,1)}, u32[]{:S(2)}, u32[]{:S(2)}) async-start(bf16[8,512,128]{2,1,0:T(8,128)(2,1)} %bitcast.14), calls=%async_computation.1 | async-start | bytes 2097152 | tf_op jit(solution)/shard_map/all_to_all | solution.py:632
  45.4 4.1 %copy-start.10 = (bf16[528,256]{1,0:T(8,128)(2,1)}, bf16[528,256]{1,0:T(8,128)(2,1)S(1)}, u32[]{:S(2)}) copy-start(bf16[528,256]{1,0:T(8,128)(2,1)S(1)} %get-tuple-element.55.qga_ref) | copy-start | bytes 811012
  45.4 4.1 %copy-start.12 = (bf16[528,256]{1,0:T(8,128)(2,1)}, bf16[528,256]{1,0:T(8,128)(2,1)S(1)}, u32[]{:S(2)}) copy-start(bf16[528,256]{1,0:T(8,128)(2,1)S(1)} %get-tuple-element.56.qgb_ref) | copy-start | bytes 811012
  49.5 12.6 %copy-start.18 = (bf16[4096,128]{1,0:T(8,128)(2,1)}, bf16[4096,128]{1,0:T(8,128)(2,1)S(1)}, u32[]{:S(2)}) copy-start(bf16[4096,128]{1,0:T(8,128)(2,1)S(1)} %get-tuple-element.31.refs_0_) | copy-start | bytes 3145732
  49.5 12.6 %copy-start.20 = (bf16[128,4096]{1,0:T(8,128)(2,1)}, bf16[128,4096]{1,0:T(8,128)(2,1)S(1)}, u32[]{:S(2)}) copy-start(bf16[128,4096]{1,0:T(8,128)(2,1)S(1)} %get-tuple-element.32.refs_1_) | copy-start | bytes 3145732
  62.1 1.4 %copy-start.15 = (bf16[208,512]{1,0:T(8,128)(2,1)}, bf16[208,512]{1,0:T(8,128)(2,1)S(1)}, u32[]{:S(2)}) copy-start(bf16[208,512]{1,0:T(8,128)(2,1)S(1)} %get-tuple-element.34.refs_1_) | copy-start | bytes 638980
  63.6 14.8 %collective-permute-start.4 = (bf16[528,256]{1,0:T(8,128)(2,1)}, bf16[528,256]{1,0:T(8,128)(2,1)}, u32[]{:S(2)}, u32[]{:S(2)}) collective-permute-start(bf16[528,256]{1,0:T(8,128)(2,1)} %get-tuple-element.37), channel_id=1, source_target_pairs={{0,8},{4,12},{8,16},{12,20},{16,24},{20,28},{1,9},{5,13},{9,17},{1... | collective-permute-start | bytes 811016 | tf_op jit(solution)/shard_map/ppermute | solution.py:587
  69.8 9.1 %collective-permute-start.5 = (bf16[528,256]{1,0:T(8,128)(2,1)}, bf16[528,256]{1,0:T(8,128)(2,1)}, u32[]{:S(2)}, u32[]{:S(2)}) collective-permute-start(bf16[528,256]{1,0:T(8,128)(2,1)} %get-tuple-element.38), channel_id=1, source_target_pairs={{8,0},{12,4},{16,8},{20,12},{24,16},{28,20},{9,1},{13,5},{17,9},{2... | collective-permute-start | bytes 811016 | tf_op jit(solution)/shard_map/ppermute | solution.py:590
  72.0 32.3 %collective-permute-start.3 = (bf16[512,1024]{1,0:T(8,128)(2,1)S(1)}, bf16[512,1024]{1,0:T(8,128)(2,1)S(1)}, u32[]{:S(2)}, u32[]{:S(2)}) collective-permute-start(bf16[512,1024]{1,0:T(8,128)(2,1)S(1)} %shard_map.107.cot_ref), channel_id=1, source_target_pairs={{0,4},{4,0},{8,12},{12,8},{16,20},{20,16},{24,28},{28,24},{1,5},{5... | collective-permute-start | bytes 3145736 | tf_op jit(solution)/shard_map/ppermute | solution.py:577
  73.5 0.9 copy-start.16
  74.4 5.6 %copy-start.21 = (bf16[128,4096]{1,0:T(8,128)(2,1)S(1)}, bf16[128,4096]{1,0:T(8,128)(2,1)}, u32[]{:S(2)}) copy-start(bf16[128,4096]{1,0:T(8,128)(2,1)} %copy-done.20) | copy-start | bytes 3145732
  78.4 1.7 %copy-start.19 = (bf16[4096,128]{1,0:T(8,128)(2,1)S(1)}, bf16[4096,128]{1,0:T(8,128)(2,1)}, u32[]{:S(2)}) copy-start(bf16[4096,128]{1,0:T(8,128)(2,1)} %copy-done.18) | copy-start | bytes 3145732
  80.1 11.4 %copy-start.11 = (bf16[528,256]{1,0:T(8,128)(2,1)S(1)}, bf16[528,256]{1,0:T(8,128)(2,1)}, u32[]{:S(2)}) copy-start(bf16[528,256]{1,0:T(8,128)(2,1)} %copy-done.10) | copy-start | bytes 811012
  80.1 11.4 %copy-start.13 = (bf16[528,256]{1,0:T(8,128)(2,1)S(1)}, bf16[528,256]{1,0:T(8,128)(2,1)}, u32[]{:S(2)}) copy-start(bf16[528,256]{1,0:T(8,128)(2,1)} %copy-done.12) | copy-start | bytes 811012
  88.3 15.9 %collective-permute-start.6 = (bf16[416,512]{1,0:T(8,128)(2,1)S(1)}, bf16[416,512]{1,0:T(8,128)(2,1)S(1)}, u32[]{:S(2)}, u32[]{:S(2)}) collective-permute-start(bf16[416,512]{1,0:T(8,128)(2,1)S(1)} %get-tuple-element.39.refs_2_), channel_id=1, source_target_pairs={{0,8},{4,12},{8,0},{12,4},{16,24},{20,28},{24,16},{28,20},{1,9},{5... | collective-permute-start | bytes 1277960 | tf_op jit(solution)/shard_map/ppermute | solution.py:577
  90.7 13.6 %copy-start.17 = (bf16[208,512]{1,0:T(8,128)(2,1)S(1)}, bf16[208,512]{1,0:T(8,128)(2,1)}, u32[]{:S(2)}) copy-start(bf16[208,512]{1,0:T(8,128)(2,1)} %copy-done.15) | copy-start | bytes 638980
  90.7 13.6 %collective-permute-start.7 = (bf16[416,512]{1,0:T(8,128)(2,1)S(1)}, bf16[416,512]{1,0:T(8,128)(2,1)S(1)}, u32[]{:S(2)}, u32[]{:S(2)}) collective-permute-start(bf16[416,512]{1,0:T(8,128)(2,1)S(1)} %get-tuple-element.40.refs_3_), channel_id=1, source_target_pairs={{8,16},{12,20},{16,8},{20,12},{9,17},{13,21},{17,9},{21,13},{10,18... | collective-permute-start | bytes 1277960 | tf_op jit(solution)/shard_map/ppermute | solution.py:651
  106.6 12.4 %collective-permute-start.8 = (bf16[512,256]{1,0:T(8,128)(2,1)S(1)}, bf16[512,256]{1,0:T(8,128)(2,1)S(1)}, u32[]{:S(2)}, u32[]{:S(2)}) collective-permute-start(bf16[512,256]{1,0:T(8,128)(2,1)S(1)} %get-tuple-element.46), channel_id=1, source_target_pairs={{0,4},{4,0},{8,12},{12,8},{16,20},{20,16},{24,28},{28,24},{1,5},{5... | collective-permute-start | bytes 786440 | tf_op jit(solution)/shard_map/ppermute | solution.py:577
  107.2 9.4 %collective-permute-start.10 = (bf16[512,128]{1,0:T(8,128)(2,1)S(1)}, bf16[512,128]{1,0:T(8,128)(2,1)S(1)}, u32[]{:S(2)}, u32[]{:S(2)}) collective-permute-start(bf16[512,128]{1,0:T(8,128)(2,1)S(1)} %get-tuple-element.48), channel_id=1, source_target_pairs={{0,6},{1,7},{2,4},{3,5},{4,2},{5,3},{6,0},{7,1},{8,14},{9,15},{10,... | collective-permute-start | bytes 393224 | tf_op jit(solution)/shard_map/ppermute | solution.py:584
  109.6 9.4 %collective-permute-start.9 = (bf16[512,128]{1,0:T(8,128)(2,1)S(1)}, bf16[512,128]{1,0:T(8,128)(2,1)S(1)}, u32[]{:S(2)}, u32[]{:S(2)}) collective-permute-start(bf16[512,128]{1,0:T(8,128)(2,1)S(1)} %get-tuple-element.47), channel_id=1, source_target_pairs={{0,2},{1,3},{2,0},{3,1},{4,6},{5,7},{6,4},{7,5},{8,10},{9,11},{10,... | collective-permute-start | bytes 393224 | tf_op jit(solution)/shard_map/ppermute | solution.py:580
  110.1 10.1 %collective-permute-start.15 = (bf16[128,256]{1,0:T(8,128)(2,1)S(1)}, bf16[128,256]{1,0:T(8,128)(2,1)S(1)}, u32[]{:S(2)}, u32[]{:S(2)}) collective-permute-start(bf16[128,256]{1,0:T(8,128)(2,1)S(1)} %get-tuple-element.52), channel_id=1, source_target_pairs={{0,8},{4,12},{8,0},{12,4},{16,24},{20,28},{24,16},{28,20},{1,9},{5... | collective-permute-start | bytes 196616 | tf_op jit(solution)/shard_map/ppermute | solution.py:577
  116.6 5.3 %collective-permute-start.16 = (bf16[128,256]{1,0:T(8,128)(2,1)S(1)}, bf16[128,256]{1,0:T(8,128)(2,1)S(1)}, u32[]{:S(2)}, u32[]{:S(2)}) collective-permute-start(bf16[128,256]{1,0:T(8,128)(2,1)S(1)} %get-tuple-element.53), channel_id=1, source_target_pairs={{0,16},{4,20},{8,24},{12,28},{16,0},{20,4},{24,8},{28,12},{1,17},{... | collective-permute-start | bytes 196616 | tf_op jit(solution)/shard_map/ppermute | solution.py:577
  116.6 6.1 %collective-permute-start.17 = (bf16[128,256]{1,0:T(8,128)(2,1)S(1)}, bf16[128,256]{1,0:T(8,128)(2,1)S(1)}, u32[]{:S(2)}, u32[]{:S(2)}) collective-permute-start(bf16[128,256]{1,0:T(8,128)(2,1)S(1)} %get-tuple-element.54), channel_id=1, source_target_pairs={{0,24},{4,28},{8,16},{12,20},{16,8},{20,12},{24,0},{28,4},{1,25},{... | collective-permute-start | bytes 196616 | tf_op jit(solution)/shard_map/ppermute | solution.py:577
  119.0 4.4 %copy-start.6 = (bf16[256,1024]{1,0:T(8,128)(2,1)S(1)}, bf16[256,1024]{1,0:T(8,128)(2,1)}, u32[]{:S(2)}) copy-start(bf16[256,1024]{1,0:T(8,128)(2,1)} %w_ref.1) | copy-start | bytes 1572868
  120.3 12.0 %collective-permute-start.11 = (bf16[512,512]{1,0:T(8,128)(2,1)S(1)}, bf16[512,512]{1,0:T(8,128)(2,1)S(1)}, u32[]{:S(2)}, u32[]{:S(2)}) collective-permute-start(bf16[512,512]{1,0:T(8,128)(2,1)S(1)} %get-tuple-element.49.here_ref), channel_id=1, source_target_pairs={{0,1},{1,0},{2,3},{3,2},{4,5},{5,4},{6,7},{7,6},{8,9},{9,8},{10,11... | collective-permute-start | bytes 1572872 | tf_op jit(solution)/shard_map/ppermute | solution.py:580
  122.7 4.3 %collective-permute-start.18 = (bf16[128,256]{1,0:T(8,128)(2,1)S(1)}, bf16[128,256]{1,0:T(8,128)(2,1)S(1)}, u32[]{:S(2)}, u32[]{:S(2)}) collective-permute-start(bf16[128,256]{1,0:T(8,128)(2,1)S(1)} %add_convert_fusion), channel_id=1, source_target_pairs={{0,4},{4,0},{8,12},{12,8},{16,20},{20,16},{24,28},{28,24},{1,5},{5... | collective-permute-start | bytes 196616 | tf_op jit(solution)/shard_map/ppermute | solution.py:577
  123.4 5.0 %collective-permute-start.12 = (bf16[256,256]{1,0:T(8,128)(2,1)S(1)}, bf16[256,256]{1,0:T(8,128)(2,1)S(1)}, u32[]{:S(2)}, u32[]{:S(2)}) collective-permute-start(bf16[256,256]{1,0:T(8,128)(2,1)S(1)} %get-tuple-element.58), channel_id=1, source_target_pairs={{0,1},{1,0},{2,3},{3,2},{4,5},{5,4},{6,7},{7,6},{8,9},{9,8},{10,11... | collective-permute-start | bytes 393224 | tf_op jit(solution)/shard_map/ppermute | solution.py:580
  123.5 6.6 %collective-permute-start.13 = (bf16[256,256]{1,0:T(8,128)(2,1)S(1)}, bf16[256,256]{1,0:T(8,128)(2,1)S(1)}, u32[]{:S(2)}, u32[]{:S(2)}) collective-permute-start(bf16[256,256]{1,0:T(8,128)(2,1)S(1)} %get-tuple-element.60), channel_id=1, source_target_pairs={{0,2},{1,3},{2,0},{3,1},{4,6},{5,7},{6,4},{7,5},{8,10},{9,11},{10,... | collective-permute-start | bytes 393224 | tf_op jit(solution)/shard_map/ppermute | solution.py:580
  125.1 7.2 %collective-permute-start.14 = (bf16[256,256]{1,0:T(8,128)(2,1)S(1)}, bf16[256,256]{1,0:T(8,128)(2,1)S(1)}, u32[]{:S(2)}, u32[]{:S(2)}) collective-permute-start(bf16[256,256]{1,0:T(8,128)(2,1)S(1)} %get-tuple-element.57), channel_id=1, source_target_pairs={{0,3},{1,2},{2,1},{3,0},{4,7},{5,6},{6,5},{7,4},{8,11},{9,10},{10,... | collective-permute-start | bytes 393224 | tf_op jit(solution)/shard_map/ppermute | solution.py:580
  127.0 6.4 %collective-permute-start.19 = (bf16[2,128,256]{2,1,0:T(8,128)(2,1)S(1)}, bf16[2,128,256]{2,1,0:T(8,128)(2,1)S(1)}, u32[]{:S(2)}, u32[]{:S(2)}) collective-permute-start(bf16[2,128,256]{2,1,0:T(8,128)(2,1)S(1)} %pad_maximum_fusion.1.refs_0_), channel_id=1, source_target_pairs={{0,8},{4,12},{8,0},{12,4},{16,24},{20,28},{24,16},{28,20},{1,9},{5... | collective-permute-start | bytes 393224 | tf_op jit(solution)/shard_map/ppermute | solution.py:577
  128.4 11.9 %collective-permute-start.20 = (bf16[2,128,256]{2,1,0:T(8,128)(2,1)S(1)}, bf16[2,128,256]{2,1,0:T(8,128)(2,1)S(1)}, u32[]{:S(2)}, u32[]{:S(2)}) collective-permute-start(bf16[2,128,256]{2,1,0:T(8,128)(2,1)S(1)} %pad_maximum_fusion.1.refs_0_), channel_id=1, source_target_pairs={{0,16},{4,20},{8,24},{12,28},{16,0},{20,4},{24,8},{28,12},{1,17},{... | collective-permute-start | bytes 393224 | tf_op jit(solution)/shard_map/ppermute | solution.py:577
  130.1 10.2 %collective-permute-start.21 = (bf16[2,128,256]{2,1,0:T(8,128)(2,1)S(1)}, bf16[2,128,256]{2,1,0:T(8,128)(2,1)S(1)}, u32[]{:S(2)}, u32[]{:S(2)}) collective-permute-start(bf16[2,128,256]{2,1,0:T(8,128)(2,1)S(1)} %pad_maximum_fusion.1.refs_0_), channel_id=1, source_target_pairs={{0,24},{4,28},{8,16},{12,20},{16,8},{20,12},{24,0},{28,4},{1,25},{... | collective-permute-start | bytes 393224 | tf_op jit(solution)/shard_map/ppermute | solution.py:577
  140.3 1.0 copy-start.9
  (1 other events, 0.7 us)

commit v2 on v1

--- a/solution.py
+++ b/solution.py
@@ -21,7 +21,7 @@
 F32 = jnp.float32
 NT = (((1,), (1,)), ((), ()))
 CLIPS = (0, 2, 1, 3)
-VMEM_LIMIT = 48 * 1024 * 1024
+VMEM_LIMIT = 24 * 1024 * 1024
 
 
 def params(*semantics):
@@ -54,6 +54,22 @@
         compiler_params=params("arbitrary"),
         cost_estimate=cost(0, 3 * rows * feats * 2),
     )(keys, values, *after)
+
+
+def gate_kernel(x_ref, after_ref, out_ref):
+    pass
+
+
+def gate(x, after):
+    hbm = pl.BlockSpec(memory_space=pltpu.HBM)
+    return pl.pallas_call(
+        gate_kernel,
+        in_specs=[hbm] * 2,
+        out_specs=hbm,
+        out_shape=jax.ShapeDtypeStruct(x.shape, x.dtype),
+        input_output_aliases={0: 0},
+        compiler_params=params(),
+    )(x, after)
 
 
 def order_kernel(idx_ref, arr_ref, *refs):
@@ -496,7 +512,8 @@
 
 
 def project_kernel(here_ref, there_ref, *refs):
-    columns, out_ref = refs[:-1], refs[-1]
+    columns, out_ref, token_ref = refs[:-2], refs[-2], refs[-1]
+    token_ref[...] = jnp.zeros_like(token_ref)
     cols = columns[0].shape[0]
     total = None
     for i, w in enumerate(columns):
@@ -513,8 +530,11 @@
     return pl.pallas_call(
         project_kernel,
         in_specs=[vm] * (2 + len(columns)),
-        out_specs=vm,
-        out_shape=jax.ShapeDtypeStruct((rows, cols), BF),
+        out_specs=[vm] * 2,
+        out_shape=[
+            jax.ShapeDtypeStruct((rows, cols), BF),
+            jax.ShapeDtypeStruct((8, 128), F32),
+        ],
         compiler_params=params(),
         cost_estimate=cost(2 * rows * cols * 4 * cols, 12 * rows * cols),
     )(here, there, *columns)
@@ -600,7 +620,8 @@
     qg_peer = swap(qg_give, 1)
     sent = [pack(teacher_key, teacher_value, groups, slots, 0)]
     sent += [
-        pack(teacher_key, teacher_value, groups, slots, s, qg_peer) for s in range(1, slots)
+        gate(pack(teacher_key, teacher_value, groups, slots, s), qg_peer)
+        for s in range(1, slots)
     ]
     qga = jnp.where(half == 0, qg_mine, qg_peer)
     qgb = jnp.where(half == 0, qg_peer, qg_mine)
@@ -632,7 +653,8 @@
         arrived = lax.all_to_all(
             sent[s].reshape(shards, 2 * piece, 2 * HDIM), "tm", 0, 0
         )
-        kvs += put_in_order(arrived, index, teacher_rows, *parts[-2:])
+        kv, kvt = put_in_order(arrived, index, teacher_rows, *parts[-2:-1])
+        kvs += [kv, kvt]
         if s == slots - 1:
             count = band.shape[0]
             ends = tails(qg_left, qg_right, count, kvs[-1])
@@ -643,7 +665,7 @@
         own = place, [s], 4, rows, own_limits, qga, qgb, kvs[-2:], False
         parts += attend(*own, *(far if s == slots - 1 else ()))
         if s == 0:
-            edge_a, edge_b = edges(place, qg_mine, qg_peer, parts[0])
+            edge_a, edge_b = edges(place, qg_mine, qg_peer, kv)
             qg_left, qg_right = up(edge_b), down(edge_a)
             cot = whole_cotangent(place, here, there, parts[0])
     parts += [swap(far[0], 2)]
@@ -660,8 +682,8 @@
     near, grad_query = heads(
         place, mine, swap(give, 1), swap_clip(xmine, 2), swap_both(xgive, 2)
     )
-    joined = project(near, swap_clip(near, 1), columns)
-    return joined, grad_query, spread(place, held, joined)
+    joined, token = project(near, swap_clip(near, 1), columns)
+    return joined, grad_query, spread(place, held, token)
 
 
 def solution(mesh):

time: 141 us -> 133 us (0.943); the launches traced: 143 us -> 130 us
  Pallas kernels: 54.3 us -> 41.5 us
  waiting for transfers between devices: 28.3 us -> 33.3 us
  local copies, waits for them, and re-layouts: 8.15 us -> 5.08 us
  starting transfers between devices: 49.7 us -> 48.1 us
    pallas_call x3, Pallas kernels: 33.5 us -> 19.6 us  [attend(): pl.pallas_call(functools.partial(attend_kernel, slots, tiles, by_exchange...]
    all_to_all x2, waiting for transfers between devices: 0.03 us -> 6.24 us  [on_device(): lax.all_to_all(sent[s].reshape(shards, 2 * piece, 2 * HDIM), 'tm', 0, 0)]
    ppermute x11, starting transfers between devices: 20.9 us -> 24.7 us  [swap(): return lax.ppermute(x, 'tm', [(i, i ^ d) for i in range(shards)])]
    unnamed x50 -> x44, local copies, waits for them, and re-layouts: 8.07 us -> 5 us
    all_to_all x2, starting transfers between devices: 13.8 us -> 11.3 us  [on_device(): lax.all_to_all(sent[s].reshape(shards, 2 * piece, 2 * HDIM), 'tm', 0, 0)]
    ppermute x11, waiting for transfers between devices: 19.8 us -> 18 us  [swap(): return lax.ppermute(x, 'tm', [(i, i ^ d) for i in range(shards)])]
    ppermute x1, starting transfers between devices: 6.25 us -> 4.64 us  [up(): return lax.ppermute(x, 'tm', [(i, i + 2) for i in range(shards - 2)])]
  transfers between devices with their start and end apart: 24 -> 24, of which waited for: 8 -> 11; matrix products, arithmetic and copies ran while one was open for 1% -> 1% of each run, Pallas kernels for 34% -> 27%
where the time goes in v2:
time: 133 us; the launch traced here: 130 us
  starting transfers between devices  48.1 us (36%)
  Pallas kernels  41.5 us (31%)
  waiting for transfers between devices  33.3 us (25%)
  local copies, waits for them, and re-layouts  5.08 us (4%)
  other arithmetic  1.33 us (1%)
    ppermute x11, starting transfers between devices, swap(): return lax.ppermute(x, 'tm', [(i, i ^ d) for i in range(shards)])  24.7 us
    pallas_call x3, Pallas kernels, attend(): pl.pallas_call(functools.partial(attend_kernel, slots, tiles, by_exchange...  19.6 us
    ppermute x11, waiting for transfers between devices, swap(): return lax.ppermute(x, 'tm', [(i, i ^ d) for i in range(shards)])  18 us
    all_to_all x2, starting transfers between devices, on_device(): lax.all_to_all(sent[s].reshape(shards, 2 * piece, 2 * HDIM), 'tm', 0, 0)  11.3 us
    ppermute x7, waiting for transfers between devices, swap_clip(): return lax.ppermute(x, 'clip', [(i, i ^ d) for i in range(clips)])  9.09 us
    pallas_call x2, Pallas kernels, put_in_order(): pl.pallas_call(order_kernel, grid=(2,), in_specs=[pl.BlockSpec((1, 1, row...  6.74 us
    all_to_all x2, waiting for transfers between devices, on_device(): lax.all_to_all(sent[s].reshape(shards, 2 * piece, 2 * HDIM), 'tm', 0, 0)  6.24 us
    unnamed x44, local copies, waits for them, and re-layouts  5 us
  transfers between devices with their start and end apart: 24, of which 11 were waited for; matrix products, arithmetic and copies ran while one was open for 1% of the time, Pallas kernels for 27%

profile of v2, /device:TPU:0, one launch (start us, length us, event | category | flops | bytes accessed | tf_op | source)
XLA Modules:
  0.0 130.4 jit_solution(8886407340222263526)
XLA Ops:
  0.6 1.2 copy-done
  1.9 1.2 copy-done.2
  3.1 1.8 %shard_map.104 = bf16[4,2,512,128]{3,2,1,0:T(8,128)(2,1)} custom-call(bf16[2048,256]{1,0:T(8,128)(2,1)S(1)} %copy-done, bf16[2048,256]{1,0:T(8,128)(2,1)S(1)} %copy-done.2), custom_call_target="tpu_custom_call" | custom-call | bytes 3145728 | tf_op jit(solution)/shard_map/pallas_call | solution.py:48
  4.9 7.4 %all-to-all-start = ((bf16[8,512,128]{2,1,0:T(8,128)(2,1)}), bf16[8,512,128]{2,1,0:T(8,128)(2,1)}, u32[]{:S(2)}, u32[]{:S(2)}) async-start(bf16[8,512,128]{2,1,0:T(8,128)(2,1)} %bitcast.8), calls=%async_computation | async-start | bytes 2097152 | tf_op jit(solution)/shard_map/all_to_all | solution.py:653
  12.4 1.6 %collective-permute-start = (bf16[512,256]{1,0:T(8,128)(2,1)S(1)}, bf16[512,256]{1,0:T(8,128)(2,1)S(1)}, u32[]{:S(2)}, u32[]{:S(2)}) collective-permute-start(bf16[512,256]{1,0:T(8,128)(2,1)S(1)} %copy-done.19), channel_id=1, source_target_pairs={{0,2},{1,3},{2,0},{3,1},{4,6},{5,7},{6,4},{7,5},{8,10},{9,11},{10,... | collective-permute-start | bytes 786440 | tf_op jit(solution)/shard_map/ppermute | solution.py:600
  13.9 6.3 %collective-permute-done = bf16[512,256]{1,0:T(8,128)(2,1)S(1)} collective-permute-done((bf16[512,256]{1,0:T(8,128)(2,1)S(1)}, bf16[512,256]{1,0:T(8,128)(2,1)S(1)}, u32[]{:S(2)}, u32[]{:S(2)}) %collective-permute-start) | collective-permute-done | bytes 262176 | tf_op jit(solution)/shard_map/ppermute | solution.py:600
  20.5 1.8 %collective-permute-done.1.there_ref = bf16[2,512,256]{2,1,0:T(8,128)(2,1)S(1)} collective-permute-done((bf16[2,512,256]{2,1,0:T(8,128)(2,1)S(1)}, bf16[2,512,256]{2,1,0:T(8,128)(2,1)S(1)}, u32[]{:S(2)}, u32[]{:S(2)}) %collective-permute-start.1) | collective-permute-done | bytes 524320 | tf_op jit(solution)/shard_map/ppermute | solution.py:600
  22.2 1.0 copy-done.4
  23.3 1.1 shard_map.103
  24.4 0.7 copy-done.6
  25.1 1.7 %collective-permute-start.2 = (bf16[528,256]{1,0:T(8,128)(2,1)S(1)}, bf16[528,256]{1,0:T(8,128)(2,1)S(1)}, u32[]{:S(2)}, u32[]{:S(2)}) collective-permute-start(bf16[528,256]{1,0:T(8,128)(2,1)S(1)} %get-tuple-element.32), channel_id=1, source_target_pairs={{0,4},{4,0},{8,12},{12,8},{16,20},{20,16},{24,28},{28,24},{1,5},{5... | collective-permute-start | bytes 811016 | tf_op jit(solution)/shard_map/ppermute | solution.py:597
  26.8 1.8 %shard_map.108.x_ref = bf16[4,2,512,128]{3,2,1,0:T(8,128)(2,1)} custom-call(bf16[2048,256]{1,0:T(8,128)(2,1)S(1)} %copy-done.1, bf16[2048,256]{1,0:T(8,128)(2,1)S(1)} %copy-done.3), custom_call_target="tpu_custom_call" | custom-call | bytes 3145728 | tf_op jit(solution)/shard_map/pallas_call | solution.py:48
  28.6 7.5 %collective-permute-done.2.after_ref.peer_ref = bf16[528,256]{1,0:T(8,128)(2,1)S(1)} collective-permute-done((bf16[528,256]{1,0:T(8,128)(2,1)S(1)}, bf16[528,256]{1,0:T(8,128)(2,1)S(1)}, u32[]{:S(2)}, u32[]{:S(2)}) %collective-permute-start.2) | collective-permute-done | bytes 270368 | tf_op jit(solution)/shard_map/ppermute | solution.py:597
  36.1 2.1 %all-to-all-done.arr_ref = bf16[8,512,128]{2,1,0:T(8,128)(2,1)} async-done(((bf16[8,512,128]{2,1,0:T(8,128)(2,1)}), bf16[8,512,128]{2,1,0:T(8,128)(2,1)}, u32[]{:S(2)}, u32[]{:S(2)}) %all-to-all-start) | async-done | bytes 1048608 | tf_op jit(solution)/shard_map/all_to_all | solution.py:653
  38.2 3.9 %all-to-all-start.1 = ((bf16[8,512,128]{2,1,0:T(8,128)(2,1)}), bf16[8,512,128]{2,1,0:T(8,128)(2,1)S(1)}, u32[]{:S(2)}, u32[]{:S(2)}) async-start(bf16[8,512,128]{2,1,0:T(8,128)(2,1)} %bitcast.9), calls=%async_computation.1 | async-start | bytes 2097152 | tf_op jit(solution)/shard_map/all_to_all | solution.py:653
  42.1 0.7 fusion.2
  43.1 3.9 %shard_map.105 = (bf16[4096,128]{1,0:T(8,128)(2,1)S(1)}, bf16[128,4096]{1,0:T(8,128)(2,1)S(1)}) custom-call(s32[2,1,2048]{2,1,0:T(1,128)S(1)} %bitcast.14, bf16[8,512,128]{2,1,0:T(8,128)(2,1)} %all-to-all-done.arr_ref), custom_call_target="tpu_custom_call" | custom-call | flops 2147483648 | bytes 3145728 | tf_op jit(solution)/shard_map/pallas_call | solution.py:94
  47.0 1.5 %shard_map.111 = (bf16[528,256]{1,0:T(8,128)(2,1)}, bf16[528,256]{1,0:T(8,128)(2,1)}) custom-call(s32[3]{0:T(128)S(1)} %pad_add_fusion.2.place_ref, bf16[528,256]{1,0:T(8,128)(2,1)S(1)} %copy-done.7, bf16[528,256]{1,0:T(8,128)(2,1)S(1)} %collective-permute-done.2.after_ref.peer_ref, bf16[4096,128]{1,0:T(8,128)(2,1)S(1)} %get-tuple-element.33.refs_0_.after_ref), custom_call_target="tpu_custom_call" | custom-call | bytes 1081344 | tf_op jit(solution)/shard_map/pallas_call | solution.py:188
  48.5 4.6 %collective-permute-start.4 = (bf16[528,256]{1,0:T(8,128)(2,1)}, bf16[528,256]{1,0:T(8,128)(2,1)}, u32[]{:S(2)}, u32[]{:S(2)}) collective-permute-start(bf16[528,256]{1,0:T(8,128)(2,1)} %get-tuple-element.39), channel_id=1, source_target_pairs={{0,8},{4,12},{8,16},{12,20},{16,24},{20,28},{1,9},{5,13},{9,17},{1... | collective-permute-start | bytes 811016 | tf_op jit(solution)/shard_map/ppermute | solution.py:607
  53.1 1.3 collective-permute-start.5
  54.4 7.8 %shard_map.106 = (bf16[208,512]{1,0:T(8,128)(2,1)S(1)}, bf16[208,512]{1,0:T(8,128)(2,1)S(1)}) custom-call(s32[3]{0:T(128)S(1)} %pad_add_fusion.2.place_ref, s32[2,32]{1,0:T(2,128)S(1)} %pad_add_fusion.lohi_ref, bf16[528,256]{1,0:T(8,128)(2,1)S(1)} %get-tuple-element.59.qga_ref, bf16[528,256]{1,0:T(8,128)(2,1)S(1)} %get-tuple-element.60.qgb_ref, ...), custom_call_target="tpu_custom_call" | custom-call | flops 2147483648 | bytes 4194304 | tf_op jit(solution)/shard_map/pallas_call | solution.py:376
  63.6 1.5 %collective-permute-start.3 = (bf16[512,1024]{1,0:T(8,128)(2,1)S(1)}, bf16[512,1024]{1,0:T(8,128)(2,1)}, u32[]{:S(2)}, u32[]{:S(2)}) collective-permute-start(bf16[512,1024]{1,0:T(8,128)(2,1)S(1)} %shard_map.107.cot_ref), channel_id=1, source_target_pairs={{0,4},{4,0},{8,12},{12,8},{16,20},{20,16},{24,28},{28,24},{1,5},{5... | collective-permute-start | bytes 3145736 | tf_op jit(solution)/shard_map/ppermute | solution.py:597
  65.1 4.2 %all-to-all-done.1.arr_ref = bf16[8,512,128]{2,1,0:T(8,128)(2,1)S(1)} async-done(((bf16[8,512,128]{2,1,0:T(8,128)(2,1)}), bf16[8,512,128]{2,1,0:T(8,128)(2,1)S(1)}, u32[]{:S(2)}, u32[]{:S(2)}) %all-to-all-start.1) | async-done | bytes 1048608 | tf_op jit(solution)/shard_map/all_to_all | solution.py:653
  69.3 2.9 %shard_map.110 = (bf16[4096,128]{1,0:T(8,128)(2,1)S(1)}, bf16[128,4096]{1,0:T(8,128)(2,1)S(1)}) custom-call(s32[2,1,2048]{2,1,0:T(1,128)S(1)} %bitcast.15, bf16[8,512,128]{2,1,0:T(8,128)(2,1)S(1)} %all-to-all-done.1.arr_ref, bf16[208,512]{1,0:T(8,128)(2,1)S(1)} %get-tuple-element.35.after_ref.refs_0_), custom_call_target="tpu_custom_call" | custom-call | flops 2147483648 | bytes 3145728 | tf_op jit(solution)/shard_map/pallas_call | solution.py:94
  72.2 1.1 shard_map.112
  73.6 4.1 %shard_map.113 = (bf16[416,512]{1,0:T(8,128)(2,1)S(1)}, bf16[416,512]{1,0:T(8,128)(2,1)S(1)}) custom-call(s32[3]{0:T(128)S(1)} %pad_add_fusion.2.place_ref, s32[2,32]{1,0:T(2,128)S(1)} %pad_add_fusion.1.lohi_ref, bf16[528,256]{1,0:T(8,128)(2,1)} %collective-permute-done.4.left_ref.qga_ref, bf16[528,256]{1,0:T(8,128)(2,1)} %collective-permute-done.5.right_ref.qgb_ref, ...), custom_call_target="tpu_custom_call" | custom-call | flops 4294967296 | bytes 8388608 | tf_op jit(solution)/shard_map/pallas_call | solution.py:376
  77.7 4.2 %collective-permute-start.6 = (bf16[416,512]{1,0:T(8,128)(2,1)S(1)}, bf16[416,512]{1,0:T(8,128)(2,1)S(1)}, u32[]{:S(2)}, u32[]{:S(2)}) collective-permute-start(bf16[416,512]{1,0:T(8,128)(2,1)S(1)} %get-tuple-element.41.refs_2_), channel_id=1, source_target_pairs={{0,8},{4,12},{8,0},{12,4},{16,24},{20,28},{24,16},{28,20},{1,9},{5... | collective-permute-start | bytes 1277960 | tf_op jit(solution)/shard_map/ppermute | solution.py:597
  81.9 0.8 collective-permute-start.7
  82.7 7.7 %shard_map.114 = (bf16[208,512]{1,0:T(8,128)(2,1)S(1)}, bf16[208,512]{1,0:T(8,128)(2,1)S(1)}) custom-call(s32[3]{0:T(128)S(1)} %pad_add_fusion.2.place_ref, s32[2,32]{1,0:T(2,128)S(1)} %pad_add_fusion.lohi_ref, bf16[528,256]{1,0:T(8,128)(2,1)S(1)} %copy-done.11, bf16[528,256]{1,0:T(8,128)(2,1)S(1)} %copy-done.13, ...), custom_call_target="tpu_custom_call" | custom-call | flops 2147483648 | bytes 4194304 | tf_op jit(solution)/shard_map/pallas_call | solution.py:376
  90.7 2.2 %shard_map.115 = (bf16[256,512]{1,0:T(8,128)(2,1)S(1)}, bf16[256,512]{1,0:T(8,128)(2,1)S(1)}, bf16[128,256]{1,0:T(8,128)(2,1)S(1)}, bf16[128,256]{1,0:T(8,128)(2...) custom-call(s32[3]{0:T(128)S(1)} %pad_add_fusion.2.place_ref, ...), custom_call_target="tpu_custom_call" | custom-call | flops 268435456 | bytes 8388608 | tf_op jit(solution)/shard_map/pallas_call | solution.py:443
  92.9 0.7 shard_map.116
  93.7 1.7 %collective-permute-start.8 = (bf16[512,256]{1,0:T(8,128)(2,1)S(1)}, bf16[512,256]{1,0:T(8,128)(2,1)S(1)}, u32[]{:S(2)}, u32[]{:S(2)}) collective-permute-start(bf16[512,256]{1,0:T(8,128)(2,1)S(1)} %get-tuple-element.48), channel_id=1, source_target_pairs={{0,4},{4,0},{8,12},{12,8},{16,20},{20,16},{24,28},{28,24},{1,5},{5... | collective-permute-start | bytes 786440 | tf_op jit(solution)/shard_map/ppermute | solution.py:597
  95.4 1.3 collective-permute-start.10
  97.2 4.0 %collective-permute-start.15 = (bf16[128,256]{1,0:T(8,128)(2,1)S(1)}, bf16[128,256]{1,0:T(8,128)(2,1)S(1)}, u32[]{:S(2)}, u32[]{:S(2)}) collective-permute-start(bf16[128,256]{1,0:T(8,128)(2,1)S(1)} %get-tuple-element.55), channel_id=1, source_target_pairs={{0,8},{4,12},{8,0},{12,4},{16,24},{20,28},{24,16},{28,20},{1,9},{5... | collective-permute-start | bytes 196616 | tf_op jit(solution)/shard_map/ppermute | solution.py:597
  101.2 3.9 %collective-permute-start.16 = (bf16[128,256]{1,0:T(8,128)(2,1)S(1)}, bf16[128,256]{1,0:T(8,128)(2,1)S(1)}, u32[]{:S(2)}, u32[]{:S(2)}) collective-permute-start(bf16[128,256]{1,0:T(8,128)(2,1)S(1)} %get-tuple-element.56), channel_id=1, source_target_pairs={{0,16},{4,20},{8,24},{12,28},{16,0},{20,4},{24,8},{28,12},{1,17},{... | collective-permute-start | bytes 196616 | tf_op jit(solution)/shard_map/ppermute | solution.py:597
  105.1 2.1 %collective-permute-start.17 = (bf16[128,256]{1,0:T(8,128)(2,1)S(1)}, bf16[128,256]{1,0:T(8,128)(2,1)S(1)}, u32[]{:S(2)}, u32[]{:S(2)}) collective-permute-start(bf16[128,256]{1,0:T(8,128)(2,1)S(1)} %get-tuple-element.57), channel_id=1, source_target_pairs={{0,24},{4,28},{8,16},{12,20},{16,8},{20,12},{24,0},{28,4},{1,25},{... | collective-permute-start | bytes 196616 | tf_op jit(solution)/shard_map/ppermute | solution.py:597
  107.2 1.3 shard_map.117
  108.5 2.6 %collective-permute-done.17 = bf16[128,256]{1,0:T(8,128)(2,1)S(1)} collective-permute-done((bf16[128,256]{1,0:T(8,128)(2,1)S(1)}, bf16[128,256]{1,0:T(8,128)(2,1)S(1)}, u32[]{:S(2)}, u32[]{:S(2)}) %collective-permute-start.17) | collective-permute-done | bytes 65568 | tf_op jit(solution)/shard_map/ppermute | solution.py:597
  111.2 1.3 %collective-permute-start.18 = (bf16[128,256]{1,0:T(8,128)(2,1)S(1)}, bf16[128,256]{1,0:T(8,128)(2,1)S(1)}, u32[]{:S(2)}, u32[]{:S(2)}) collective-permute-start(bf16[128,256]{1,0:T(8,128)(2,1)S(1)} %add_convert_fusion), channel_id=1, source_target_pairs={{0,4},{4,0},{8,12},{12,8},{16,20},{20,16},{24,28},{28,24},{1,5},{5... | collective-permute-start | bytes 196616 | tf_op jit(solution)/shard_map/ppermute | solution.py:597
  112.7 1.6 %collective-permute-start.13 = (bf16[256,256]{1,0:T(8,128)(2,1)S(1)}, bf16[256,256]{1,0:T(8,128)(2,1)S(1)}, u32[]{:S(2)}, u32[]{:S(2)}) collective-permute-start(bf16[256,256]{1,0:T(8,128)(2,1)S(1)} %get-tuple-element.64), channel_id=1, source_target_pairs={{0,2},{1,3},{2,0},{3,1},{4,6},{5,7},{6,4},{7,5},{8,10},{9,11},{10,... | collective-permute-start | bytes 393224 | tf_op jit(solution)/shard_map/ppermute | solution.py:600
  114.5 1.0 collective-permute-done.18
  115.6 1.3 collective-permute-start.19
  116.9 1.4 %collective-permute-start.20 = (bf16[2,128,256]{2,1,0:T(8,128)(2,1)S(1)}, bf16[2,128,256]{2,1,0:T(8,128)(2,1)S(1)}, u32[]{:S(2)}, u32[]{:S(2)}) collective-permute-start(bf16[2,128,256]{2,1,0:T(8,128)(2,1)S(1)} %pad_maximum_fusion.1.refs_0_), channel_id=1, source_target_pairs={{0,16},{4,20},{8,24},{12,28},{16,0},{20,4},{24,8},{28,12},{1,17},{... | collective-permute-start | bytes 393224 | tf_op jit(solution)/shard_map/ppermute | solution.py:597
  118.3 0.8 collective-permute-done.13.refs_2_
  119.0 1.6 %collective-permute-start.21 = (bf16[2,128,256]{2,1,0:T(8,128)(2,1)S(1)}, bf16[2,128,256]{2,1,0:T(8,128)(2,1)S(1)}, u32[]{:S(2)}, u32[]{:S(2)}) collective-permute-start(bf16[2,128,256]{2,1,0:T(8,128)(2,1)S(1)} %pad_maximum_fusion.1.refs_0_), channel_id=1, source_target_pairs={{0,24},{4,28},{8,16},{12,20},{16,8},{20,12},{24,0},{28,4},{1,25},{... | collective-permute-start | bytes 393224 | tf_op jit(solution)/shard_map/ppermute | solution.py:597
  121.0 1.2 shard_map.118
  122.1 6.6 %collective-permute-done.20.refs_2_ = bf16[2,128,256]{2,1,0:T(8,128)(2,1)S(1)} collective-permute-done((bf16[2,128,256]{2,1,0:T(8,128)(2,1)S(1)}, bf16[2,128,256]{2,1,0:T(8,128)(2,1)S(1)}, u32[]{:S(2)}, u32[]{:S(2)}) %collective-permute-start.20) | collective-permute-done | bytes 131104 | tf_op jit(solution)/shard_map/ppermute | solution.py:597
  128.7 1.6 %shard_map.119 = f32[256,1024]{1,0:T(8,128)} custom-call(s32[3]{0:T(128)S(1)} %pad_add_fusion.2.place_ref, bf16[2,128,256]{2,1,0:T(8,128)(2,1)S(1)} %pad_maximum_fusion.1.refs_0_, bf16[2,128,256]{2,1,0:T(8,128)(2,1)S(1)} %collective-permute-done.19.refs_1_, bf16[2,128,256]{2,1,0:T(8,128)(2,1)S(1)} %collective-permute-done.20.refs_2_, ...), custom_call_target="tpu_custom_call" | custom-call | bytes 1572864 | tf_op jit(solution)/shard_map/pallas_call | solution.py:559
  (81 shorter events, 3.6 us)
Async XLA Ops:
  0.6 1.2 copy-start
  1.9 1.2 copy-start.2
  4.9 7.4 %copy-start.19 = (bf16[512,256]{1,0:T(8,128)(2,1)S(1)}, bf16[512,256]{1,0:T(8,128)(2,1)}, u32[]{:S(2)}) copy-start(bf16[512,256]{1,0:T(8,128)(2,1)} %param.15) | copy-start | bytes 786436
  4.9 15.5 %copy-start.20 = (s32[16]{0:T(128)S(1)}, s32[16]{0:T(128)}, u32[]{:S(2)}) copy-start(s32[16]{0:T(128)} %param.13) | copy-start | bytes 196
  4.9 15.5 %copy-start.21 = (s32[16]{0:T(128)S(1)}, s32[16]{0:T(128)}, u32[]{:S(2)}) copy-start(s32[16]{0:T(128)} %param.12) | copy-start | bytes 196
  4.9 17.3 %copy-start.14 = (bf16[512,256]{1,0:T(8,128)(2,1)S(1)}, bf16[512,256]{1,0:T(8,128)(2,1)}, u32[]{:S(2)}) copy-start(bf16[512,256]{1,0:T(8,128)(2,1)} %q_ref.1) | copy-start | bytes 786436
  4.9 33.3 %all-to-all-start = ((bf16[8,512,128]{2,1,0:T(8,128)(2,1)}), bf16[8,512,128]{2,1,0:T(8,128)(2,1)}, u32[]{:S(2)}, u32[]{:S(2)}) async-start(bf16[8,512,128]{2,1,0:T(8,128)(2,1)} %bitcast.8), calls=%async_computation | async-start | bytes 2097152 | tf_op jit(solution)/shard_map/all_to_all | solution.py:653
  12.4 7.8 %collective-permute-start = (bf16[512,256]{1,0:T(8,128)(2,1)S(1)}, bf16[512,256]{1,0:T(8,128)(2,1)S(1)}, u32[]{:S(2)}, u32[]{:S(2)}) collective-permute-start(bf16[512,256]{1,0:T(8,128)(2,1)S(1)} %copy-done.19), channel_id=1, source_target_pairs={{0,2},{1,3},{2,0},{3,1},{4,6},{5,7},{6,4},{7,5},{8,10},{9,11},{10,... | collective-permute-start | bytes 786440 | tf_op jit(solution)/shard_map/ppermute | solution.py:600
  20.2 6.6 %copy-start.3 = (bf16[2048,256]{1,0:T(8,128)(2,1)S(1)}, bf16[2048,256]{1,0:T(8,128)(2,1)}, u32[]{:S(2)}) copy-start(bf16[2048,256]{1,0:T(8,128)(2,1)} %v_ref.3) | copy-start | bytes 3145732
  20.2 6.5 %copy-start.1 = (bf16[2048,256]{1,0:T(8,128)(2,1)S(1)}, bf16[2048,256]{1,0:T(8,128)(2,1)}, u32[]{:S(2)}) copy-start(bf16[2048,256]{1,0:T(8,128)(2,1)} %k_ref.3) | copy-start | bytes 3145732
  20.2 2.0 %collective-permute-start.1 = (bf16[2,512,256]{2,1,0:T(8,128)(2,1)S(1)}, bf16[2,512,256]{2,1,0:T(8,128)(2,1)S(1)}, u32[]{:S(2)}, u32[]{:S(2)}) collective-permute-start(bf16[2,512,256]{2,1,0:T(8,128)(2,1)S(1)} %pad_maximum_fusion.here_ref), channel_id=1, source_target_pairs={{0,1},{1,0},{2,3},{3,2},{4,5},{5,4},{6,7},{7,6},{8,9},{9,8},{10,11... | collective-permute-start | bytes 1572872 | tf_op jit(solution)/shard_map/ppermute | solution.py:600
  22.2 1.0 copy-start.4
  24.4 0.7 copy-start.6
  25.1 11.0 %collective-permute-start.2 = (bf16[528,256]{1,0:T(8,128)(2,1)S(1)}, bf16[528,256]{1,0:T(8,128)(2,1)S(1)}, u32[]{:S(2)}, u32[]{:S(2)}) collective-permute-start(bf16[528,256]{1,0:T(8,128)(2,1)S(1)} %get-tuple-element.32), channel_id=1, source_target_pairs={{0,4},{4,0},{8,12},{12,8},{16,20},{20,16},{24,28},{28,24},{1,5},{5... | collective-permute-start | bytes 811016 | tf_op jit(solution)/shard_map/ppermute | solution.py:597
  38.2 4.6 %copy-start.7 = (bf16[528,256]{1,0:T(8,128)(2,1)S(1)}, bf16[528,256]{1,0:T(8,128)(2,1)}, u32[]{:S(2)}) copy-start(bf16[528,256]{1,0:T(8,128)(2,1)} %copy-done.6) | copy-start | bytes 811012
  38.2 31.1 %all-to-all-start.1 = ((bf16[8,512,128]{2,1,0:T(8,128)(2,1)}), bf16[8,512,128]{2,1,0:T(8,128)(2,1)S(1)}, u32[]{:S(2)}, u32[]{:S(2)}) async-start(bf16[8,512,128]{2,1,0:T(8,128)(2,1)} %bitcast.9), calls=%async_computation.1 | async-start | bytes 2097152 | tf_op jit(solution)/shard_map/all_to_all | solution.py:653
  42.9 11.5 %copy-start.10 = (bf16[528,256]{1,0:T(8,128)(2,1)}, bf16[528,256]{1,0:T(8,128)(2,1)S(1)}, u32[]{:S(2)}) copy-start(bf16[528,256]{1,0:T(8,128)(2,1)S(1)} %get-tuple-element.59.qga_ref) | copy-start | bytes 811012
  42.9 11.5 %copy-start.12 = (bf16[528,256]{1,0:T(8,128)(2,1)}, bf16[528,256]{1,0:T(8,128)(2,1)S(1)}, u32[]{:S(2)}) copy-start(bf16[528,256]{1,0:T(8,128)(2,1)S(1)} %get-tuple-element.60.qgb_ref) | copy-start | bytes 811012
  47.0 15.2 %copy-start.8 = (bf16[4096,128]{1,0:T(8,128)(2,1)}, bf16[4096,128]{1,0:T(8,128)(2,1)S(1)}, u32[]{:S(2)}) copy-start(bf16[4096,128]{1,0:T(8,128)(2,1)S(1)} %get-tuple-element.33.refs_0_.after_ref) | copy-start | bytes 3145732
  47.0 15.2 %copy-start.17 = (bf16[128,4096]{1,0:T(8,128)(2,1)}, bf16[128,4096]{1,0:T(8,128)(2,1)S(1)}, u32[]{:S(2)}) copy-start(bf16[128,4096]{1,0:T(8,128)(2,1)S(1)} %get-tuple-element.34.refs_1_) | copy-start | bytes 3145732
  48.5 23.7 %collective-permute-start.4 = (bf16[528,256]{1,0:T(8,128)(2,1)}, bf16[528,256]{1,0:T(8,128)(2,1)}, u32[]{:S(2)}, u32[]{:S(2)}) collective-permute-start(bf16[528,256]{1,0:T(8,128)(2,1)} %get-tuple-element.39), channel_id=1, source_target_pairs={{0,8},{4,12},{8,16},{12,20},{16,24},{20,28},{1,9},{5,13},{9,17},{1... | collective-permute-start | bytes 811016 | tf_op jit(solution)/shard_map/ppermute | solution.py:607
  53.1 19.1 %collective-permute-start.5 = (bf16[528,256]{1,0:T(8,128)(2,1)}, bf16[528,256]{1,0:T(8,128)(2,1)}, u32[]{:S(2)}, u32[]{:S(2)}) collective-permute-start(bf16[528,256]{1,0:T(8,128)(2,1)} %get-tuple-element.40), channel_id=1, source_target_pairs={{8,0},{12,4},{16,8},{20,12},{24,16},{28,20},{9,1},{13,5},{17,9},{2... | collective-permute-start | bytes 811016 | tf_op jit(solution)/shard_map/ppermute | solution.py:610
  62.2 0.7 copy-start.15
  63.6 26.9 %collective-permute-start.3 = (bf16[512,1024]{1,0:T(8,128)(2,1)S(1)}, bf16[512,1024]{1,0:T(8,128)(2,1)}, u32[]{:S(2)}, u32[]{:S(2)}) collective-permute-start(bf16[512,1024]{1,0:T(8,128)(2,1)S(1)} %shard_map.107.cot_ref), channel_id=1, source_target_pairs={{0,4},{4,0},{8,12},{12,8},{16,20},{20,16},{24,28},{28,24},{1,5},{5... | collective-permute-start | bytes 3145736 | tf_op jit(solution)/shard_map/ppermute | solution.py:597
  69.3 4.2 %copy-start.18 = (bf16[128,4096]{1,0:T(8,128)(2,1)S(1)}, bf16[128,4096]{1,0:T(8,128)(2,1)}, u32[]{:S(2)}) copy-start(bf16[128,4096]{1,0:T(8,128)(2,1)} %copy-done.17) | copy-start | bytes 3145732
  72.2 1.4 %copy-start.9 = (bf16[4096,128]{1,0:T(8,128)(2,1)S(1)}, bf16[4096,128]{1,0:T(8,128)(2,1)}, u32[]{:S(2)}) copy-start(bf16[4096,128]{1,0:T(8,128)(2,1)} %copy-done.8) | copy-start | bytes 3145732
  73.6 9.1 %copy-start.11 = (bf16[528,256]{1,0:T(8,128)(2,1)S(1)}, bf16[528,256]{1,0:T(8,128)(2,1)}, u32[]{:S(2)}) copy-start(bf16[528,256]{1,0:T(8,128)(2,1)} %copy-done.10) | copy-start | bytes 811012
  73.6 9.2 %copy-start.13 = (bf16[528,256]{1,0:T(8,128)(2,1)S(1)}, bf16[528,256]{1,0:T(8,128)(2,1)}, u32[]{:S(2)}) copy-start(bf16[528,256]{1,0:T(8,128)(2,1)} %copy-done.12) | copy-start | bytes 811012
  77.7 12.9 %collective-permute-start.6 = (bf16[416,512]{1,0:T(8,128)(2,1)S(1)}, bf16[416,512]{1,0:T(8,128)(2,1)S(1)}, u32[]{:S(2)}, u32[]{:S(2)}) collective-permute-start(bf16[416,512]{1,0:T(8,128)(2,1)S(1)} %get-tuple-element.41.refs_2_), channel_id=1, source_target_pairs={{0,8},{4,12},{8,0},{12,4},{16,24},{20,28},{24,16},{28,20},{1,9},{5... | collective-permute-start | bytes 1277960 | tf_op jit(solution)/shard_map/ppermute | solution.py:597
  81.9 8.8 %copy-start.16 = (bf16[208,512]{1,0:T(8,128)(2,1)S(1)}, bf16[208,512]{1,0:T(8,128)(2,1)}, u32[]{:S(2)}) copy-start(bf16[208,512]{1,0:T(8,128)(2,1)} %copy-done.15) | copy-start | bytes 638980
  81.9 8.8 %collective-permute-start.7 = (bf16[416,512]{1,0:T(8,128)(2,1)S(1)}, bf16[416,512]{1,0:T(8,128)(2,1)S(1)}, u32[]{:S(2)}, u32[]{:S(2)}) collective-permute-start(bf16[416,512]{1,0:T(8,128)(2,1)S(1)} %get-tuple-element.42.refs_3_), channel_id=1, source_target_pairs={{8,16},{12,20},{16,8},{20,12},{9,17},{13,21},{17,9},{21,13},{10,18... | collective-permute-start | bytes 1277960 | tf_op jit(solution)/shard_map/ppermute | solution.py:673
  93.7 13.5 %collective-permute-start.8 = (bf16[512,256]{1,0:T(8,128)(2,1)S(1)}, bf16[512,256]{1,0:T(8,128)(2,1)S(1)}, u32[]{:S(2)}, u32[]{:S(2)}) collective-permute-start(bf16[512,256]{1,0:T(8,128)(2,1)S(1)} %get-tuple-element.48), channel_id=1, source_target_pairs={{0,4},{4,0},{8,12},{12,8},{16,20},{20,16},{24,28},{28,24},{1,5},{5... | collective-permute-start | bytes 786440 | tf_op jit(solution)/shard_map/ppermute | solution.py:597
  95.4 9.7 %collective-permute-start.10 = (bf16[512,128]{1,0:T(8,128)(2,1)S(1)}, bf16[512,128]{1,0:T(8,128)(2,1)S(1)}, u32[]{:S(2)}, u32[]{:S(2)}) collective-permute-start(bf16[512,128]{1,0:T(8,128)(2,1)S(1)} %get-tuple-element.50), channel_id=1, source_target_pairs={{0,6},{1,7},{2,4},{3,5},{4,2},{5,3},{6,0},{7,1},{8,14},{9,15},{10,... | collective-permute-start | bytes 393224 | tf_op jit(solution)/shard_map/ppermute | solution.py:604
  96.7 10.5 %collective-permute-start.9 = (bf16[512,128]{1,0:T(8,128)(2,1)S(1)}, bf16[512,128]{1,0:T(8,128)(2,1)S(1)}, u32[]{:S(2)}, u32[]{:S(2)}) collective-permute-start(bf16[512,128]{1,0:T(8,128)(2,1)S(1)} %get-tuple-element.49), channel_id=1, source_target_pairs={{0,2},{1,3},{2,0},{3,1},{4,6},{5,7},{6,4},{7,5},{8,10},{9,11},{10,... | collective-permute-start | bytes 393224 | tf_op jit(solution)/shard_map/ppermute | solution.py:600
  97.2 11.3 %collective-permute-start.15 = (bf16[128,256]{1,0:T(8,128)(2,1)S(1)}, bf16[128,256]{1,0:T(8,128)(2,1)S(1)}, u32[]{:S(2)}, u32[]{:S(2)}) collective-permute-start(bf16[128,256]{1,0:T(8,128)(2,1)S(1)} %get-tuple-element.55), channel_id=1, source_target_pairs={{0,8},{4,12},{8,0},{12,4},{16,24},{20,28},{24,16},{28,20},{1,9},{5... | collective-permute-start | bytes 196616 | tf_op jit(solution)/shard_map/ppermute | solution.py:597
  101.2 7.3 %collective-permute-start.16 = (bf16[128,256]{1,0:T(8,128)(2,1)S(1)}, bf16[128,256]{1,0:T(8,128)(2,1)S(1)}, u32[]{:S(2)}, u32[]{:S(2)}) collective-permute-start(bf16[128,256]{1,0:T(8,128)(2,1)S(1)} %get-tuple-element.56), channel_id=1, source_target_pairs={{0,16},{4,20},{8,24},{12,28},{16,0},{20,4},{24,8},{28,12},{1,17},{... | collective-permute-start | bytes 196616 | tf_op jit(solution)/shard_map/ppermute | solution.py:597
  105.1 6.1 %collective-permute-start.17 = (bf16[128,256]{1,0:T(8,128)(2,1)S(1)}, bf16[128,256]{1,0:T(8,128)(2,1)S(1)}, u32[]{:S(2)}, u32[]{:S(2)}) collective-permute-start(bf16[128,256]{1,0:T(8,128)(2,1)S(1)} %get-tuple-element.57), channel_id=1, source_target_pairs={{0,24},{4,28},{8,16},{12,20},{16,8},{20,12},{24,0},{28,4},{1,25},{... | collective-permute-start | bytes 196616 | tf_op jit(solution)/shard_map/ppermute | solution.py:597
  107.2 5.3 %copy-start.5 = (bf16[256,1024]{1,0:T(8,128)(2,1)S(1)}, bf16[256,1024]{1,0:T(8,128)(2,1)}, u32[]{:S(2)}) copy-start(bf16[256,1024]{1,0:T(8,128)(2,1)} %w_ref.1) | copy-start | bytes 1572868
  108.5 12.4 %collective-permute-start.11 = (bf16[512,512]{1,0:T(8,128)(2,1)S(1)}, bf16[512,512]{1,0:T(8,128)(2,1)S(1)}, u32[]{:S(2)}, u32[]{:S(2)}) collective-permute-start(bf16[512,512]{1,0:T(8,128)(2,1)S(1)} %get-tuple-element.51.here_ref), channel_id=1, source_target_pairs={{0,1},{1,0},{2,3},{3,2},{4,5},{5,4},{6,7},{7,6},{8,9},{9,8},{10,11... | collective-permute-start | bytes 1572872 | tf_op jit(solution)/shard_map/ppermute | solution.py:600
  111.2 4.3 %collective-permute-start.18 = (bf16[128,256]{1,0:T(8,128)(2,1)S(1)}, bf16[128,256]{1,0:T(8,128)(2,1)S(1)}, u32[]{:S(2)}, u32[]{:S(2)}) collective-permute-start(bf16[128,256]{1,0:T(8,128)(2,1)S(1)} %add_convert_fusion), channel_id=1, source_target_pairs={{0,4},{4,0},{8,12},{12,8},{16,20},{20,16},{24,28},{28,24},{1,5},{5... | collective-permute-start | bytes 196616 | tf_op jit(solution)/shard_map/ppermute | solution.py:597
  112.6 4.3 %collective-permute-start.12 = (bf16[256,256]{1,0:T(8,128)(2,1)S(1)}, bf16[256,256]{1,0:T(8,128)(2,1)S(1)}, u32[]{:S(2)}, u32[]{:S(2)}) collective-permute-start(bf16[256,256]{1,0:T(8,128)(2,1)S(1)} %get-tuple-element.62), channel_id=1, source_target_pairs={{0,1},{1,0},{2,3},{3,2},{4,5},{5,4},{6,7},{7,6},{8,9},{9,8},{10,11... | collective-permute-start | bytes 393224 | tf_op jit(solution)/shard_map/ppermute | solution.py:600
  112.7 6.4 %collective-permute-start.13 = (bf16[256,256]{1,0:T(8,128)(2,1)S(1)}, bf16[256,256]{1,0:T(8,128)(2,1)S(1)}, u32[]{:S(2)}, u32[]{:S(2)}) collective-permute-start(bf16[256,256]{1,0:T(8,128)(2,1)S(1)} %get-tuple-element.64), channel_id=1, source_target_pairs={{0,2},{1,3},{2,0},{3,1},{4,6},{5,7},{6,4},{7,5},{8,10},{9,11},{10,... | collective-permute-start | bytes 393224 | tf_op jit(solution)/shard_map/ppermute | solution.py:600
  114.3 6.7 %collective-permute-start.14 = (bf16[256,256]{1,0:T(8,128)(2,1)S(1)}, bf16[256,256]{1,0:T(8,128)(2,1)S(1)}, u32[]{:S(2)}, u32[]{:S(2)}) collective-permute-start(bf16[256,256]{1,0:T(8,128)(2,1)S(1)} %get-tuple-element.61), channel_id=1, source_target_pairs={{0,3},{1,2},{2,1},{3,0},{4,7},{5,6},{6,5},{7,4},{8,11},{9,10},{10,... | collective-permute-start | bytes 393224 | tf_op jit(solution)/shard_map/ppermute | solution.py:600
  115.6 6.6 %collective-permute-start.19 = (bf16[2,128,256]{2,1,0:T(8,128)(2,1)S(1)}, bf16[2,128,256]{2,1,0:T(8,128)(2,1)S(1)}, u32[]{:S(2)}, u32[]{:S(2)}) collective-permute-start(bf16[2,128,256]{2,1,0:T(8,128)(2,1)S(1)} %pad_maximum_fusion.1.refs_0_), channel_id=1, source_target_pairs={{0,8},{4,12},{8,0},{12,4},{16,24},{20,28},{24,16},{28,20},{1,9},{5... | collective-permute-start | bytes 393224 | tf_op jit(solution)/shard_map/ppermute | solution.py:597
  116.9 11.9 %collective-permute-start.20 = (bf16[2,128,256]{2,1,0:T(8,128)(2,1)S(1)}, bf16[2,128,256]{2,1,0:T(8,128)(2,1)S(1)}, u32[]{:S(2)}, u32[]{:S(2)}) collective-permute-start(bf16[2,128,256]{2,1,0:T(8,128)(2,1)S(1)} %pad_maximum_fusion.1.refs_0_), channel_id=1, source_target_pairs={{0,16},{4,20},{8,24},{12,28},{16,0},{20,4},{24,8},{28,12},{1,17},{... | collective-permute-start | bytes 393224 | tf_op jit(solution)/shard_map/ppermute | solution.py:597
  119.0 9.7 %collective-permute-start.21 = (bf16[2,128,256]{2,1,0:T(8,128)(2,1)S(1)}, bf16[2,128,256]{2,1,0:T(8,128)(2,1)S(1)}, u32[]{:S(2)}, u32[]{:S(2)}) collective-permute-start(bf16[2,128,256]{2,1,0:T(8,128)(2,1)S(1)} %pad_maximum_fusion.1.refs_0_), channel_id=1, source_target_pairs={{0,24},{4,28},{8,16},{12,20},{16,8},{20,12},{24,0},{28,4},{1,25},{... | collective-permute-start | bytes 393224 | tf_op jit(solution)/shard_map/ppermute | solution.py:597

commit v3 on v2

--- a/solution.py
+++ b/solution.py
@@ -201,20 +201,21 @@
 
 
 def tails_kernel(left_ref, right_ref, after_ref, out_ref):
-    n = out_ref.shape[0] // 2
-    out_ref[:n] = left_ref[left_ref.shape[0] - n :]
-    out_ref[n:] = right_ref[right_ref.shape[0] - n :]
+    out_ref[0] = left_ref[...]
+    out_ref[1] = right_ref[...]
 
 
 def tails(left, right, count, after):
-    vm = pl.BlockSpec(memory_space=pltpu.VMEM)
+    width = left.shape[1]
+    last = pl.BlockSpec((count, width), lambda i: (left.shape[0] // count - 1, 0))
     return pl.pallas_call(
         tails_kernel,
-        in_specs=[vm, vm, pl.BlockSpec(memory_space=pl.ANY)],
-        out_specs=vm,
-        out_shape=jax.ShapeDtypeStruct((2 * count, left.shape[1]), BF),
-        compiler_params=params(),
-        cost_estimate=cost(0, 8 * count * left.shape[1]),
+        grid=(1,),
+        in_specs=[last, last, pl.BlockSpec(memory_space=pl.ANY)],
+        out_specs=pl.BlockSpec((2, count, width), lambda i: (0, 0, 0)),
+        out_shape=jax.ShapeDtypeStruct((2, count, width), BF),
+        compiler_params=params("arbitrary"),
+        cost_estimate=cost(0, 8 * count * width),
     )(left, right, after)
 
 
@@ -542,29 +543,28 @@
 
 def spread_kernel(groups, place_ref, *refs):
     held, out_ref, buf = refs[:groups], refs[-2], refs[-1]
-    _, rows, step = held[0].shape
+    step = held[0].shape[2]
+    y = pl.program_id(0) ^ place_ref[0]
     for d, ref in enumerate(held):
-        buf[d] = ref[...].astype(F32)
-    for y in range(2):
-        for g in range(groups):
-            out_ref[y * rows : (y + 1) * rows, g * step : (g + 1) * step] = buf[
-                g ^ place_ref[2], y ^ place_ref[0]
-            ]
+        buf[d] = ref[y].astype(F32)
+    for g in range(groups):
+        out_ref[:, g * step : (g + 1) * step] = buf[g ^ place_ref[2]]
 
 
 def spread(place, held, *after):
     groups = len(held)
     _, rows, step = held[0].shape
-    vm = pl.BlockSpec(memory_space=pltpu.VMEM)
+    whole = pl.BlockSpec(held[0].shape, lambda i: (0, 0, 0))
     return pl.pallas_call(
         functools.partial(spread_kernel, groups),
+        grid=(2,),
         in_specs=[pl.BlockSpec(memory_space=pltpu.SMEM)]
-        + [vm] * groups
+        + [whole] * groups
         + [pl.BlockSpec(memory_space=pl.ANY)] * len(after),
-        out_specs=vm,
+        out_specs=pl.BlockSpec((rows, groups * step), lambda i: (i, 0)),
         out_shape=jax.ShapeDtypeStruct((2 * rows, groups * step), F32),
-        scratch_shapes=[pltpu.VMEM((groups, 2, rows, step), F32)],
-        compiler_params=params(),
+        scratch_shapes=[pltpu.VMEM((groups, rows, step), F32)],
+        compiler_params=params("arbitrary"),
         cost_estimate=cost(0, 2 * groups * rows * step * 6),
     )(place, *held, *after)
 
@@ -658,7 +658,7 @@
         if s == slots - 1:
             count = band.shape[0]
             ends = tails(qg_left, qg_right, count, kvs[-1])
-            halo_limits = limits((ends[:count], ends[count:]), -blocks, 2 * blocks)
+            halo_limits = limits(ends, -blocks, 2 * blocks)
             far = attend(
                 place, range(slots), 2, rows, halo_limits, qg_left, qg_right, kvs, True
             )

time: 133 us -> 133 us (level); the launches traced: 130 us -> 135 us
  Pallas kernels: 41.5 us -> 51.9 us
  starting transfers between devices: 48.1 us -> 39.4 us
  waiting for transfers between devices: 33.3 us -> 35.6 us
    pallas_call x3, Pallas kernels: 19.6 us -> 30.4 us  [attend(): pl.pallas_call(functools.partial(attend_kernel, slots, tiles, by_exchange...]
    ppermute x11, starting transfers between devices: 24.7 us -> 15.7 us  [swap(): return lax.ppermute(x, 'tm', [(i, i ^ d) for i in range(shards)])]
    all_to_all x2, waiting for transfers between devices: 6.24 us -> 2.94 us  [on_device(): lax.all_to_all(sent[s].reshape(shards, 2 * piece, 2 * HDIM), 'tm', 0, 0)]
    ppermute x1, waiting for transfers between devices: 0.01 us -> 3.21 us  [swap_both(): lax.ppermute(x, ('tm', 'clip'), [(i, i ^ clips + d) for i in range(n)])]
    ppermute x11, waiting for transfers between devices: 18 us -> 20 us  [swap(): return lax.ppermute(x, 'tm', [(i, i ^ d) for i in range(shards)])]
  transfers between devices with their start and end apart: 24 -> 24, of which waited for: 11 -> 12; matrix products, arithmetic and copies ran while one was open for 1% -> 1% of each run, Pallas kernels for 27% -> 34%
where the time goes in v3:
time: 133 us; the launch traced here: 135 us
  Pallas kernels  51.9 us (39%)
  starting transfers between devices  39.4 us (30%)
  waiting for transfers between devices  35.6 us (27%)
  local copies, waits for them, and re-layouts  5.27 us (4%)
  other arithmetic  1.33 us (1%)
    pallas_call x3, Pallas kernels, attend(): pl.pallas_call(functools.partial(attend_kernel, slots, tiles, by_exchange...  30.4 us
    ppermute x11, waiting for transfers between devices, swap(): return lax.ppermute(x, 'tm', [(i, i ^ d) for i in range(shards)])  20 us
    ppermute x11, starting transfers between devices, swap(): return lax.ppermute(x, 'tm', [(i, i ^ d) for i in range(shards)])  15.7 us
    all_to_all x2, starting transfers between devices, on_device(): lax.all_to_all(sent[s].reshape(shards, 2 * piece, 2 * HDIM), 'tm', 0, 0)  11.3 us
    ppermute x7, waiting for transfers between devices, swap_clip(): return lax.ppermute(x, 'clip', [(i, i ^ d) for i in range(clips)])  9.49 us
    pallas_call x2, Pallas kernels, put_in_order(): pl.pallas_call(order_kernel, grid=(2,), in_specs=[pl.BlockSpec((1, 1, row...  6.74 us
    unnamed x44, local copies, waits for them, and re-layouts  5.18 us
    ppermute x1, starting transfers between devices, up(): return lax.ppermute(x, 'tm', [(i, i + 2) for i in range(shards - 2)])  4.64 us
  transfers between devices with their start and end apart: 24, of which 12 were waited for; matrix products, arithmetic and copies ran while one was open for 1% of the time, Pallas kernels for 34%

profile of v3, /device:TPU:0, one launch (start us, length us, event | category | flops | bytes accessed | tf_op | source)
XLA Modules:
  0.0 134.5 jit_solution(14068259941166701312)
XLA Ops:
  0.6 1.2 copy-done
  1.9 1.2 copy-done.2
  3.1 1.8 %shard_map.104 = bf16[4,2,512,128]{3,2,1,0:T(8,128)(2,1)} custom-call(bf16[2048,256]{1,0:T(8,128)(2,1)S(1)} %copy-done, bf16[2048,256]{1,0:T(8,128)(2,1)S(1)} %copy-done.2), custom_call_target="tpu_custom_call" | custom-call | bytes 3145728 | tf_op jit(solution)/shard_map/pallas_call | solution.py:48
  4.9 7.4 %all-to-all-start = ((bf16[8,512,128]{2,1,0:T(8,128)(2,1)}), bf16[8,512,128]{2,1,0:T(8,128)(2,1)}, u32[]{:S(2)}, u32[]{:S(2)}) async-start(bf16[8,512,128]{2,1,0:T(8,128)(2,1)} %bitcast.8), calls=%async_computation | async-start | bytes 2097152 | tf_op jit(solution)/shard_map/all_to_all | solution.py:653
  12.4 1.6 %collective-permute-start = (bf16[512,256]{1,0:T(8,128)(2,1)S(1)}, bf16[512,256]{1,0:T(8,128)(2,1)S(1)}, u32[]{:S(2)}, u32[]{:S(2)}) collective-permute-start(bf16[512,256]{1,0:T(8,128)(2,1)S(1)} %copy-done.19), channel_id=1, source_target_pairs={{0,2},{1,3},{2,0},{3,1},{4,6},{5,7},{6,4},{7,5},{8,10},{9,11},{10,... | collective-permute-start | bytes 786440 | tf_op jit(solution)/shard_map/ppermute | solution.py:600
  13.9 6.3 %collective-permute-done = bf16[512,256]{1,0:T(8,128)(2,1)S(1)} collective-permute-done((bf16[512,256]{1,0:T(8,128)(2,1)S(1)}, bf16[512,256]{1,0:T(8,128)(2,1)S(1)}, u32[]{:S(2)}, u32[]{:S(2)}) %collective-permute-start) | collective-permute-done | bytes 262176 | tf_op jit(solution)/shard_map/ppermute | solution.py:600
  20.5 1.8 %collective-permute-done.1.there_ref = bf16[2,512,256]{2,1,0:T(8,128)(2,1)S(1)} collective-permute-done((bf16[2,512,256]{2,1,0:T(8,128)(2,1)S(1)}, bf16[2,512,256]{2,1,0:T(8,128)(2,1)S(1)}, u32[]{:S(2)}, u32[]{:S(2)}) %collective-permute-start.1) | collective-permute-done | bytes 524320 | tf_op jit(solution)/shard_map/ppermute | solution.py:600
  22.2 1.0 copy-done.4
  23.3 1.1 shard_map.103
  24.4 0.7 copy-done.6
  25.1 1.7 %collective-permute-start.2 = (bf16[528,256]{1,0:T(8,128)(2,1)S(1)}, bf16[528,256]{1,0:T(8,128)(2,1)S(1)}, u32[]{:S(2)}, u32[]{:S(2)}) collective-permute-start(bf16[528,256]{1,0:T(8,128)(2,1)S(1)} %get-tuple-element.32), channel_id=1, source_target_pairs={{0,4},{4,0},{8,12},{12,8},{16,20},{20,16},{24,28},{28,24},{1,5},{5... | collective-permute-start | bytes 811016 | tf_op jit(solution)/shard_map/ppermute | solution.py:597
  26.8 1.8 %shard_map.108.x_ref = bf16[4,2,512,128]{3,2,1,0:T(8,128)(2,1)} custom-call(bf16[2048,256]{1,0:T(8,128)(2,1)S(1)} %copy-done.1, bf16[2048,256]{1,0:T(8,128)(2,1)S(1)} %copy-done.3), custom_call_target="tpu_custom_call" | custom-call | bytes 3145728 | tf_op jit(solution)/shard_map/pallas_call | solution.py:48
  28.6 7.5 %collective-permute-done.2.after_ref.peer_ref = bf16[528,256]{1,0:T(8,128)(2,1)S(1)} collective-permute-done((bf16[528,256]{1,0:T(8,128)(2,1)S(1)}, bf16[528,256]{1,0:T(8,128)(2,1)S(1)}, u32[]{:S(2)}, u32[]{:S(2)}) %collective-permute-start.2) | collective-permute-done | bytes 270368 | tf_op jit(solution)/shard_map/ppermute | solution.py:597
  36.1 2.1 %all-to-all-done.arr_ref = bf16[8,512,128]{2,1,0:T(8,128)(2,1)} async-done(((bf16[8,512,128]{2,1,0:T(8,128)(2,1)}), bf16[8,512,128]{2,1,0:T(8,128)(2,1)}, u32[]{:S(2)}, u32[]{:S(2)}) %all-to-all-start) | async-done | bytes 1048608 | tf_op jit(solution)/shard_map/all_to_all | solution.py:653
  38.2 3.9 %all-to-all-start.1 = ((bf16[8,512,128]{2,1,0:T(8,128)(2,1)}), bf16[8,512,128]{2,1,0:T(8,128)(2,1)S(1)}, u32[]{:S(2)}, u32[]{:S(2)}) async-start(bf16[8,512,128]{2,1,0:T(8,128)(2,1)} %bitcast.9), calls=%async_computation.1 | async-start | bytes 2097152 | tf_op jit(solution)/shard_map/all_to_all | solution.py:653
  42.1 0.7 fusion.2
  43.1 3.9 %shard_map.105 = (bf16[4096,128]{1,0:T(8,128)(2,1)S(1)}, bf16[128,4096]{1,0:T(8,128)(2,1)S(1)}) custom-call(s32[2,1,2048]{2,1,0:T(1,128)S(1)} %bitcast.18, bf16[8,512,128]{2,1,0:T(8,128)(2,1)} %all-to-all-done.arr_ref), custom_call_target="tpu_custom_call" | custom-call | flops 2147483648 | bytes 3145728 | tf_op jit(solution)/shard_map/pallas_call | solution.py:94
  47.0 1.5 %shard_map.111 = (bf16[528,256]{1,0:T(8,128)(2,1)}, bf16[528,256]{1,0:T(8,128)(2,1)}) custom-call(s32[3]{0:T(128)S(1)} %pad_add_fusion.2.place_ref, bf16[528,256]{1,0:T(8,128)(2,1)S(1)} %copy-done.7, bf16[528,256]{1,0:T(8,128)(2,1)S(1)} %collective-permute-done.2.after_ref.peer_ref, bf16[4096,128]{1,0:T(8,128)(2,1)S(1)} %get-tuple-element.33.refs_0_.after_ref), custom_call_target="tpu_custom_call" | custom-call | bytes 1081344 | tf_op jit(solution)/shard_map/pallas_call | solution.py:188
  48.5 4.6 %collective-permute-start.4 = (bf16[528,256]{1,0:T(8,128)(2,1)}, bf16[528,256]{1,0:T(8,128)(2,1)}, u32[]{:S(2)}, u32[]{:S(2)}) collective-permute-start(bf16[528,256]{1,0:T(8,128)(2,1)} %get-tuple-element.39), channel_id=1, source_target_pairs={{0,8},{4,12},{8,16},{12,20},{16,24},{20,28},{1,9},{5,13},{9,17},{1... | collective-permute-start | bytes 811016 | tf_op jit(solution)/shard_map/ppermute | solution.py:607
  53.1 1.3 collective-permute-start.5
  54.4 11.1 %shard_map.106 = (bf16[208,512]{1,0:T(8,128)(2,1)S(1)}, bf16[208,512]{1,0:T(8,128)(2,1)S(1)}) custom-call(s32[3]{0:T(128)S(1)} %pad_add_fusion.2.place_ref, s32[2,32]{1,0:T(2,128)S(1)} %pad_add_fusion.lohi_ref, bf16[528,256]{1,0:T(8,128)(2,1)S(1)} %get-tuple-element.59.qga_ref, bf16[528,256]{1,0:T(8,128)(2,1)S(1)} %get-tuple-element.60.qgb_ref, ...), custom_call_target="tpu_custom_call" | custom-call | flops 2147483648 | bytes 4194304 | tf_op jit(solution)/shard_map/pallas_call | solution.py:377
  65.6 0.7 copy-done.15
  66.2 0.7 shard_map.107.cot_ref
  66.9 1.5 %collective-permute-start.3 = (bf16[512,1024]{1,0:T(8,128)(2,1)S(1)}, bf16[512,1024]{1,0:T(8,128)(2,1)}, u32[]{:S(2)}, u32[]{:S(2)}) collective-permute-start(bf16[512,1024]{1,0:T(8,128)(2,1)S(1)} %shard_map.107.cot_ref), channel_id=1, source_target_pairs={{0,4},{4,0},{8,12},{12,8},{16,20},{20,16},{24,28},{28,24},{1,5},{5... | collective-permute-start | bytes 3145736 | tf_op jit(solution)/shard_map/ppermute | solution.py:597
  68.4 0.9 all-to-all-done.1.arr_ref
  69.3 2.9 %shard_map.110 = (bf16[4096,128]{1,0:T(8,128)(2,1)S(1)}, bf16[128,4096]{1,0:T(8,128)(2,1)S(1)}) custom-call(s32[2,1,2048]{2,1,0:T(1,128)S(1)} %bitcast.19, bf16[8,512,128]{2,1,0:T(8,128)(2,1)S(1)} %all-to-all-done.1.arr_ref, bf16[208,512]{1,0:T(8,128)(2,1)S(1)} %get-tuple-element.35.after_ref.refs_0_), custom_call_target="tpu_custom_call" | custom-call | flops 2147483648 | bytes 3145728 | tf_op jit(solution)/shard_map/pallas_call | solution.py:94
  72.2 0.8 shard_map.112
  73.5 8.2 %shard_map.113 = (bf16[416,512]{1,0:T(8,128)(2,1)S(1)}, bf16[416,512]{1,0:T(8,128)(2,1)S(1)}) custom-call(s32[3]{0:T(128)S(1)} %pad_add_fusion.2.place_ref, s32[2,32]{1,0:T(2,128)S(1)} %pad_add_fusion.1.lohi_ref, bf16[528,256]{1,0:T(8,128)(2,1)} %collective-permute-done.4.left_ref.qga_ref, bf16[528,256]{1,0:T(8,128)(2,1)} %collective-permute-done.5.right_ref.qgb_ref, ...), custom_call_target="tpu_custom_call" | custom-call | flops 4294967296 | bytes 8388608 | tf_op jit(solution)/shard_map/pallas_call | solution.py:377
  81.7 6.0 %collective-permute-start.6 = (bf16[416,512]{1,0:T(8,128)(2,1)S(1)}, bf16[416,512]{1,0:T(8,128)(2,1)S(1)}, u32[]{:S(2)}, u32[]{:S(2)}) collective-permute-start(bf16[416,512]{1,0:T(8,128)(2,1)S(1)} %get-tuple-element.41.refs_2_), channel_id=1, source_target_pairs={{0,8},{4,12},{8,0},{12,4},{16,24},{20,28},{24,16},{28,20},{1,9},{5... | collective-permute-start | bytes 1277960 | tf_op jit(solution)/shard_map/ppermute | solution.py:597
  87.7 0.8 collective-permute-start.7
  88.5 11.1 %shard_map.114 = (bf16[208,512]{1,0:T(8,128)(2,1)S(1)}, bf16[208,512]{1,0:T(8,128)(2,1)S(1)}) custom-call(s32[3]{0:T(128)S(1)} %pad_add_fusion.2.place_ref, s32[2,32]{1,0:T(2,128)S(1)} %pad_add_fusion.lohi_ref, bf16[528,256]{1,0:T(8,128)(2,1)S(1)} %copy-done.11, bf16[528,256]{1,0:T(8,128)(2,1)S(1)} %copy-done.13, ...), custom_call_target="tpu_custom_call" | custom-call | flops 2147483648 | bytes 4194304 | tf_op jit(solution)/shard_map/pallas_call | solution.py:377
  99.7 2.2 %shard_map.115 = (bf16[256,512]{1,0:T(8,128)(2,1)S(1)}, bf16[256,512]{1,0:T(8,128)(2,1)S(1)}, bf16[128,256]{1,0:T(8,128)(2,1)S(1)}, bf16[128,256]{1,0:T(8,128)(2...) custom-call(s32[3]{0:T(128)S(1)} %pad_add_fusion.2.place_ref, ...), custom_call_target="tpu_custom_call" | custom-call | flops 268435456 | bytes 8388608 | tf_op jit(solution)/shard_map/pallas_call | solution.py:444
  101.9 0.7 shard_map.116
  102.7 1.4 %collective-permute-start.8 = (bf16[512,256]{1,0:T(8,128)(2,1)S(1)}, bf16[512,256]{1,0:T(8,128)(2,1)S(1)}, u32[]{:S(2)}, u32[]{:S(2)}) collective-permute-start(bf16[512,256]{1,0:T(8,128)(2,1)S(1)} %get-tuple-element.48), channel_id=1, source_target_pairs={{0,4},{4,0},{8,12},{12,8},{16,20},{20,16},{24,28},{28,24},{1,5},{5... | collective-permute-start | bytes 786440 | tf_op jit(solution)/shard_map/ppermute | solution.py:597
  104.1 1.6 %collective-permute-start.10 = (bf16[512,128]{1,0:T(8,128)(2,1)S(1)}, bf16[512,128]{1,0:T(8,128)(2,1)S(1)}, u32[]{:S(2)}, u32[]{:S(2)}) collective-permute-start(bf16[512,128]{1,0:T(8,128)(2,1)S(1)} %get-tuple-element.50), channel_id=1, source_target_pairs={{0,6},{1,7},{2,4},{3,5},{4,2},{5,3},{6,0},{7,1},{8,14},{9,15},{10,... | collective-permute-start | bytes 393224 | tf_op jit(solution)/shard_map/ppermute | solution.py:604
  106.2 0.6 collective-permute-start.15
  107.2 3.2 %collective-permute-done.10.xpeer_ref = bf16[512,128]{1,0:T(8,128)(2,1)S(1)} collective-permute-done((bf16[512,128]{1,0:T(8,128)(2,1)S(1)}, bf16[512,128]{1,0:T(8,128)(2,1)S(1)}, u32[]{:S(2)}, u32[]{:S(2)}) %collective-permute-start.10) | collective-permute-done | bytes 131104 | tf_op jit(solution)/shard_map/ppermute | solution.py:604
  110.9 1.3 collective-permute-done.8.peer_ref
  112.3 1.3 shard_map.117
  113.6 3.0 %collective-permute-done.17 = bf16[128,256]{1,0:T(8,128)(2,1)S(1)} collective-permute-done((bf16[128,256]{1,0:T(8,128)(2,1)S(1)}, bf16[128,256]{1,0:T(8,128)(2,1)S(1)}, u32[]{:S(2)}, u32[]{:S(2)}) %collective-permute-start.17) | collective-permute-done | bytes 65568 | tf_op jit(solution)/shard_map/ppermute | solution.py:597
  117.2 1.6 %collective-permute-start.13 = (bf16[256,256]{1,0:T(8,128)(2,1)S(1)}, bf16[256,256]{1,0:T(8,128)(2,1)S(1)}, u32[]{:S(2)}, u32[]{:S(2)}) collective-permute-start(bf16[256,256]{1,0:T(8,128)(2,1)S(1)} %get-tuple-element.64), channel_id=1, source_target_pairs={{0,2},{1,3},{2,0},{3,1},{4,6},{5,7},{6,4},{7,5},{8,10},{9,11},{10,... | collective-permute-start | bytes 393224 | tf_op jit(solution)/shard_map/ppermute | solution.py:600
  119.0 1.9 %collective-permute-done.18 = bf16[128,256]{1,0:T(8,128)(2,1)S(1)} collective-permute-done((bf16[128,256]{1,0:T(8,128)(2,1)S(1)}, bf16[128,256]{1,0:T(8,128)(2,1)S(1)}, u32[]{:S(2)}, u32[]{:S(2)}) %collective-permute-start.18) | collective-permute-done | bytes 65568 | tf_op jit(solution)/shard_map/ppermute | solution.py:597
  121.0 1.1 collective-permute-start.20
  122.1 1.4 %collective-permute-done.13.refs_2_ = bf16[256,256]{1,0:T(8,128)(2,1)S(1)} collective-permute-done((bf16[256,256]{1,0:T(8,128)(2,1)S(1)}, bf16[256,256]{1,0:T(8,128)(2,1)S(1)}, u32[]{:S(2)}, u32[]{:S(2)}) %collective-permute-start.13) | collective-permute-done | bytes 131104 | tf_op jit(solution)/shard_map/ppermute | solution.py:600
  123.5 1.8 %collective-permute-start.21 = (bf16[2,128,256]{2,1,0:T(8,128)(2,1)S(1)}, bf16[2,128,256]{2,1,0:T(8,128)(2,1)S(1)}, u32[]{:S(2)}, u32[]{:S(2)}) collective-permute-start(bf16[2,128,256]{2,1,0:T(8,128)(2,1)S(1)} %pad_maximum_fusion.1.refs_0_), channel_id=1, source_target_pairs={{0,24},{4,28},{8,16},{12,20},{16,8},{20,12},{24,0},{28,4},{1,25},{... | collective-permute-start | bytes 393224 | tf_op jit(solution)/shard_map/ppermute | solution.py:597
  125.4 1.2 shard_map.118
  126.6 6.3 %collective-permute-done.20.refs_2_ = bf16[2,128,256]{2,1,0:T(8,128)(2,1)S(1)} collective-permute-done((bf16[2,128,256]{2,1,0:T(8,128)(2,1)S(1)}, bf16[2,128,256]{2,1,0:T(8,128)(2,1)S(1)}, u32[]{:S(2)}, u32[]{:S(2)}) %collective-permute-start.20) | collective-permute-done | bytes 131104 | tf_op jit(solution)/shard_map/ppermute | solution.py:597
  132.9 1.6 %shard_map.119 = f32[256,1024]{1,0:T(8,128)} custom-call(s32[3]{0:T(128)S(1)} %pad_add_fusion.2.place_ref, bf16[2,128,256]{2,1,0:T(8,128)(2,1)S(1)} %pad_maximum_fusion.1.refs_0_, bf16[2,128,256]{2,1,0:T(8,128)(2,1)S(1)} %collective-permute-done.19.refs_1_, bf16[2,128,256]{2,1,0:T(8,128)(2,1)S(1)} %collective-permute-done.20.refs_2_, ...), custom_call_target="tpu_custom_call" | custom-call | bytes 1572864 | tf_op jit(solution)/shard_map/pallas_call | solution.py:558
  (83 shorter events, 3.5 us)
Async XLA Ops:
  0.6 1.2 copy-start
  1.9 1.2 copy-start.2
  4.9 7.4 %copy-start.19 = (bf16[512,256]{1,0:T(8,128)(2,1)S(1)}, bf16[512,256]{1,0:T(8,128)(2,1)}, u32[]{:S(2)}) copy-start(bf16[512,256]{1,0:T(8,128)(2,1)} %param.15) | copy-start | bytes 786436
  4.9 15.5 %copy-start.20 = (s32[16]{0:T(128)S(1)}, s32[16]{0:T(128)}, u32[]{:S(2)}) copy-start(s32[16]{0:T(128)} %param.13) | copy-start | bytes 196
  4.9 15.5 %copy-start.21 = (s32[16]{0:T(128)S(1)}, s32[16]{0:T(128)}, u32[]{:S(2)}) copy-start(s32[16]{0:T(128)} %param.12) | copy-start | bytes 196
  4.9 17.3 %copy-start.14 = (bf16[512,256]{1,0:T(8,128)(2,1)S(1)}, bf16[512,256]{1,0:T(8,128)(2,1)}, u32[]{:S(2)}) copy-start(bf16[512,256]{1,0:T(8,128)(2,1)} %q_ref.1) | copy-start | bytes 786436
  4.9 33.3 %all-to-all-start = ((bf16[8,512,128]{2,1,0:T(8,128)(2,1)}), bf16[8,512,128]{2,1,0:T(8,128)(2,1)}, u32[]{:S(2)}, u32[]{:S(2)}) async-start(bf16[8,512,128]{2,1,0:T(8,128)(2,1)} %bitcast.8), calls=%async_computation | async-start | bytes 2097152 | tf_op jit(solution)/shard_map/all_to_all | solution.py:653
  12.4 7.8 %collective-permute-start = (bf16[512,256]{1,0:T(8,128)(2,1)S(1)}, bf16[512,256]{1,0:T(8,128)(2,1)S(1)}, u32[]{:S(2)}, u32[]{:S(2)}) collective-permute-start(bf16[512,256]{1,0:T(8,128)(2,1)S(1)} %copy-done.19), channel_id=1, source_target_pairs={{0,2},{1,3},{2,0},{3,1},{4,6},{5,7},{6,4},{7,5},{8,10},{9,11},{10,... | collective-permute-start | bytes 786440 | tf_op jit(solution)/shard_map/ppermute | solution.py:600
  20.2 6.6 %copy-start.3 = (bf16[2048,256]{1,0:T(8,128)(2,1)S(1)}, bf16[2048,256]{1,0:T(8,128)(2,1)}, u32[]{:S(2)}) copy-start(bf16[2048,256]{1,0:T(8,128)(2,1)} %v_ref.3) | copy-start | bytes 3145732
  20.2 6.5 %copy-start.1 = (bf16[2048,256]{1,0:T(8,128)(2,1)S(1)}, bf16[2048,256]{1,0:T(8,128)(2,1)}, u32[]{:S(2)}) copy-start(bf16[2048,256]{1,0:T(8,128)(2,1)} %k_ref.3) | copy-start | bytes 3145732
  20.2 2.0 %collective-permute-start.1 = (bf16[2,512,256]{2,1,0:T(8,128)(2,1)S(1)}, bf16[2,512,256]{2,1,0:T(8,128)(2,1)S(1)}, u32[]{:S(2)}, u32[]{:S(2)}) collective-permute-start(bf16[2,512,256]{2,1,0:T(8,128)(2,1)S(1)} %pad_maximum_fusion.here_ref), channel_id=1, source_target_pairs={{0,1},{1,0},{2,3},{3,2},{4,5},{5,4},{6,7},{7,6},{8,9},{9,8},{10,11... | collective-permute-start | bytes 1572872 | tf_op jit(solution)/shard_map/ppermute | solution.py:600
  22.2 1.0 copy-start.4
  24.4 0.7 copy-start.6
  25.1 11.0 %collective-permute-start.2 = (bf16[528,256]{1,0:T(8,128)(2,1)S(1)}, bf16[528,256]{1,0:T(8,128)(2,1)S(1)}, u32[]{:S(2)}, u32[]{:S(2)}) collective-permute-start(bf16[528,256]{1,0:T(8,128)(2,1)S(1)} %get-tuple-element.32), channel_id=1, source_target_pairs={{0,4},{4,0},{8,12},{12,8},{16,20},{20,16},{24,28},{28,24},{1,5},{5... | collective-permute-start | bytes 811016 | tf_op jit(solution)/shard_map/ppermute | solution.py:597
  38.2 4.6 %copy-start.7 = (bf16[528,256]{1,0:T(8,128)(2,1)S(1)}, bf16[528,256]{1,0:T(8,128)(2,1)}, u32[]{:S(2)}) copy-start(bf16[528,256]{1,0:T(8,128)(2,1)} %copy-done.6) | copy-start | bytes 811012
  38.2 31.1 %all-to-all-start.1 = ((bf16[8,512,128]{2,1,0:T(8,128)(2,1)}), bf16[8,512,128]{2,1,0:T(8,128)(2,1)S(1)}, u32[]{:S(2)}, u32[]{:S(2)}) async-start(bf16[8,512,128]{2,1,0:T(8,128)(2,1)} %bitcast.9), calls=%async_computation.1 | async-start | bytes 2097152 | tf_op jit(solution)/shard_map/all_to_all | solution.py:653
  42.9 11.5 %copy-start.10 = (bf16[528,256]{1,0:T(8,128)(2,1)}, bf16[528,256]{1,0:T(8,128)(2,1)S(1)}, u32[]{:S(2)}) copy-start(bf16[528,256]{1,0:T(8,128)(2,1)S(1)} %get-tuple-element.59.qga_ref) | copy-start | bytes 811012
  42.9 11.5 %copy-start.12 = (bf16[528,256]{1,0:T(8,128)(2,1)}, bf16[528,256]{1,0:T(8,128)(2,1)S(1)}, u32[]{:S(2)}) copy-start(bf16[528,256]{1,0:T(8,128)(2,1)S(1)} %get-tuple-element.60.qgb_ref) | copy-start | bytes 811012
  47.0 18.5 %copy-start.8 = (bf16[4096,128]{1,0:T(8,128)(2,1)}, bf16[4096,128]{1,0:T(8,128)(2,1)S(1)}, u32[]{:S(2)}) copy-start(bf16[4096,128]{1,0:T(8,128)(2,1)S(1)} %get-tuple-element.33.refs_0_.after_ref) | copy-start | bytes 3145732
  47.0 18.5 %copy-start.17 = (bf16[128,4096]{1,0:T(8,128)(2,1)}, bf16[128,4096]{1,0:T(8,128)(2,1)S(1)}, u32[]{:S(2)}) copy-start(bf16[128,4096]{1,0:T(8,128)(2,1)S(1)} %get-tuple-element.34.refs_1_) | copy-start | bytes 3145732
  48.5 23.7 %collective-permute-start.4 = (bf16[528,256]{1,0:T(8,128)(2,1)}, bf16[528,256]{1,0:T(8,128)(2,1)}, u32[]{:S(2)}, u32[]{:S(2)}) collective-permute-start(bf16[528,256]{1,0:T(8,128)(2,1)} %get-tuple-element.39), channel_id=1, source_target_pairs={{0,8},{4,12},{8,16},{12,20},{16,24},{20,28},{1,9},{5,13},{9,17},{1... | collective-permute-start | bytes 811016 | tf_op jit(solution)/shard_map/ppermute | solution.py:607
  53.1 19.1 %collective-permute-start.5 = (bf16[528,256]{1,0:T(8,128)(2,1)}, bf16[528,256]{1,0:T(8,128)(2,1)}, u32[]{:S(2)}, u32[]{:S(2)}) collective-permute-start(bf16[528,256]{1,0:T(8,128)(2,1)} %get-tuple-element.40), channel_id=1, source_target_pairs={{8,0},{12,4},{16,8},{20,12},{24,16},{28,20},{9,1},{13,5},{17,9},{2... | collective-permute-start | bytes 811016 | tf_op jit(solution)/shard_map/ppermute | solution.py:610
  65.6 0.7 copy-start.15
  66.9 32.7 %collective-permute-start.3 = (bf16[512,1024]{1,0:T(8,128)(2,1)S(1)}, bf16[512,1024]{1,0:T(8,128)(2,1)}, u32[]{:S(2)}, u32[]{:S(2)}) collective-permute-start(bf16[512,1024]{1,0:T(8,128)(2,1)S(1)} %shard_map.107.cot_ref), channel_id=1, source_target_pairs={{0,4},{4,0},{8,12},{12,8},{16,20},{20,16},{24,28},{28,24},{1,5},{5... | collective-permute-start | bytes 3145736 | tf_op jit(solution)/shard_map/ppermute | solution.py:597
  69.3 3.9 %copy-start.18 = (bf16[128,4096]{1,0:T(8,128)(2,1)S(1)}, bf16[128,4096]{1,0:T(8,128)(2,1)}, u32[]{:S(2)}) copy-start(bf16[128,4096]{1,0:T(8,128)(2,1)} %copy-done.17) | copy-start | bytes 3145732
  72.2 1.3 copy-start.9
  73.5 15.1 %copy-start.11 = (bf16[528,256]{1,0:T(8,128)(2,1)S(1)}, bf16[528,256]{1,0:T(8,128)(2,1)}, u32[]{:S(2)}) copy-start(bf16[528,256]{1,0:T(8,128)(2,1)} %copy-done.10) | copy-start | bytes 811012
  73.5 15.1 %copy-start.13 = (bf16[528,256]{1,0:T(8,128)(2,1)S(1)}, bf16[528,256]{1,0:T(8,128)(2,1)}, u32[]{:S(2)}) copy-start(bf16[528,256]{1,0:T(8,128)(2,1)} %copy-done.12) | copy-start | bytes 811012
  81.7 18.0 %collective-permute-start.6 = (bf16[416,512]{1,0:T(8,128)(2,1)S(1)}, bf16[416,512]{1,0:T(8,128)(2,1)S(1)}, u32[]{:S(2)}, u32[]{:S(2)}) collective-permute-start(bf16[416,512]{1,0:T(8,128)(2,1)S(1)} %get-tuple-element.41.refs_2_), channel_id=1, source_target_pairs={{0,8},{4,12},{8,0},{12,4},{16,24},{20,28},{24,16},{28,20},{1,9},{5... | collective-permute-start | bytes 1277960 | tf_op jit(solution)/shard_map/ppermute | solution.py:597
  87.7 12.0 %copy-start.16 = (bf16[208,512]{1,0:T(8,128)(2,1)S(1)}, bf16[208,512]{1,0:T(8,128)(2,1)}, u32[]{:S(2)}) copy-start(bf16[208,512]{1,0:T(8,128)(2,1)} %copy-done.15) | copy-start | bytes 638980
  87.7 11.9 %collective-permute-start.7 = (bf16[416,512]{1,0:T(8,128)(2,1)S(1)}, bf16[416,512]{1,0:T(8,128)(2,1)S(1)}, u32[]{:S(2)}, u32[]{:S(2)}) collective-permute-start(bf16[416,512]{1,0:T(8,128)(2,1)S(1)} %get-tuple-element.42.refs_3_), channel_id=1, source_target_pairs={{8,16},{12,20},{16,8},{20,12},{9,17},{13,21},{17,9},{21,13},{10,18... | collective-permute-start | bytes 1277960 | tf_op jit(solution)/shard_map/ppermute | solution.py:673
  102.7 9.6 %collective-permute-start.8 = (bf16[512,256]{1,0:T(8,128)(2,1)S(1)}, bf16[512,256]{1,0:T(8,128)(2,1)S(1)}, u32[]{:S(2)}, u32[]{:S(2)}) collective-permute-start(bf16[512,256]{1,0:T(8,128)(2,1)S(1)} %get-tuple-element.48), channel_id=1, source_target_pairs={{0,4},{4,0},{8,12},{12,8},{16,20},{20,16},{24,28},{28,24},{1,5},{5... | collective-permute-start | bytes 786440 | tf_op jit(solution)/shard_map/ppermute | solution.py:597
  104.1 6.3 %collective-permute-start.10 = (bf16[512,128]{1,0:T(8,128)(2,1)S(1)}, bf16[512,128]{1,0:T(8,128)(2,1)S(1)}, u32[]{:S(2)}, u32[]{:S(2)}) collective-permute-start(bf16[512,128]{1,0:T(8,128)(2,1)S(1)} %get-tuple-element.50), channel_id=1, source_target_pairs={{0,6},{1,7},{2,4},{3,5},{4,2},{5,3},{6,0},{7,1},{8,14},{9,15},{10,... | collective-permute-start | bytes 393224 | tf_op jit(solution)/shard_map/ppermute | solution.py:604
  105.7 5.3 %collective-permute-start.9 = (bf16[512,128]{1,0:T(8,128)(2,1)S(1)}, bf16[512,128]{1,0:T(8,128)(2,1)S(1)}, u32[]{:S(2)}, u32[]{:S(2)}) collective-permute-start(bf16[512,128]{1,0:T(8,128)(2,1)S(1)} %get-tuple-element.49), channel_id=1, source_target_pairs={{0,2},{1,3},{2,0},{3,1},{4,6},{5,7},{6,4},{7,5},{8,10},{9,11},{10,... | collective-permute-start | bytes 393224 | tf_op jit(solution)/shard_map/ppermute | solution.py:600
  106.2 7.3 %collective-permute-start.15 = (bf16[128,256]{1,0:T(8,128)(2,1)S(1)}, bf16[128,256]{1,0:T(8,128)(2,1)S(1)}, u32[]{:S(2)}, u32[]{:S(2)}) collective-permute-start(bf16[128,256]{1,0:T(8,128)(2,1)S(1)} %get-tuple-element.55), channel_id=1, source_target_pairs={{0,8},{4,12},{8,0},{12,4},{16,24},{20,28},{24,16},{28,20},{1,9},{5... | collective-permute-start | bytes 196616 | tf_op jit(solution)/shard_map/ppermute | solution.py:597
  106.8 6.8 %collective-permute-start.16 = (bf16[128,256]{1,0:T(8,128)(2,1)S(1)}, bf16[128,256]{1,0:T(8,128)(2,1)S(1)}, u32[]{:S(2)}, u32[]{:S(2)}) collective-permute-start(bf16[128,256]{1,0:T(8,128)(2,1)S(1)} %get-tuple-element.56), channel_id=1, source_target_pairs={{0,16},{4,20},{8,24},{12,28},{16,0},{20,4},{24,8},{28,12},{1,17},{... | collective-permute-start | bytes 196616 | tf_op jit(solution)/shard_map/ppermute | solution.py:597
  110.5 6.1 %collective-permute-start.17 = (bf16[128,256]{1,0:T(8,128)(2,1)S(1)}, bf16[128,256]{1,0:T(8,128)(2,1)S(1)}, u32[]{:S(2)}, u32[]{:S(2)}) collective-permute-start(bf16[128,256]{1,0:T(8,128)(2,1)S(1)} %get-tuple-element.57), channel_id=1, source_target_pairs={{0,24},{4,28},{8,16},{12,20},{16,8},{20,12},{24,0},{28,4},{1,25},{... | collective-permute-start | bytes 196616 | tf_op jit(solution)/shard_map/ppermute | solution.py:597
  112.3 4.8 %copy-start.5 = (bf16[256,1024]{1,0:T(8,128)(2,1)S(1)}, bf16[256,1024]{1,0:T(8,128)(2,1)}, u32[]{:S(2)}) copy-start(bf16[256,1024]{1,0:T(8,128)(2,1)} %w_ref.1) | copy-start | bytes 1572868
  113.6 11.9 %collective-permute-start.11 = (bf16[512,512]{1,0:T(8,128)(2,1)S(1)}, bf16[512,512]{1,0:T(8,128)(2,1)S(1)}, u32[]{:S(2)}, u32[]{:S(2)}) collective-permute-start(bf16[512,512]{1,0:T(8,128)(2,1)S(1)} %get-tuple-element.51.here_ref), channel_id=1, source_target_pairs={{0,1},{1,0},{2,3},{3,2},{4,5},{5,4},{6,7},{7,6},{8,9},{9,8},{10,11... | collective-permute-start | bytes 1572872 | tf_op jit(solution)/shard_map/ppermute | solution.py:600
  116.6 4.3 %collective-permute-start.18 = (bf16[128,256]{1,0:T(8,128)(2,1)S(1)}, bf16[128,256]{1,0:T(8,128)(2,1)S(1)}, u32[]{:S(2)}, u32[]{:S(2)}) collective-permute-start(bf16[128,256]{1,0:T(8,128)(2,1)S(1)} %add_convert_fusion), channel_id=1, source_target_pairs={{0,4},{4,0},{8,12},{12,8},{16,20},{20,16},{24,28},{28,24},{1,5},{5... | collective-permute-start | bytes 196616 | tf_op jit(solution)/shard_map/ppermute | solution.py:597
  117.1 3.9 %collective-permute-start.12 = (bf16[256,256]{1,0:T(8,128)(2,1)S(1)}, bf16[256,256]{1,0:T(8,128)(2,1)S(1)}, u32[]{:S(2)}, u32[]{:S(2)}) collective-permute-start(bf16[256,256]{1,0:T(8,128)(2,1)S(1)} %get-tuple-element.62), channel_id=1, source_target_pairs={{0,1},{1,0},{2,3},{3,2},{4,5},{5,4},{6,7},{7,6},{8,9},{9,8},{10,11... | collective-permute-start | bytes 393224 | tf_op jit(solution)/shard_map/ppermute | solution.py:600
  117.2 6.4 %collective-permute-start.13 = (bf16[256,256]{1,0:T(8,128)(2,1)S(1)}, bf16[256,256]{1,0:T(8,128)(2,1)S(1)}, u32[]{:S(2)}, u32[]{:S(2)}) collective-permute-start(bf16[256,256]{1,0:T(8,128)(2,1)S(1)} %get-tuple-element.64), channel_id=1, source_target_pairs={{0,2},{1,3},{2,0},{3,1},{4,6},{5,7},{6,4},{7,5},{8,10},{9,11},{10,... | collective-permute-start | bytes 393224 | tf_op jit(solution)/shard_map/ppermute | solution.py:600
  118.7 6.7 %collective-permute-start.14 = (bf16[256,256]{1,0:T(8,128)(2,1)S(1)}, bf16[256,256]{1,0:T(8,128)(2,1)S(1)}, u32[]{:S(2)}, u32[]{:S(2)}) collective-permute-start(bf16[256,256]{1,0:T(8,128)(2,1)S(1)} %get-tuple-element.61), channel_id=1, source_target_pairs={{0,3},{1,2},{2,1},{3,0},{4,7},{5,6},{6,5},{7,4},{8,11},{9,10},{10,... | collective-permute-start | bytes 393224 | tf_op jit(solution)/shard_map/ppermute | solution.py:600
  120.9 5.7 %collective-permute-start.19 = (bf16[2,128,256]{2,1,0:T(8,128)(2,1)S(1)}, bf16[2,128,256]{2,1,0:T(8,128)(2,1)S(1)}, u32[]{:S(2)}, u32[]{:S(2)}) collective-permute-start(bf16[2,128,256]{2,1,0:T(8,128)(2,1)S(1)} %pad_maximum_fusion.1.refs_0_), channel_id=1, source_target_pairs={{0,8},{4,12},{8,0},{12,4},{16,24},{20,28},{24,16},{28,20},{1,9},{5... | collective-permute-start | bytes 393224 | tf_op jit(solution)/shard_map/ppermute | solution.py:597
  121.0 11.9 %collective-permute-start.20 = (bf16[2,128,256]{2,1,0:T(8,128)(2,1)S(1)}, bf16[2,128,256]{2,1,0:T(8,128)(2,1)S(1)}, u32[]{:S(2)}, u32[]{:S(2)}) collective-permute-start(bf16[2,128,256]{2,1,0:T(8,128)(2,1)S(1)} %pad_maximum_fusion.1.refs_0_), channel_id=1, source_target_pairs={{0,16},{4,20},{8,24},{12,28},{16,0},{20,4},{24,8},{28,12},{1,17},{... | collective-permute-start | bytes 393224 | tf_op jit(solution)/shard_map/ppermute | solution.py:597
  123.5 9.4 %collective-permute-start.21 = (bf16[2,128,256]{2,1,0:T(8,128)(2,1)S(1)}, bf16[2,128,256]{2,1,0:T(8,128)(2,1)S(1)}, u32[]{:S(2)}, u32[]{:S(2)}) collective-permute-start(bf16[2,128,256]{2,1,0:T(8,128)(2,1)S(1)} %pad_maximum_fusion.1.refs_0_), channel_id=1, source_target_pairs={{0,24},{4,28},{8,16},{12,20},{16,8},{20,12},{24,0},{28,4},{1,25},{... | collective-permute-start | bytes 393224 | tf_op jit(solution)/shard_map/ppermute | solution.py:597

commit v4 on v3

--- a/solution.py
+++ b/solution.py
@@ -391,7 +391,8 @@
 
 def combine_kernel(groups, slots, place_ref, cot_ref, pcot_ref, *refs):
     parts, refs = refs[: 2 * slots + 2], refs[2 * slots + 2 :]
-    oqa_ref, oqb_ref, shares, buf = refs[0], refs[1], refs[2:-1], refs[-1]
+    mine_ref, give_ref, xmine_ref, xgive_ref = refs[:4]
+    shares, buf, oqa_ref, oqb_ref = refs[4:-3], refs[-3], refs[-2], refs[-1]
     scale = 1.0 / math.sqrt(HDIM)
     odd = place_ref[2] % 2 == 1
     for u, oq_ref in enumerate((oqa_ref, oqb_ref)):
@@ -434,6 +435,12 @@
         buf[g] = total[:, g * step : (g + 1) * step]
     for d in range(groups):
         shares[d][...] = buf[place_ref[2] ^ d]
+    a, b = oqa_ref[...], oqb_ref[...]
+    mine, give = jnp.where(first, a, b).T, jnp.where(first, b, a).T
+    mine_ref[...] = mine
+    give_ref[...] = give
+    xmine_ref[...] = mine[:, : slots * HDIM]
+    xgive_ref[...] = give[:, : slots * HDIM]
 
 
 def combine(place, cot, peer_cot, parts, groups, slots):
@@ -444,41 +451,17 @@
     return pl.pallas_call(
         functools.partial(combine_kernel, groups, slots),
         in_specs=[pl.BlockSpec(memory_space=pltpu.SMEM)] + [vm] * (4 + 2 * slots),
-        out_specs=[vm] * (2 + groups),
-        out_shape=[jax.ShapeDtypeStruct((2 * slots * HDIM, rows), BF)] * 2
+        out_specs=[vm] * (4 + groups),
+        out_shape=[jax.ShapeDtypeStruct((rows, 2 * slots * HDIM), BF)] * 2
+        + [jax.ShapeDtypeStruct((rows, slots * HDIM), BF)] * 2
         + [jax.ShapeDtypeStruct(share, BF)] * groups,
-        scratch_shapes=[pltpu.VMEM((groups, *share), BF)],
+        scratch_shapes=[pltpu.VMEM((groups, *share), BF)]
+        + [pltpu.VMEM((2 * slots * HDIM, rows), BF)] * 2,
         compiler_params=params(),
         cost_estimate=cost(
             4 * rows * slots * HDIM * width, 4 * rows * width + 24 * rows * slots * 256
         ),
     )(place, cot, peer_cot, *parts)
-
-
-def turn_kernel(place_ref, oqa_ref, oqb_ref, mine_ref, give_ref, xmine_ref, xgive_ref):
-    width = xmine_ref.shape[1]
-    first = place_ref[0] == 0
-    a, b = oqa_ref[...], oqb_ref[...]
-    mine = jnp.where(first, a, b).T
-    give = jnp.where(first, b, a).T
-    mine_ref[...] = mine
-    give_ref[...] = give
-    xmine_ref[...] = mine[:, :width]
-    xgive_ref[...] = give[:, :width]
-
-
-def turn(place, oqa, oqb):
-    width, rows = oqa.shape
-    vm = pl.BlockSpec(memory_space=pltpu.VMEM)
-    return pl.pallas_call(
-        turn_kernel,
-        in_specs=[pl.BlockSpec(memory_space=pltpu.SMEM)] + [vm] * 2,
-        out_specs=[vm] * 4,
-        out_shape=[jax.ShapeDtypeStruct((rows, width), BF)] * 2
-        + [jax.ShapeDtypeStruct((rows, width // 2), BF)] * 2,
-        compiler_params=params(),
-        cost_estimate=cost(0, 10 * rows * width),
-    )(place, oqa, oqb)
 
 
 def heads_kernel(place_ref, mine_ref, peer_ref, xmine_ref, xpeer_ref, x_ref, gq_ref):
@@ -671,8 +654,7 @@
     parts += [swap(far[0], 2)]
     links = [(i, i + 2) for i in range(shards - 2) if i // 2 % 2]
     parts += [lax.ppermute(far[1], "tm", links + [(j, i) for i, j in links])]
-    oqa, oqb, *got = combine(place, cot, swap(cot, 1), parts, groups, slots)
-    mine, give, xmine, xgive = turn(place, oqa, oqb)
+    mine, give, xmine, xgive, *got = combine(place, cot, swap(cot, 1), parts, groups, slots)
     total = got[0].astype(F32)
     for d in range(1, groups):
         total += swap(got[d], 2 * d).astype(F32)

time: 133 us -> 133 us (level)
  starting transfers between devices: 39.4 us -> 47.5 us
  Pallas kernels: 51.9 us -> 47 us
  waiting for transfers between devices: 35.6 us -> 31.5 us
    ppermute x11, starting transfers between devices: 15.7 us -> 23.8 us  [swap(): return lax.ppermute(x, 'tm', [(i, i ^ d) for i in range(shards)])]
    pallas_call x3, Pallas kernels: 30.4 us -> 26.3 us  [attend(): pl.pallas_call(functools.partial(attend_kernel, slots, tiles, by_exchange...]
    ppermute x11, waiting for transfers between devices: 20 us -> 18 us  [swap(): return lax.ppermute(x, 'tm', [(i, i ^ d) for i in range(shards)])]
    ppermute x7, waiting for transfers between devices: 9.49 us -> 8.05 us  [swap_clip(): return lax.ppermute(x, 'clip', [(i, i ^ d) for i in range(clips)])]
  transfers between devices with their start and end apart: 24 -> 24, of which waited for: 12 -> 9; matrix products, arithmetic and copies ran while one was open for 1% -> 1% of each run, Pallas kernels for 34% -> 31%
where the time goes in v4:
time: 133 us; the launch traced here: 134 us
  starting transfers between devices  47.5 us (36%)
  Pallas kernels  47 us (35%)
  waiting for transfers between devices  31.5 us (24%)
  local copies, waits for them, and re-layouts  5.28 us (4%)
  other arithmetic  1.33 us (1%)
    pallas_call x3, Pallas kernels, attend(): pl.pallas_call(functools.partial(attend_kernel, slots, tiles, by_exchange...  26.3 us
    ppermute x11, starting transfers between devices, swap(): return lax.ppermute(x, 'tm', [(i, i ^ d) for i in range(shards)])  23.8 us
    ppermute x11, waiting for transfers between devices, swap(): return lax.ppermute(x, 'tm', [(i, i ^ d) for i in range(shards)])  18 us
    all_to_all x2, starting transfers between devices, on_device(): lax.all_to_all(sent[s].reshape(shards, 2 * piece, 2 * HDIM), 'tm', 0, 0)  11.3 us
    ppermute x7, waiting for transfers between devices, swap_clip(): return lax.ppermute(x, 'clip', [(i, i ^ d) for i in range(clips)])  8.05 us
    pallas_call x2, Pallas kernels, put_in_order(): pl.pallas_call(order_kernel, grid=(2,), in_specs=[pl.BlockSpec((1, 1, row...  6.75 us
    unnamed x44, local copies, waits for them, and re-layouts  5.19 us
    ppermute x1, starting transfers between devices, up(): return lax.ppermute(x, 'tm', [(i, i + 2) for i in range(shards - 2)])  4.64 us
  transfers between devices with their start and end apart: 24, of which 9 were waited for; matrix products, arithmetic and copies ran while one was open for 1% of the time, Pallas kernels for 31%

profile of v4, /device:TPU:0, one launch (start us, length us, event | category | flops | bytes accessed | tf_op | source)
XLA Modules:
  0.0 133.6 jit_solution(325730650215563076)
XLA Ops:
  0.6 1.2 copy-done
  1.9 1.2 copy-done.2
  3.1 1.8 %shard_map.104 = bf16[4,2,512,128]{3,2,1,0:T(8,128)(2,1)} custom-call(bf16[2048,256]{1,0:T(8,128)(2,1)S(1)} %copy-done, bf16[2048,256]{1,0:T(8,128)(2,1)S(1)} %copy-done.2), custom_call_target="tpu_custom_call" | custom-call | bytes 3145728 | tf_op jit(solution)/shard_map/pallas_call | solution.py:48
  4.9 7.4 %all-to-all-start = ((bf16[8,512,128]{2,1,0:T(8,128)(2,1)}), bf16[8,512,128]{2,1,0:T(8,128)(2,1)}, u32[]{:S(2)}, u32[]{:S(2)}) async-start(bf16[8,512,128]{2,1,0:T(8,128)(2,1)} %bitcast.8), calls=%async_computation | async-start | bytes 2097152 | tf_op jit(solution)/shard_map/all_to_all | solution.py:636
  12.4 1.6 %collective-permute-start = (bf16[512,256]{1,0:T(8,128)(2,1)S(1)}, bf16[512,256]{1,0:T(8,128)(2,1)S(1)}, u32[]{:S(2)}, u32[]{:S(2)}) collective-permute-start(bf16[512,256]{1,0:T(8,128)(2,1)S(1)} %copy-done.19), channel_id=1, source_target_pairs={{0,2},{1,3},{2,0},{3,1},{4,6},{5,7},{6,4},{7,5},{8,10},{9,11},{10,... | collective-permute-start | bytes 786440 | tf_op jit(solution)/shard_map/ppermute | solution.py:583
  13.9 6.3 %collective-permute-done = bf16[512,256]{1,0:T(8,128)(2,1)S(1)} collective-permute-done((bf16[512,256]{1,0:T(8,128)(2,1)S(1)}, bf16[512,256]{1,0:T(8,128)(2,1)S(1)}, u32[]{:S(2)}, u32[]{:S(2)}) %collective-permute-start) | collective-permute-done | bytes 262176 | tf_op jit(solution)/shard_map/ppermute | solution.py:583
  20.5 1.8 %collective-permute-done.1.there_ref = bf16[2,512,256]{2,1,0:T(8,128)(2,1)S(1)} collective-permute-done((bf16[2,512,256]{2,1,0:T(8,128)(2,1)S(1)}, bf16[2,512,256]{2,1,0:T(8,128)(2,1)S(1)}, u32[]{:S(2)}, u32[]{:S(2)}) %collective-permute-start.1) | collective-permute-done | bytes 524320 | tf_op jit(solution)/shard_map/ppermute | solution.py:583
  22.2 1.0 copy-done.4
  23.3 1.1 shard_map.103
  24.4 0.7 copy-done.6
  25.1 1.7 %collective-permute-start.2 = (bf16[528,256]{1,0:T(8,128)(2,1)S(1)}, bf16[528,256]{1,0:T(8,128)(2,1)S(1)}, u32[]{:S(2)}, u32[]{:S(2)}) collective-permute-start(bf16[528,256]{1,0:T(8,128)(2,1)S(1)} %get-tuple-element.30), channel_id=1, source_target_pairs={{0,4},{4,0},{8,12},{12,8},{16,20},{20,16},{24,28},{28,24},{1,5},{5... | collective-permute-start | bytes 811016 | tf_op jit(solution)/shard_map/ppermute | solution.py:580
  26.8 1.8 %shard_map.108.x_ref = bf16[4,2,512,128]{3,2,1,0:T(8,128)(2,1)} custom-call(bf16[2048,256]{1,0:T(8,128)(2,1)S(1)} %copy-done.1, bf16[2048,256]{1,0:T(8,128)(2,1)S(1)} %copy-done.3), custom_call_target="tpu_custom_call" | custom-call | bytes 3145728 | tf_op jit(solution)/shard_map/pallas_call | solution.py:48
  28.6 7.5 %collective-permute-done.2.after_ref.peer_ref = bf16[528,256]{1,0:T(8,128)(2,1)S(1)} collective-permute-done((bf16[528,256]{1,0:T(8,128)(2,1)S(1)}, bf16[528,256]{1,0:T(8,128)(2,1)S(1)}, u32[]{:S(2)}, u32[]{:S(2)}) %collective-permute-start.2) | collective-permute-done | bytes 270368 | tf_op jit(solution)/shard_map/ppermute | solution.py:580
  36.1 2.1 %all-to-all-done.arr_ref = bf16[8,512,128]{2,1,0:T(8,128)(2,1)} async-done(((bf16[8,512,128]{2,1,0:T(8,128)(2,1)}), bf16[8,512,128]{2,1,0:T(8,128)(2,1)}, u32[]{:S(2)}, u32[]{:S(2)}) %all-to-all-start) | async-done | bytes 1048608 | tf_op jit(solution)/shard_map/all_to_all | solution.py:636
  38.2 3.9 %all-to-all-start.1 = ((bf16[8,512,128]{2,1,0:T(8,128)(2,1)}), bf16[8,512,128]{2,1,0:T(8,128)(2,1)S(1)}, u32[]{:S(2)}, u32[]{:S(2)}) async-start(bf16[8,512,128]{2,1,0:T(8,128)(2,1)} %bitcast.9), calls=%async_computation.1 | async-start | bytes 2097152 | tf_op jit(solution)/shard_map/all_to_all | solution.py:636
  42.1 0.7 fusion.2
  43.1 3.9 %shard_map.105 = (bf16[4096,128]{1,0:T(8,128)(2,1)S(1)}, bf16[128,4096]{1,0:T(8,128)(2,1)S(1)}) custom-call(s32[2,1,2048]{2,1,0:T(1,128)S(1)} %bitcast.18, bf16[8,512,128]{2,1,0:T(8,128)(2,1)} %all-to-all-done.arr_ref), custom_call_target="tpu_custom_call" | custom-call | flops 2147483648 | bytes 3145728 | tf_op jit(solution)/shard_map/pallas_call | solution.py:94
  47.0 1.5 %shard_map.111 = (bf16[528,256]{1,0:T(8,128)(2,1)}, bf16[528,256]{1,0:T(8,128)(2,1)}) custom-call(s32[3]{0:T(128)S(1)} %pad_add_fusion.2.place_ref, bf16[528,256]{1,0:T(8,128)(2,1)S(1)} %copy-done.7, bf16[528,256]{1,0:T(8,128)(2,1)S(1)} %collective-permute-done.2.after_ref.peer_ref, bf16[4096,128]{1,0:T(8,128)(2,1)S(1)} %get-tuple-element.31.refs_0_.after_ref), custom_call_target="tpu_custom_call" | custom-call | bytes 1081344 | tf_op jit(solution)/shard_map/pallas_call | solution.py:188
  48.5 4.6 %collective-permute-start.4 = (bf16[528,256]{1,0:T(8,128)(2,1)}, bf16[528,256]{1,0:T(8,128)(2,1)}, u32[]{:S(2)}, u32[]{:S(2)}) collective-permute-start(bf16[528,256]{1,0:T(8,128)(2,1)} %get-tuple-element.37), channel_id=1, source_target_pairs={{0,8},{4,12},{8,16},{12,20},{16,24},{20,28},{1,9},{5,13},{9,17},{1... | collective-permute-start | bytes 811016 | tf_op jit(solution)/shard_map/ppermute | solution.py:590
  53.1 1.3 collective-permute-start.5
  54.4 11.2 %shard_map.106 = (bf16[208,512]{1,0:T(8,128)(2,1)S(1)}, bf16[208,512]{1,0:T(8,128)(2,1)S(1)}) custom-call(s32[3]{0:T(128)S(1)} %pad_add_fusion.2.place_ref, s32[2,32]{1,0:T(2,128)S(1)} %pad_add_fusion.lohi_ref, bf16[528,256]{1,0:T(8,128)(2,1)S(1)} %get-tuple-element.55.qga_ref, bf16[528,256]{1,0:T(8,128)(2,1)S(1)} %get-tuple-element.56.qgb_ref, ...), custom_call_target="tpu_custom_call" | custom-call | flops 2147483648 | bytes 4194304 | tf_op jit(solution)/shard_map/pallas_call | solution.py:377
  65.7 0.7 copy-done.15
  66.3 0.7 shard_map.107.cot_ref
  67.0 1.5 %collective-permute-start.3 = (bf16[512,1024]{1,0:T(8,128)(2,1)S(1)}, bf16[512,1024]{1,0:T(8,128)(2,1)}, u32[]{:S(2)}, u32[]{:S(2)}) collective-permute-start(bf16[512,1024]{1,0:T(8,128)(2,1)S(1)} %shard_map.107.cot_ref), channel_id=1, source_target_pairs={{0,4},{4,0},{8,12},{12,8},{16,20},{20,16},{24,28},{28,24},{1,5},{5... | collective-permute-start | bytes 3145736 | tf_op jit(solution)/shard_map/ppermute | solution.py:580
  68.5 0.8 all-to-all-done.1.arr_ref
  69.3 2.9 %shard_map.110 = (bf16[4096,128]{1,0:T(8,128)(2,1)S(1)}, bf16[128,4096]{1,0:T(8,128)(2,1)S(1)}) custom-call(s32[2,1,2048]{2,1,0:T(1,128)S(1)} %bitcast.19, bf16[8,512,128]{2,1,0:T(8,128)(2,1)S(1)} %all-to-all-done.1.arr_ref, bf16[208,512]{1,0:T(8,128)(2,1)S(1)} %get-tuple-element.33.after_ref.refs_0_), custom_call_target="tpu_custom_call" | custom-call | flops 2147483648 | bytes 3145728 | tf_op jit(solution)/shard_map/pallas_call | solution.py:94
  72.2 0.8 shard_map.112
  73.5 4.2 %shard_map.113 = (bf16[416,512]{1,0:T(8,128)(2,1)S(1)}, bf16[416,512]{1,0:T(8,128)(2,1)S(1)}) custom-call(s32[3]{0:T(128)S(1)} %pad_add_fusion.2.place_ref, s32[2,32]{1,0:T(2,128)S(1)} %pad_add_fusion.1.lohi_ref, bf16[528,256]{1,0:T(8,128)(2,1)} %collective-permute-done.4.left_ref.qga_ref, bf16[528,256]{1,0:T(8,128)(2,1)} %collective-permute-done.5.right_ref.qgb_ref, ...), custom_call_target="tpu_custom_call" | custom-call | flops 4294967296 | bytes 8388608 | tf_op jit(solution)/shard_map/pallas_call | solution.py:377
  77.6 10.1 %collective-permute-start.6 = (bf16[416,512]{1,0:T(8,128)(2,1)S(1)}, bf16[416,512]{1,0:T(8,128)(2,1)S(1)}, u32[]{:S(2)}, u32[]{:S(2)}) collective-permute-start(bf16[416,512]{1,0:T(8,128)(2,1)S(1)} %get-tuple-element.39.refs_2_), channel_id=1, source_target_pairs={{0,8},{4,12},{8,0},{12,4},{16,24},{20,28},{24,16},{28,20},{1,9},{5... | collective-permute-start | bytes 1277960 | tf_op jit(solution)/shard_map/ppermute | solution.py:580
  87.7 0.8 collective-permute-start.7
  88.5 11.0 %shard_map.114 = (bf16[208,512]{1,0:T(8,128)(2,1)S(1)}, bf16[208,512]{1,0:T(8,128)(2,1)S(1)}) custom-call(s32[3]{0:T(128)S(1)} %pad_add_fusion.2.place_ref, s32[2,32]{1,0:T(2,128)S(1)} %pad_add_fusion.lohi_ref, bf16[528,256]{1,0:T(8,128)(2,1)S(1)} %copy-done.11, bf16[528,256]{1,0:T(8,128)(2,1)S(1)} %copy-done.13, ...), custom_call_target="tpu_custom_call" | custom-call | flops 2147483648 | bytes 4194304 | tf_op jit(solution)/shard_map/pallas_call | solution.py:377
  99.6 2.1 %shard_map.115 = (bf16[512,256]{1,0:T(8,128)(2,1)S(1)}, bf16[512,256]{1,0:T(8,128)(2,1)S(1)}, bf16[512,128]{1,0:T(8,128)(2,1)S(1)}, bf16[512,128]{1,0:T(8,128)(2...) custom-call(s32[3]{0:T(128)S(1)} %pad_add_fusion.2.place_ref, ...), custom_call_target="tpu_custom_call" | custom-call | flops 268435456 | bytes 8388608 | tf_op jit(solution)/shard_map/pallas_call | solution.py:451
  101.8 1.4 %collective-permute-start.8 = (bf16[512,256]{1,0:T(8,128)(2,1)S(1)}, bf16[512,256]{1,0:T(8,128)(2,1)S(1)}, u32[]{:S(2)}, u32[]{:S(2)}) collective-permute-start(bf16[512,256]{1,0:T(8,128)(2,1)S(1)} %get-tuple-element.44), channel_id=1, source_target_pairs={{0,4},{4,0},{8,12},{12,8},{16,20},{20,16},{24,28},{28,24},{1,5},{5... | collective-permute-start | bytes 786440 | tf_op jit(solution)/shard_map/ppermute | solution.py:580
  103.2 1.6 %collective-permute-start.10 = (bf16[512,128]{1,0:T(8,128)(2,1)S(1)}, bf16[512,128]{1,0:T(8,128)(2,1)S(1)}, u32[]{:S(2)}, u32[]{:S(2)}) collective-permute-start(bf16[512,128]{1,0:T(8,128)(2,1)S(1)} %get-tuple-element.46), channel_id=1, source_target_pairs={{0,6},{1,7},{2,4},{3,5},{4,2},{5,3},{6,0},{7,1},{8,14},{9,15},{10,... | collective-permute-start | bytes 393224 | tf_op jit(solution)/shard_map/ppermute | solution.py:587
  104.8 0.5 collective-permute-start.9
  105.3 0.6 collective-permute-start.15
  105.9 1.0 collective-permute-start.16
  107.0 2.6 %collective-permute-done.10.xpeer_ref = bf16[512,128]{1,0:T(8,128)(2,1)S(1)} collective-permute-done((bf16[512,128]{1,0:T(8,128)(2,1)S(1)}, bf16[512,128]{1,0:T(8,128)(2,1)S(1)}, u32[]{:S(2)}, u32[]{:S(2)}) %collective-permute-start.10) | collective-permute-done | bytes 131104 | tf_op jit(solution)/shard_map/ppermute | solution.py:587
  109.6 2.2 %collective-permute-start.17 = (bf16[128,256]{1,0:T(8,128)(2,1)S(1)}, bf16[128,256]{1,0:T(8,128)(2,1)S(1)}, u32[]{:S(2)}, u32[]{:S(2)}) collective-permute-start(bf16[128,256]{1,0:T(8,128)(2,1)S(1)} %get-tuple-element.53), channel_id=1, source_target_pairs={{0,24},{4,28},{8,16},{12,20},{16,8},{20,12},{24,0},{28,4},{1,25},{... | collective-permute-start | bytes 196616 | tf_op jit(solution)/shard_map/ppermute | solution.py:580
  111.8 1.3 shard_map.116
  113.1 2.5 %collective-permute-done.17 = bf16[128,256]{1,0:T(8,128)(2,1)S(1)} collective-permute-done((bf16[128,256]{1,0:T(8,128)(2,1)S(1)}, bf16[128,256]{1,0:T(8,128)(2,1)S(1)}, u32[]{:S(2)}, u32[]{:S(2)}) %collective-permute-start.17) | collective-permute-done | bytes 65568 | tf_op jit(solution)/shard_map/ppermute | solution.py:580
  116.2 1.5 %collective-permute-start.13 = (bf16[256,256]{1,0:T(8,128)(2,1)S(1)}, bf16[256,256]{1,0:T(8,128)(2,1)S(1)}, u32[]{:S(2)}, u32[]{:S(2)}) collective-permute-start(bf16[256,256]{1,0:T(8,128)(2,1)S(1)} %get-tuple-element.60), channel_id=1, source_target_pairs={{0,2},{1,3},{2,0},{3,1},{4,6},{5,7},{6,4},{7,5},{8,10},{9,11},{10,... | collective-permute-start | bytes 393224 | tf_op jit(solution)/shard_map/ppermute | solution.py:583
  118.1 1.9 %collective-permute-done.18 = bf16[128,256]{1,0:T(8,128)(2,1)S(1)} collective-permute-done((bf16[128,256]{1,0:T(8,128)(2,1)S(1)}, bf16[128,256]{1,0:T(8,128)(2,1)S(1)}, u32[]{:S(2)}, u32[]{:S(2)}) %collective-permute-start.18) | collective-permute-done | bytes 65568 | tf_op jit(solution)/shard_map/ppermute | solution.py:580
  120.1 2.8 %collective-permute-start.20 = (bf16[2,128,256]{2,1,0:T(8,128)(2,1)S(1)}, bf16[2,128,256]{2,1,0:T(8,128)(2,1)S(1)}, u32[]{:S(2)}, u32[]{:S(2)}) collective-permute-start(bf16[2,128,256]{2,1,0:T(8,128)(2,1)S(1)} %pad_maximum_fusion.1.refs_0_), channel_id=1, source_target_pairs={{0,16},{4,20},{8,24},{12,28},{16,0},{20,4},{24,8},{28,12},{1,17},{... | collective-permute-start | bytes 393224 | tf_op jit(solution)/shard_map/ppermute | solution.py:580
  122.9 2.0 %collective-permute-start.21 = (bf16[2,128,256]{2,1,0:T(8,128)(2,1)S(1)}, bf16[2,128,256]{2,1,0:T(8,128)(2,1)S(1)}, u32[]{:S(2)}, u32[]{:S(2)}) collective-permute-start(bf16[2,128,256]{2,1,0:T(8,128)(2,1)S(1)} %pad_maximum_fusion.1.refs_0_), channel_id=1, source_target_pairs={{0,24},{4,28},{8,16},{12,20},{16,8},{20,12},{24,0},{28,4},{1,25},{... | collective-permute-start | bytes 393224 | tf_op jit(solution)/shard_map/ppermute | solution.py:580
  124.8 1.2 shard_map.117
  126.0 6.0 %collective-permute-done.20.refs_2_ = bf16[2,128,256]{2,1,0:T(8,128)(2,1)S(1)} collective-permute-done((bf16[2,128,256]{2,1,0:T(8,128)(2,1)S(1)}, bf16[2,128,256]{2,1,0:T(8,128)(2,1)S(1)}, u32[]{:S(2)}, u32[]{:S(2)}) %collective-permute-start.20) | collective-permute-done | bytes 131104 | tf_op jit(solution)/shard_map/ppermute | solution.py:580
  132.0 1.6 %shard_map.118 = f32[256,1024]{1,0:T(8,128)} custom-call(s32[3]{0:T(128)S(1)} %pad_add_fusion.2.place_ref, bf16[2,128,256]{2,1,0:T(8,128)(2,1)S(1)} %pad_maximum_fusion.1.refs_0_, bf16[2,128,256]{2,1,0:T(8,128)(2,1)S(1)} %collective-permute-done.19.refs_1_, bf16[2,128,256]{2,1,0:T(8,128)(2,1)S(1)} %collective-permute-done.20.refs_2_, ...), custom_call_target="tpu_custom_call" | custom-call | bytes 1572864 | tf_op jit(solution)/shard_map/pallas_call | solution.py:541
  (82 shorter events, 2.0 us)
Async XLA Ops:
  0.6 1.2 copy-start
  1.9 1.2 copy-start.2
  4.9 7.4 %copy-start.19 = (bf16[512,256]{1,0:T(8,128)(2,1)S(1)}, bf16[512,256]{1,0:T(8,128)(2,1)}, u32[]{:S(2)}) copy-start(bf16[512,256]{1,0:T(8,128)(2,1)} %param.15) | copy-start | bytes 786436
  4.9 15.5 %copy-start.20 = (s32[16]{0:T(128)S(1)}, s32[16]{0:T(128)}, u32[]{:S(2)}) copy-start(s32[16]{0:T(128)} %param.13) | copy-start | bytes 196
  4.9 15.5 %copy-start.21 = (s32[16]{0:T(128)S(1)}, s32[16]{0:T(128)}, u32[]{:S(2)}) copy-start(s32[16]{0:T(128)} %param.12) | copy-start | bytes 196
  4.9 17.3 %copy-start.14 = (bf16[512,256]{1,0:T(8,128)(2,1)S(1)}, bf16[512,256]{1,0:T(8,128)(2,1)}, u32[]{:S(2)}) copy-start(bf16[512,256]{1,0:T(8,128)(2,1)} %q_ref.1) | copy-start | bytes 786436
  4.9 33.3 %all-to-all-start = ((bf16[8,512,128]{2,1,0:T(8,128)(2,1)}), bf16[8,512,128]{2,1,0:T(8,128)(2,1)}, u32[]{:S(2)}, u32[]{:S(2)}) async-start(bf16[8,512,128]{2,1,0:T(8,128)(2,1)} %bitcast.8), calls=%async_computation | async-start | bytes 2097152 | tf_op jit(solution)/shard_map/all_to_all | solution.py:636
  12.4 7.8 %collective-permute-start = (bf16[512,256]{1,0:T(8,128)(2,1)S(1)}, bf16[512,256]{1,0:T(8,128)(2,1)S(1)}, u32[]{:S(2)}, u32[]{:S(2)}) collective-permute-start(bf16[512,256]{1,0:T(8,128)(2,1)S(1)} %copy-done.19), channel_id=1, source_target_pairs={{0,2},{1,3},{2,0},{3,1},{4,6},{5,7},{6,4},{7,5},{8,10},{9,11},{10,... | collective-permute-start | bytes 786440 | tf_op jit(solution)/shard_map/ppermute | solution.py:583
  20.2 6.6 %copy-start.3 = (bf16[2048,256]{1,0:T(8,128)(2,1)S(1)}, bf16[2048,256]{1,0:T(8,128)(2,1)}, u32[]{:S(2)}) copy-start(bf16[2048,256]{1,0:T(8,128)(2,1)} %v_ref.3) | copy-start | bytes 3145732
  20.2 6.5 %copy-start.1 = (bf16[2048,256]{1,0:T(8,128)(2,1)S(1)}, bf16[2048,256]{1,0:T(8,128)(2,1)}, u32[]{:S(2)}) copy-start(bf16[2048,256]{1,0:T(8,128)(2,1)} %k_ref.3) | copy-start | bytes 3145732
  20.2 2.0 %collective-permute-start.1 = (bf16[2,512,256]{2,1,0:T(8,128)(2,1)S(1)}, bf16[2,512,256]{2,1,0:T(8,128)(2,1)S(1)}, u32[]{:S(2)}, u32[]{:S(2)}) collective-permute-start(bf16[2,512,256]{2,1,0:T(8,128)(2,1)S(1)} %pad_maximum_fusion.here_ref), channel_id=1, source_target_pairs={{0,1},{1,0},{2,3},{3,2},{4,5},{5,4},{6,7},{7,6},{8,9},{9,8},{10,11... | collective-permute-start | bytes 1572872 | tf_op jit(solution)/shard_map/ppermute | solution.py:583
  22.2 1.0 copy-start.4
  24.4 0.7 copy-start.6
  25.1 11.0 %collective-permute-start.2 = (bf16[528,256]{1,0:T(8,128)(2,1)S(1)}, bf16[528,256]{1,0:T(8,128)(2,1)S(1)}, u32[]{:S(2)}, u32[]{:S(2)}) collective-permute-start(bf16[528,256]{1,0:T(8,128)(2,1)S(1)} %get-tuple-element.30), channel_id=1, source_target_pairs={{0,4},{4,0},{8,12},{12,8},{16,20},{20,16},{24,28},{28,24},{1,5},{5... | collective-permute-start | bytes 811016 | tf_op jit(solution)/shard_map/ppermute | solution.py:580
  38.2 4.6 %copy-start.7 = (bf16[528,256]{1,0:T(8,128)(2,1)S(1)}, bf16[528,256]{1,0:T(8,128)(2,1)}, u32[]{:S(2)}) copy-start(bf16[528,256]{1,0:T(8,128)(2,1)} %copy-done.6) | copy-start | bytes 811012
  38.2 31.1 %all-to-all-start.1 = ((bf16[8,512,128]{2,1,0:T(8,128)(2,1)}), bf16[8,512,128]{2,1,0:T(8,128)(2,1)S(1)}, u32[]{:S(2)}, u32[]{:S(2)}) async-start(bf16[8,512,128]{2,1,0:T(8,128)(2,1)} %bitcast.9), calls=%async_computation.1 | async-start | bytes 2097152 | tf_op jit(solution)/shard_map/all_to_all | solution.py:636
  42.9 11.5 %copy-start.10 = (bf16[528,256]{1,0:T(8,128)(2,1)}, bf16[528,256]{1,0:T(8,128)(2,1)S(1)}, u32[]{:S(2)}) copy-start(bf16[528,256]{1,0:T(8,128)(2,1)S(1)} %get-tuple-element.55.qga_ref) | copy-start | bytes 811012
  42.9 11.5 %copy-start.12 = (bf16[528,256]{1,0:T(8,128)(2,1)}, bf16[528,256]{1,0:T(8,128)(2,1)S(1)}, u32[]{:S(2)}) copy-start(bf16[528,256]{1,0:T(8,128)(2,1)S(1)} %get-tuple-element.56.qgb_ref) | copy-start | bytes 811012
  47.0 18.6 %copy-start.8 = (bf16[4096,128]{1,0:T(8,128)(2,1)}, bf16[4096,128]{1,0:T(8,128)(2,1)S(1)}, u32[]{:S(2)}) copy-start(bf16[4096,128]{1,0:T(8,128)(2,1)S(1)} %get-tuple-element.31.refs_0_.after_ref) | copy-start | bytes 3145732
  47.0 18.6 %copy-start.17 = (bf16[128,4096]{1,0:T(8,128)(2,1)}, bf16[128,4096]{1,0:T(8,128)(2,1)S(1)}, u32[]{:S(2)}) copy-start(bf16[128,4096]{1,0:T(8,128)(2,1)S(1)} %get-tuple-element.32.refs_1_) | copy-start | bytes 3145732
  48.5 23.7 %collective-permute-start.4 = (bf16[528,256]{1,0:T(8,128)(2,1)}, bf16[528,256]{1,0:T(8,128)(2,1)}, u32[]{:S(2)}, u32[]{:S(2)}) collective-permute-start(bf16[528,256]{1,0:T(8,128)(2,1)} %get-tuple-element.37), channel_id=1, source_target_pairs={{0,8},{4,12},{8,16},{12,20},{16,24},{20,28},{1,9},{5,13},{9,17},{1... | collective-permute-start | bytes 811016 | tf_op jit(solution)/shard_map/ppermute | solution.py:590
  53.1 19.1 %collective-permute-start.5 = (bf16[528,256]{1,0:T(8,128)(2,1)}, bf16[528,256]{1,0:T(8,128)(2,1)}, u32[]{:S(2)}, u32[]{:S(2)}) collective-permute-start(bf16[528,256]{1,0:T(8,128)(2,1)} %get-tuple-element.38), channel_id=1, source_target_pairs={{8,0},{12,4},{16,8},{20,12},{24,16},{28,20},{9,1},{13,5},{17,9},{2... | collective-permute-start | bytes 811016 | tf_op jit(solution)/shard_map/ppermute | solution.py:593
  65.6 0.7 copy-start.15
  67.0 32.6 %collective-permute-start.3 = (bf16[512,1024]{1,0:T(8,128)(2,1)S(1)}, bf16[512,1024]{1,0:T(8,128)(2,1)}, u32[]{:S(2)}, u32[]{:S(2)}) collective-permute-start(bf16[512,1024]{1,0:T(8,128)(2,1)S(1)} %shard_map.107.cot_ref), channel_id=1, source_target_pairs={{0,4},{4,0},{8,12},{12,8},{16,20},{20,16},{24,28},{28,24},{1,5},{5... | collective-permute-start | bytes 3145736 | tf_op jit(solution)/shard_map/ppermute | solution.py:580
  69.3 3.9 %copy-start.18 = (bf16[128,4096]{1,0:T(8,128)(2,1)S(1)}, bf16[128,4096]{1,0:T(8,128)(2,1)}, u32[]{:S(2)}) copy-start(bf16[128,4096]{1,0:T(8,128)(2,1)} %copy-done.17) | copy-start | bytes 3145732
  72.2 1.3 copy-start.9
  73.5 15.1 %copy-start.11 = (bf16[528,256]{1,0:T(8,128)(2,1)S(1)}, bf16[528,256]{1,0:T(8,128)(2,1)}, u32[]{:S(2)}) copy-start(bf16[528,256]{1,0:T(8,128)(2,1)} %copy-done.10) | copy-start | bytes 811012
  73.5 15.1 %copy-start.13 = (bf16[528,256]{1,0:T(8,128)(2,1)S(1)}, bf16[528,256]{1,0:T(8,128)(2,1)}, u32[]{:S(2)}) copy-start(bf16[528,256]{1,0:T(8,128)(2,1)} %copy-done.12) | copy-start | bytes 811012
  77.6 21.9 %collective-permute-start.6 = (bf16[416,512]{1,0:T(8,128)(2,1)S(1)}, bf16[416,512]{1,0:T(8,128)(2,1)S(1)}, u32[]{:S(2)}, u32[]{:S(2)}) collective-permute-start(bf16[416,512]{1,0:T(8,128)(2,1)S(1)} %get-tuple-element.39.refs_2_), channel_id=1, source_target_pairs={{0,8},{4,12},{8,0},{12,4},{16,24},{20,28},{24,16},{28,20},{1,9},{5... | collective-permute-start | bytes 1277960 | tf_op jit(solution)/shard_map/ppermute | solution.py:580
  87.7 11.9 %copy-start.16 = (bf16[208,512]{1,0:T(8,128)(2,1)S(1)}, bf16[208,512]{1,0:T(8,128)(2,1)}, u32[]{:S(2)}) copy-start(bf16[208,512]{1,0:T(8,128)(2,1)} %copy-done.15) | copy-start | bytes 638980
  87.7 11.9 %collective-permute-start.7 = (bf16[416,512]{1,0:T(8,128)(2,1)S(1)}, bf16[416,512]{1,0:T(8,128)(2,1)S(1)}, u32[]{:S(2)}, u32[]{:S(2)}) collective-permute-start(bf16[416,512]{1,0:T(8,128)(2,1)S(1)} %get-tuple-element.40.refs_3_), channel_id=1, source_target_pairs={{8,16},{12,20},{16,8},{20,12},{9,17},{13,21},{17,9},{21,13},{10,18... | collective-permute-start | bytes 1277960 | tf_op jit(solution)/shard_map/ppermute | solution.py:656
  101.8 10.0 %collective-permute-start.8 = (bf16[512,256]{1,0:T(8,128)(2,1)S(1)}, bf16[512,256]{1,0:T(8,128)(2,1)S(1)}, u32[]{:S(2)}, u32[]{:S(2)}) collective-permute-start(bf16[512,256]{1,0:T(8,128)(2,1)S(1)} %get-tuple-element.44), channel_id=1, source_target_pairs={{0,4},{4,0},{8,12},{12,8},{16,20},{20,16},{24,28},{28,24},{1,5},{5... | collective-permute-start | bytes 786440 | tf_op jit(solution)/shard_map/ppermute | solution.py:580
  103.2 6.4 %collective-permute-start.10 = (bf16[512,128]{1,0:T(8,128)(2,1)S(1)}, bf16[512,128]{1,0:T(8,128)(2,1)S(1)}, u32[]{:S(2)}, u32[]{:S(2)}) collective-permute-start(bf16[512,128]{1,0:T(8,128)(2,1)S(1)} %get-tuple-element.46), channel_id=1, source_target_pairs={{0,6},{1,7},{2,4},{3,5},{4,2},{5,3},{6,0},{7,1},{8,14},{9,15},{10,... | collective-permute-start | bytes 393224 | tf_op jit(solution)/shard_map/ppermute | solution.py:587
  104.8 7.0 %collective-permute-start.9 = (bf16[512,128]{1,0:T(8,128)(2,1)S(1)}, bf16[512,128]{1,0:T(8,128)(2,1)S(1)}, u32[]{:S(2)}, u32[]{:S(2)}) collective-permute-start(bf16[512,128]{1,0:T(8,128)(2,1)S(1)} %get-tuple-element.45), channel_id=1, source_target_pairs={{0,2},{1,3},{2,0},{3,1},{4,6},{5,7},{6,4},{7,5},{8,10},{9,11},{10,... | collective-permute-start | bytes 393224 | tf_op jit(solution)/shard_map/ppermute | solution.py:583
  105.3 7.8 %collective-permute-start.15 = (bf16[128,256]{1,0:T(8,128)(2,1)S(1)}, bf16[128,256]{1,0:T(8,128)(2,1)S(1)}, u32[]{:S(2)}, u32[]{:S(2)}) collective-permute-start(bf16[128,256]{1,0:T(8,128)(2,1)S(1)} %get-tuple-element.51), channel_id=1, source_target_pairs={{0,8},{4,12},{8,0},{12,4},{16,24},{20,28},{24,16},{28,20},{1,9},{5... | collective-permute-start | bytes 196616 | tf_op jit(solution)/shard_map/ppermute | solution.py:580
  105.9 7.2 %collective-permute-start.16 = (bf16[128,256]{1,0:T(8,128)(2,1)S(1)}, bf16[128,256]{1,0:T(8,128)(2,1)S(1)}, u32[]{:S(2)}, u32[]{:S(2)}) collective-permute-start(bf16[128,256]{1,0:T(8,128)(2,1)S(1)} %get-tuple-element.52), channel_id=1, source_target_pairs={{0,16},{4,20},{8,24},{12,28},{16,0},{20,4},{24,8},{28,12},{1,17},{... | collective-permute-start | bytes 196616 | tf_op jit(solution)/shard_map/ppermute | solution.py:580
  109.6 6.1 %collective-permute-start.17 = (bf16[128,256]{1,0:T(8,128)(2,1)S(1)}, bf16[128,256]{1,0:T(8,128)(2,1)S(1)}, u32[]{:S(2)}, u32[]{:S(2)}) collective-permute-start(bf16[128,256]{1,0:T(8,128)(2,1)S(1)} %get-tuple-element.53), channel_id=1, source_target_pairs={{0,24},{4,28},{8,16},{12,20},{16,8},{20,12},{24,0},{28,4},{1,25},{... | collective-permute-start | bytes 196616 | tf_op jit(solution)/shard_map/ppermute | solution.py:580
  111.8 4.3 %copy-start.5 = (bf16[256,1024]{1,0:T(8,128)(2,1)S(1)}, bf16[256,1024]{1,0:T(8,128)(2,1)}, u32[]{:S(2)}) copy-start(bf16[256,1024]{1,0:T(8,128)(2,1)} %w_ref.1) | copy-start | bytes 1572868
  113.1 11.7 %collective-permute-start.11 = (bf16[512,512]{1,0:T(8,128)(2,1)S(1)}, bf16[512,512]{1,0:T(8,128)(2,1)S(1)}, u32[]{:S(2)}, u32[]{:S(2)}) collective-permute-start(bf16[512,512]{1,0:T(8,128)(2,1)S(1)} %get-tuple-element.47.here_ref), channel_id=1, source_target_pairs={{0,1},{1,0},{2,3},{3,2},{4,5},{5,4},{6,7},{7,6},{8,9},{9,8},{10,11... | collective-permute-start | bytes 1572872 | tf_op jit(solution)/shard_map/ppermute | solution.py:583
  115.7 4.3 %collective-permute-start.18 = (bf16[128,256]{1,0:T(8,128)(2,1)S(1)}, bf16[128,256]{1,0:T(8,128)(2,1)S(1)}, u32[]{:S(2)}, u32[]{:S(2)}) collective-permute-start(bf16[128,256]{1,0:T(8,128)(2,1)S(1)} %add_convert_fusion), channel_id=1, source_target_pairs={{0,4},{4,0},{8,12},{12,8},{16,20},{20,16},{24,28},{28,24},{1,5},{5... | collective-permute-start | bytes 196616 | tf_op jit(solution)/shard_map/ppermute | solution.py:580
  116.2 3.9 %collective-permute-start.12 = (bf16[256,256]{1,0:T(8,128)(2,1)S(1)}, bf16[256,256]{1,0:T(8,128)(2,1)S(1)}, u32[]{:S(2)}, u32[]{:S(2)}) collective-permute-start(bf16[256,256]{1,0:T(8,128)(2,1)S(1)} %get-tuple-element.58), channel_id=1, source_target_pairs={{0,1},{1,0},{2,3},{3,2},{4,5},{5,4},{6,7},{7,6},{8,9},{9,8},{10,11... | collective-permute-start | bytes 393224 | tf_op jit(solution)/shard_map/ppermute | solution.py:583
  116.2 6.6 %collective-permute-start.13 = (bf16[256,256]{1,0:T(8,128)(2,1)S(1)}, bf16[256,256]{1,0:T(8,128)(2,1)S(1)}, u32[]{:S(2)}, u32[]{:S(2)}) collective-permute-start(bf16[256,256]{1,0:T(8,128)(2,1)S(1)} %get-tuple-element.60), channel_id=1, source_target_pairs={{0,2},{1,3},{2,0},{3,1},{4,6},{5,7},{6,4},{7,5},{8,10},{9,11},{10,... | collective-permute-start | bytes 393224 | tf_op jit(solution)/shard_map/ppermute | solution.py:583
  117.8 7.0 %collective-permute-start.14 = (bf16[256,256]{1,0:T(8,128)(2,1)S(1)}, bf16[256,256]{1,0:T(8,128)(2,1)S(1)}, u32[]{:S(2)}, u32[]{:S(2)}) collective-permute-start(bf16[256,256]{1,0:T(8,128)(2,1)S(1)} %get-tuple-element.57), channel_id=1, source_target_pairs={{0,3},{1,2},{2,1},{3,0},{4,7},{5,6},{6,5},{7,4},{8,11},{9,10},{10,... | collective-permute-start | bytes 393224 | tf_op jit(solution)/shard_map/ppermute | solution.py:583
  120.0 6.0 %collective-permute-start.19 = (bf16[2,128,256]{2,1,0:T(8,128)(2,1)S(1)}, bf16[2,128,256]{2,1,0:T(8,128)(2,1)S(1)}, u32[]{:S(2)}, u32[]{:S(2)}) collective-permute-start(bf16[2,128,256]{2,1,0:T(8,128)(2,1)S(1)} %pad_maximum_fusion.1.refs_0_), channel_id=1, source_target_pairs={{0,8},{4,12},{8,0},{12,4},{16,24},{20,28},{24,16},{28,20},{1,9},{5... | collective-permute-start | bytes 393224 | tf_op jit(solution)/shard_map/ppermute | solution.py:580
  120.1 11.9 %collective-permute-start.20 = (bf16[2,128,256]{2,1,0:T(8,128)(2,1)S(1)}, bf16[2,128,256]{2,1,0:T(8,128)(2,1)S(1)}, u32[]{:S(2)}, u32[]{:S(2)}) collective-permute-start(bf16[2,128,256]{2,1,0:T(8,128)(2,1)S(1)} %pad_maximum_fusion.1.refs_0_), channel_id=1, source_target_pairs={{0,16},{4,20},{8,24},{12,28},{16,0},{20,4},{24,8},{28,12},{1,17},{... | collective-permute-start | bytes 393224 | tf_op jit(solution)/shard_map/ppermute | solution.py:580
  122.9 9.1 %collective-permute-start.21 = (bf16[2,128,256]{2,1,0:T(8,128)(2,1)S(1)}, bf16[2,128,256]{2,1,0:T(8,128)(2,1)S(1)}, u32[]{:S(2)}, u32[]{:S(2)}) collective-permute-start(bf16[2,128,256]{2,1,0:T(8,128)(2,1)S(1)} %pad_maximum_fusion.1.refs_0_), channel_id=1, source_target_pairs={{0,24},{4,28},{8,16},{12,20},{16,8},{20,12},{24,0},{28,4},{1,25},{... | collective-permute-start | bytes 393224 | tf_op jit(solution)/shard_map/ppermute | solution.py:580
